TPU v7x, 128 devices: a whole 4x4x4 slice. The times are simulated.
128 devices in a mesh: dp: 32 (over y, z, core), mp: 4 (over x).
Axes of the slice: x: 4, y: 4, z: 4, core: 2. Of those that a mesh axis runs over, the one named last changes fastest.
Arguments:
- layer_input: bfloat16 [262144, 384], P(('dp', 'mp')), may hold values from -6 to 6
- segments: int32 [32, 8192], P('dp'), may hold values from -1 to 121, as said below
- cotangent: bfloat16 [262144, 384], P(('dp', 'mp')), may hold values from -6 to 6
- first_gain: float32 [384], replicated, may hold values from 0.5 to 1.5
- first_shift: float32 [384], replicated, may hold values from -3 to 3
- inward_weight: bfloat16 [384, 1152], replicated, may hold values from -0.3125 to 0.3125
- inward_bias: float32 [2, 384], replicated, may hold values from -3 to 3
- outward_weight: bfloat16 [384, 384], replicated, may hold values from -1.75 to 1.75
- outward_bias: float32 [384], replicated, may hold values from -3 to 3
- second_gain: float32 [384], replicated, may hold values from 0.5 to 1.5
- second_shift: float32 [384], replicated, may hold values from -3 to 3
- expand_weight: bfloat16 [384, 1536], replicated, may hold values from -0.3125 to 0.3125
- expand_bias: float32 [1536], replicated, may hold values from -3 to 3
- shrink_weight: bfloat16 [1536, 384], replicated, may hold values from -0.15625 to 0.15625
- shrink_bias: float32 [384], replicated, may hold values from -3 to 3
Outputs:
- result: bfloat16 [262144, 384], P(('dp', 'mp'))
- input_gradient: float32 [262144, 384], P(('dp', 'mp'))
- first_gain_gradient: float32 [384], replicated
- first_shift_gradient: float32 [384], replicated
- inward_weight_gradient: float32 [384, 1152], replicated
- inward_bias_gradient: float32 [2, 384], replicated
- outward_weight_gradient: float32 [384, 384], replicated
- outward_bias_gradient: float32 [384], replicated
- second_gain_gradient: float32 [384], replicated
- second_shift_gradient: float32 [384], replicated
- expand_weight_gradient: float32 [384, 1536], replicated
- expand_bias_gradient: float32 [1536], replicated
- shrink_weight_gradient: float32 [1536, 384], replicated
- shrink_bias_gradient: float32 [384], replicated
Inputs may be any that keep to these rules, and one draw needn't show every extreme that they name: `segments`: per pack, image numbers count up from 0 in consecutive runs; each image fills 198 // 3 slots or more and 198 at most, the first image of every pack exactly 198; padding (-1) follows the last image, fills 1 to 198 slots and includes the pack's last slot.
All inputs are finite; a program needn't handle non-finite values.
Results may differ from a plain program's by a relative error of at most 0.02.
Values may be sent and summed in bfloat16 or wider, within the bound.
No kernel may reach another device: no remote copies, remote signals or barrier semaphores. Data moves between devices by JAX's collectives and lax.ppermute only.
A program may use at most 192 MiB of HBM per device.

v0:
```python
from functools import partial

import jax
import jax.numpy as jnp
from jax import lax
from jax.sharding import PartitionSpec as P

HD = 64
SEQ = 198


EPSILON = 1e-06
MASKED = -1000000000.0


def padded(block, sides, width):
    for axis, dim in sides:
        count = lax.axis_size(axis)
        forward = [(i, i + 1) for i in range(count - 1)]
        backward = [(target, source) for source, target in forward]
        low = lax.ppermute(
            lax.slice_in_dim(block, block.shape[dim] - width, None, axis=dim), axis, forward
        )
        high = lax.ppermute(lax.slice_in_dim(block, 0, width, axis=dim), axis, backward)
        block = jnp.concatenate([low, block, high], axis=dim)
    return block


def passed_along(block, axis, distance):
    devices = range(lax.axis_size(axis))
    route = [(i - distance, i) for i in devices if i - distance in devices]
    return lax.ppermute(block, axis, route)


def normalize_parts(rows, gain, shift):
    center = jnp.mean(rows, axis=-1, keepdims=True)
    centred = rows - center
    spread = jnp.mean(centred * centred, axis=-1, keepdims=True)
    inverse = lax.rsqrt(spread + EPSILON)
    scaled = centred * inverse
    return (scaled, inverse, scaled * gain + shift)


def normalize_back(upstream, scaled, inverse, gain):
    direct = upstream * gain
    first_mean = jnp.mean(direct, axis=-1, keepdims=True)
    second_mean = jnp.mean(direct * scaled, axis=-1, keepdims=True)
    return inverse * (direct - first_mean - scaled * second_mean)


def contract_rows(left, right):
    return lax.dot_general(
        left, right, (((0,), (0,)), ((), ())), preferred_element_type=jnp.float32
    )


def contract_cols(left, right):
    return lax.dot_general(
        left, right, (((1,), (1,)), ((), ())), preferred_element_type=jnp.float32
    )


def body(
    layer_input,
    segments,
    cotangent,
    first_gain,
    first_shift,
    inward_weight,
    inward_bias,
    outward_weight,
    outward_bias,
    second_gain,
    second_shift,
    expand_weight,
    expand_bias,
    shrink_weight,
    shrink_bias,
):
    position = lax.axis_index("mp")
    block_rows, width = layer_input.shape
    heads = width // HD
    reach = SEQ - 1
    tile = min(512, block_rows)
    tiles = block_rows // tile
    span = tile + 2 * reach
    factor = HD ** (-0.5)
    rows = layer_input.astype(jnp.float32)
    seg_padded = jnp.pad(segments[0], (reach, reach), constant_values=-2)
    seg_keys = lax.dynamic_slice_in_dim(seg_padded, position * block_rows, block_rows + 2 * reach)
    seg_rows = seg_keys[reach : reach + block_rows]
    own_valid = (seg_rows >= 0).astype(jnp.float32)[:, None]
    indices = jnp.arange(tiles, dtype=jnp.int32)
    scaled1, inverse1, normed1 = normalize_parts(rows, first_gain, first_shift)
    normed1_low = normed1.astype(jnp.bfloat16)
    bias_row = jnp.concatenate([inward_bias[0], jnp.zeros((width,), jnp.float32), inward_bias[1]])
    triple = (
        jnp.dot(normed1_low, inward_weight, preferred_element_type=jnp.float32) + bias_row
    ).astype(jnp.bfloat16)
    queries = triple[:, :width]
    pair_ext = padded(triple[:, width:], (("mp", 0),), reach)

    def tile_scores(index):
        begin = index * tile
        query_tile = lax.dynamic_slice_in_dim(queries, begin, tile, 0).reshape(tile, heads, HD)
        window = lax.dynamic_slice_in_dim(pair_ext, begin, span, 0)
        key_tile = window[:, :width].reshape(span, heads, HD)
        value_tile = window[:, width:].reshape(span, heads, HD)
        seg_query = lax.dynamic_slice_in_dim(seg_rows, begin, tile)
        seg_window = lax.dynamic_slice_in_dim(seg_keys, begin, span)
        allowed = seg_query[:, None] == seg_window[None, :]
        raw = (
            jnp.einsum("qhd,khd->hqk", query_tile, key_tile, preferred_element_type=jnp.float32)
            * factor
        )
        return (query_tile, key_tile, value_tile, jnp.where(allowed[None], raw, MASKED))

    def forward_tile(index):
        query_tile, key_tile, value_tile, scores = tile_scores(index)
        highest = jnp.max(scores, axis=-1, keepdims=True)
        raised = jnp.exp(scores - highest)
        total = jnp.sum(raised, axis=-1, keepdims=True)
        probs_low = (raised / total).astype(jnp.bfloat16)
        outcome = jnp.einsum(
            "hqk,khd->qhd", probs_low, value_tile, preferred_element_type=jnp.float32
        )
        return (
            outcome.reshape(tile, width).astype(jnp.bfloat16),
            (highest + jnp.log(total))[..., 0],
        )

    attended, log_totals = lax.map(forward_tile, indices)
    attended = attended.reshape(block_rows, width)
    middle = (
        rows + jnp.dot(attended, outward_weight, preferred_element_type=jnp.float32) + outward_bias
    )
    scaled2, inverse2, normed2 = normalize_parts(middle, second_gain, second_shift)
    normed2_low = normed2.astype(jnp.bfloat16)
    before = jnp.dot(normed2_low, expand_weight, preferred_element_type=jnp.float32) + expand_bias
    hidden = jax.nn.gelu(before, approximate=False).astype(jnp.bfloat16)
    branch = jnp.dot(hidden, shrink_weight, preferred_element_type=jnp.float32)
    result = ((middle + branch + shrink_bias) * own_valid).astype(jnp.bfloat16)
    back = cotangent.astype(jnp.float32) * own_valid
    back_low = back.astype(jnp.bfloat16)
    shrink_bias_grad = jnp.sum(back, axis=0)
    shrink_grad = contract_rows(hidden, back_low)
    hidden_grad = contract_cols(back_low, shrink_weight)
    unused, gelu_pull = jax.vjp(partial(jax.nn.gelu, approximate=False), before)
    before_grad = gelu_pull(hidden_grad)[0].astype(jnp.bfloat16)
    expand_grad = contract_rows(normed2_low, before_grad)
    expand_bias_grad = jnp.sum(before_grad.astype(jnp.float32), axis=0)
    normed2_grad = contract_cols(before_grad, expand_weight)
    middle_grad = back + normalize_back(normed2_grad, scaled2, inverse2, second_gain)
    second_gain_grad = jnp.sum(normed2_grad * scaled2, axis=0)
    second_shift_grad = jnp.sum(normed2_grad, axis=0)
    outward_bias_grad = jnp.sum(middle_grad, axis=0)
    middle_low = middle_grad.astype(jnp.bfloat16)
    outward_grad = contract_rows(attended, middle_low)
    attended_grad = contract_cols(middle_low, outward_weight).astype(jnp.bfloat16)

    def backward_tile(pair_grads, items):
        index, grad_tile, log_tile = items
        query_tile, key_tile, value_tile, scores = tile_scores(index)
        probs = jnp.exp(scores - log_tile[..., None])
        probs_low = probs.astype(jnp.bfloat16)
        probs_grad = jnp.einsum(
            "qhd,khd->hqk", grad_tile, value_tile, preferred_element_type=jnp.float32
        )
        values_part = jnp.einsum(
            "hqk,qhd->khd", probs_low, grad_tile, preferred_element_type=jnp.float32
        )
        agreement = jnp.sum(probs_grad * probs, axis=-1, keepdims=True)
        scores_grad = (probs * (probs_grad - agreement)).astype(jnp.bfloat16)
        query_grad = (
            (
                jnp.einsum(
                    "hqk,khd->qhd", scores_grad, key_tile, preferred_element_type=jnp.float32
                )
                * factor
            )
            .reshape(tile, width)
            .astype(jnp.bfloat16)
        )
        keys_part = (
            jnp.einsum("hqk,qhd->khd", scores_grad, query_tile, preferred_element_type=jnp.float32)
            * factor
        )
        addition = jnp.concatenate(
            [keys_part.reshape(span, width), values_part.reshape(span, width)], axis=1
        )
        begin = index * tile
        current = lax.dynamic_slice_in_dim(pair_grads, begin, span, 0)
        pair_grads = lax.dynamic_update_slice_in_dim(pair_grads, current + addition, begin, 0)
        return (pair_grads, query_grad)

    pair_start = jnp.zeros((block_rows + 2 * reach, 2 * width), jnp.float32)
    pair_grads, queries_grad = lax.scan(
        backward_tile,
        pair_start,
        (indices, attended_grad.reshape(tiles, tile, heads, HD), log_totals),
    )
    queries_grad = queries_grad.reshape(block_rows, width)
    from_above = passed_along(pair_grads[:reach].astype(jnp.bfloat16), "mp", -1).astype(jnp.float32)
    from_below = passed_along(
        pair_grads[reach + block_rows :].astype(jnp.bfloat16), "mp", 1
    ).astype(jnp.float32)
    own_pairs = pair_grads[reach : reach + block_rows]
    own_pairs = own_pairs + jnp.pad(from_below, ((0, block_rows - reach), (0, 0)))
    own_pairs = own_pairs + jnp.pad(from_above, ((block_rows - reach, 0), (0, 0)))
    triple_grad = jnp.concatenate([queries_grad, own_pairs.astype(jnp.bfloat16)], axis=1)
    inward_grad = contract_rows(normed1_low, triple_grad)
    triple_sums = jnp.sum(triple_grad.astype(jnp.float32), axis=0)
    inward_bias_grad = jnp.stack([triple_sums[:width], triple_sums[2 * width :]])
    normed1_grad = contract_cols(triple_grad, inward_weight)
    input_gradient = middle_grad + normalize_back(normed1_grad, scaled1, inverse1, first_gain)
    first_gain_grad = jnp.sum(normed1_grad * scaled1, axis=0)
    first_shift_grad = jnp.sum(normed1_grad, axis=0)
    grads = (
        first_gain_grad,
        first_shift_grad,
        inward_grad,
        inward_bias_grad,
        outward_grad,
        outward_bias_grad,
        second_gain_grad,
        second_shift_grad,
        expand_grad,
        expand_bias_grad,
        shrink_grad,
        shrink_bias_grad,
    )
    summed = lax.psum(
        (
            grads[0],
            grads[1],
            grads[2],
            grads[3],
            grads[4],
            grads[5],
            grads[6],
            grads[7],
            grads[8],
            grads[9],
            grads[10],
            grads[11],
        ),
        ("dp", "mp"),
    )
    return (
        result,
        input_gradient,
        summed[0],
        summed[1],
        summed[2],
        summed[3],
        summed[4],
        summed[5],
        summed[6],
        summed[7],
        summed[8],
        summed[9],
        summed[10],
        summed[11],
    )


def solution(mesh):
    in_specs = (
        P(("dp", "mp"), None),
        P("dp", None),
        P(("dp", "mp"), None),
        P(),
        P(),
        P(),
        P(),
        P(),
        P(),
        P(),
        P(),
        P(),
        P(),
        P(),
        P(),
    )
    out_specs = (
        P(("dp", "mp"), None),
        P(("dp", "mp"), None),
        P(),
        P(),
        P(),
        P(),
        P(),
        P(),
        P(),
        P(),
        P(),
        P(),
        P(),
        P(),
    )
    return jax.shard_map(body, mesh=mesh, in_specs=in_specs, out_specs=out_specs, check_vma=False)
```

profile of v0, /device:TPU:1, one launch (start us, length us, event | category | flops | bytes accessed | tf_op | source)
XLA Modules:
  0.0 611.1 jit_solution(5194415556272228644)
XLA Ops:
  37.1 19.0 %concatenate.13 = bf16[2442,768]{1,0:T(8,128)(2,1)} concatenate(bf16[197,768]{1,0:T(8,128)(2,1)S(1)} %collective-permute-done, bf16[2048,768]{1,0:T(8,128)(2,1)} %slice.65, bf16[197,768]{1,0:T(8,128)(2,1)S(1)} %collective-permute-done.1), dimensions={0} | concatenate | bytes 7501824 | tf_op jit(solution)/shard_map/concatenate | solution.py:25
  56.1 6.1 %copy.44 = bf16[2442,768]{0,1:T(8,128)(2,1)} copy(bf16[2442,768]{1,0:T(8,128)(2,1)} %concatenate.13) | data formatting | bytes 7501824 | tf_op jit(solution)/shard_map/while | solution.py:132
  64.0 67.6 %while.24 = (s32[]{:T(128)}, bf16[4,512,384]{2,1,0:T(8,128)(2,1)}, f32[4,6,512]{2,1,0:T(8,128)}, s32[4]{0:T(128)}, bf16[2442,768]{0,1:T(8,128)(2,1)}, /*index=5*...) while((s32[]{:T(128)}, bf16[4,512,384]{2,1,0:T(8,128)(2,1)}, ...), condition=%wide.region_5.6_spmd, body=%wide.region_2.5_spmd.sunk | while | flops 746563584 | bytes 42747804 | solution.py:132
  135.1 33.8 %multiply_convert_fusion.1 = (bf16[2048,1536]{1,0:T(8,128)(2,1)}, f32[2048,1536]{1,0:T(8,128)}, f32[2048,1536]{1,0:T(8,128)}) fusion(f32[1536]{0:T(1024)S(1)} %copy-done.40, bf16[384,1536]{1,0:T(8,128)(2,1)S(1)} %copy-done, f32[2048,384]{0,1:T(8,128)S(1)} %get-tuple-element.256, f32[384]{0:T(512)S(1)} %copy-done.41, f32[384]{0:T(512)S(1)} %copy-done.29, ...), kind=kOutput, calls=%fused_computation.42 | convolution fusion | flops 2627469312 | bytes 35808256 | tf_op jit(solution)/shard_map/dot_general | solution.py:139
  168.9 16.6 %convert_reduce_fusion = (f32[1536]{0:T(1024)}, bf16[2048,1536]{1,0:T(8,128)(2,1)}) fusion(f32[2048,1536]{1,0:T(8,128)} %get-tuple-element.239, bf16[1536,384]{1,0:T(8,128)(2,1)S(1)} %copy-done.37, bf16[2048,384]{0,1:T(8,128)(2,1)S(1)} %copy-done.14, f32[2048]{0:T(1024)S(1)} %copy-done.27, f32[2048,1536]{1,0:T(8,128)} %get-tuple-element.257, ...), kind=kOutput, calls=%fused_computation.40 | convolution fusion | flops 2471754240 | bytes 34230272 | tf_op jit(solution)/shard_map/dot_general | solution.py:58
  185.4 7.0 %fusion.56 = f32[384,1536]{1,0:T(8,128)} fusion(bf16[2048,1536]{1,0:T(8,128)(2,1)} %get-tuple-element.263, f32[2048,384]{0,1:T(8,128)S(1)} %get-tuple-element.256, f32[384]{0:T(512)S(1)} %copy-done.41, f32[384]{0:T(512)S(1)} %copy-done.29, f32[2048]{0:T(1024)S(1)} %add_rsqrt_fusion, f32[2048]{0:T(1024)S(1)} %broadcast_multiply_fusion.4), kind=kOutput, calls=%fused_computation.115 | convolution fusion | flops 2419851264 | bytes 11815936 | tf_op jit(solution)/shard_map/dot_general | solution.py:52
  192.4 5.7 fusion.66
  198.2 5.0 fusion.44
  224.7 180.9 %while.25 = (s32[]{:T(128)}, f32[2442,768]{0,1:T(8,128)}, bf16[4,512,384]{2,1,0:T(8,128)(2,1)}, s32[4]{0:T(128)S(1)}, bf16[2048,384]{0,1:T(8,128)(2,1)}, /*index...) while((s32[]{:T(128)}, f32[2442,768]{0,1:T(8,128)}, ...), condition=%wide.region_12.13_spmd, body=%wide.region_10.12_spmd.sunk | while | flops 1825610496 | bytes 116917688 | solution.py:197
  233.6 5.1 fusion.128
  238.7 4.8 multiply_reduce_fusion.7
  255.5 15.0 %dynamic_update_slice.24 = f32[2442,768]{0,1:T(8,128)} dynamic-update-slice(f32[2442,768]{0,1:T(8,128)} %get-tuple-element.451, f32[906,768]{0,1:T(8,128)S(1)} %maximum_add_fusion.2, s32[]{:T(128)S(6)} %select_n.68, s32[]{:T(128)} %constant.77.clone.1..sunk.1) | dynamic-update-slice | bytes 5566468 | tf_op jit(solution)/shard_map/while/body/eval_jaxpr/dynamic_update_slice | solution.py:193
  279.2 5.1 fusion.128
  284.3 4.8 multiply_reduce_fusion.7
  301.0 15.0 %dynamic_update_slice.24 = f32[2442,768]{0,1:T(8,128)} dynamic-update-slice(f32[2442,768]{0,1:T(8,128)} %get-tuple-element.451, f32[906,768]{0,1:T(8,128)S(1)} %maximum_add_fusion.2, s32[]{:T(128)S(6)} %select_n.68, s32[]{:T(128)} %constant.77.clone.1..sunk.1) | dynamic-update-slice | bytes 5566468 | tf_op jit(solution)/shard_map/while/body/eval_jaxpr/dynamic_update_slice | solution.py:193
  324.8 5.1 fusion.128
  329.9 4.8 multiply_reduce_fusion.7
  346.7 14.6 %dynamic_update_slice.24 = f32[2442,768]{0,1:T(8,128)} dynamic-update-slice(f32[2442,768]{0,1:T(8,128)} %get-tuple-element.451, f32[906,768]{0,1:T(8,128)S(1)} %maximum_add_fusion.2, s32[]{:T(128)S(6)} %select_n.68, s32[]{:T(128)} %constant.77.clone.1..sunk.1) | dynamic-update-slice | bytes 5566468 | tf_op jit(solution)/shard_map/while/body/eval_jaxpr/dynamic_update_slice | solution.py:193
  370.0 5.1 fusion.128
  375.0 4.8 multiply_reduce_fusion.7
  391.7 13.8 %dynamic_update_slice.24 = f32[2442,768]{0,1:T(8,128)} dynamic-update-slice(f32[2442,768]{0,1:T(8,128)} %get-tuple-element.451, f32[906,768]{0,1:T(8,128)S(1)} %maximum_add_fusion.2, s32[]{:T(128)S(6)} %select_n.68, s32[]{:T(128)} %constant.77.clone.1..sunk.1) | dynamic-update-slice | bytes 5566468 | tf_op jit(solution)/shard_map/while/body/eval_jaxpr/dynamic_update_slice | solution.py:193
  434.8 7.9 %multiply_convert_fusion.2 = bf16[2048,384]{0,1:T(8,128)(2,1)} fusion(f32[2048,384]{0,1:T(8,128)} %copy-done.4, bf16[2048,1536]{1,0:T(8,128)(2,1)} %get-tuple-element.238, bf16[1536,384]{1,0:T(8,128)(2,1)} %param.32, f32[2048]{0:T(1024)S(1)} %copy-done.28, f32[384]{0:T(512)S(1)} %copy-done.44), kind=kOutput, calls=%fused_computation.85 | convolution fusion | flops 2419064832 | bytes 12199424 | tf_op jit(solution)/shard_map/dot_general | solution.py:141
  468.9 68.6 %all-reduce.3 = (f32[384]{0:T(512)}, f32[384]{0:T(512)}, f32[2,384]{1,0:T(2,128)}, f32[384]{0:T(512)}, f32[384]{0:T(512)}, /*index=5*/f32[384]{0:T(512)}, f32[1536]{0:T(1024)}, f32[384]{0:T(512)}) all-reduce(f32[384]{0:T(512)S(1)} %get-tuple-element.180, ...), channel_id=1, replica_groups=mesh['dp'=32,'mp'=4] {'dp','mp'}, use_global_device_ids=true, to_apply=%region_16.17 | all-reduce | flops 4608 | bytes 36864 | tf_op jit(solution)/shard_map/psum | solution.py:232
  537.5 59.8 %all-reduce.7.cloned.1.call-done = (f32[384,1152]{1,0:T(8,128)}, f32[384,384]{1,0:T(8,128)}, f32[384,1536]{1,0:T(8,128)}, f32[1536,384]{1,0:T(8,128)}) async-done(((f32[384,1152]{1,0:T(8,128)}, f32[384,384]{1,0:T(8,128)}, f32[384,1536]{1,0:T(8,128)}, f32[1536,384]{1,0:T(8,128)}), (f32[384,1152]{1,0:T(8,128)}, f32[384,384]{1,0:T(8,128)}, f32[384,1536]{1,0:T(8,128)}, ...) | async-done | bytes 7077904 | tf_op jit(solution)/shard_map/psum | solution.py:232
  (282 shorter events, 262.8 us)
Async XLA Ops:
  7.2 127.5 %copy-start = (bf16[384,1536]{1,0:T(8,128)(2,1)S(1)}, bf16[384,1536]{1,0:T(8,128)(2,1)}, u32[]{:S(2)}) copy-start(bf16[384,1536]{1,0:T(8,128)(2,1)} %param.30) | copy-start | bytes 3538948
  7.2 590.2 %all-reduce.7.cloned.1.call-start = ((), (), s32[]{:S(2)}) async-start(), calls=%async_computation | async-start | bytes 14155776 | tf_op jit(solution)/shard_map/psum | solution.py:232
  9.8 121.8 %copy-start.2 = (bf16[2048,384]{0,1:T(8,128)(2,1)}, bf16[2048,384]{0,1:T(8,128)(2,1)S(1)}, u32[]{:S(2)}) copy-start(bf16[2048,384]{0,1:T(8,128)(2,1)S(1)} %copy.43) | copy-start | bytes 4718596
  10.1 4.8 copy-start.22
  17.9 19.1 %collective-permute-start.1 = (bf16[197,768]{1,0:T(8,128)(2,1)}, bf16[197,768]{1,0:T(8,128)(2,1)S(1)}, u32[]{:S(2)}, u32[]{:S(2)}) collective-permute-start(bf16[197,768]{1,0:T(8,128)(2,1)} %get-tuple-element.248), channel_id=1, source_target_pairs={{1,0},{2,1},{3,2},{5,4},{6,5},{7,6},{9,8},{10,9},{11,10},{13,12},{... | collective-permute-start | bytes 907784 | tf_op jit(solution)/shard_map/ppermute | solution.py:24
  19.2 17.8 %collective-permute-start = (bf16[197,768]{1,0:T(8,128)(2,1)}, bf16[197,768]{1,0:T(8,128)(2,1)S(1)}, u32[]{:S(2)}, u32[]{:S(2)}) collective-permute-start(bf16[197,768]{1,0:T(8,128)(2,1)} %get-tuple-element.249), channel_id=1, source_target_pairs={{0,1},{1,2},{2,3},{4,5},{5,6},{6,7},{8,9},{9,10},{10,11},{12,13},{... | collective-permute-start | bytes 907784 | tf_op jit(solution)/shard_map/ppermute | solution.py:21
  30.5 5.2 copy-start.24
  134.2 51.2 %copy-start.4 = (f32[2048,384]{0,1:T(8,128)}, f32[2048,384]{0,1:T(8,128)S(1)}, u32[]{:S(2)}) copy-start(f32[2048,384]{0,1:T(8,128)S(1)} %get-tuple-element.256) | copy-start | bytes 9437188
  135.1 33.8 %copy-start.14 = (bf16[2048,384]{0,1:T(8,128)(2,1)S(1)}, bf16[2048,384]{0,1:T(8,128)(2,1)}, u32[]{:S(2)}) copy-start(bf16[2048,384]{0,1:T(8,128)(2,1)} %copy.48) | copy-start | bytes 4718596
  135.1 33.8 %copy-start.27 = (f32[2048]{0:T(1024)S(1)}, f32[2048]{0:T(1024)}, u32[]{:S(2)}) copy-start(f32[2048]{0:T(1024)} %get-tuple-element.236) | copy-start | bytes 24580
  135.1 33.8 %copy-start.37 = (bf16[1536,384]{1,0:T(8,128)(2,1)S(1)}, bf16[1536,384]{1,0:T(8,128)(2,1)}, u32[]{:S(2)}) copy-start(bf16[1536,384]{1,0:T(8,128)(2,1)} %param.32) | copy-start | bytes 3538948
  185.4 7.0 %copy-start.46 = (bf16[2048,1536]{1,0:T(8,128)(2,1)S(1)}, bf16[2048,1536]{1,0:T(8,128)(2,1)}, u32[]{:S(2)}) copy-start(bf16[2048,1536]{1,0:T(8,128)(2,1)} %get-tuple-element.263) | copy-start | bytes 18874372
  192.4 5.8 copy-start.45
  407.5 18.7 %slice-start = ((s8[7864320]{0:T(1024)(128)(4,1)}), s8[4194304]{0:T(1024)(128)(4,1)S(1)}, s32[]{:S(2)}) async-start(s8[7864320]{0:T(1024)(128)(4,1)} %bitcast.114), calls=%async_computation.1 | async-start | bytes 8388608
  407.5 9.0 %copy-start.7 = (f32[2048,384]{0,1:T(8,128)S(1)}, f32[2048,384]{0,1:T(8,128)}, u32[]{:S(2)}) copy-start(f32[2048,384]{0,1:T(8,128)} %copy-done.6) | copy-start | bytes 9437188
  407.5 9.0 %copy-start.11 = (bf16[4,512,384]{2,1,0:T(8,128)(2,1)S(1)}, bf16[4,512,384]{2,1,0:T(8,128)(2,1)}, u32[]{:S(2)}) copy-start(bf16[4,512,384]{2,1,0:T(8,128)(2,1)} %get-tuple-element.110) | copy-start | bytes 4718596
  407.5 18.7 %slice-start.1 = ((s8[7864320]{0:T(1024)(128)(4,1)}), s8[3670016]{0:T(1024)(128)(4,1)S(1)}, s32[]{:S(2)}) async-start(s8[7864320]{0:T(1024)(128)(4,1)} %bitcast.114), calls=%async_computation.2 | async-start | bytes 7340032
  411.5 10.8 %collective-permute-start.2 = (bf16[197,768]{0,1:T(8,128)(2,1)S(1)}, bf16[197,768]{0,1:T(8,128)(2,1)S(1)}, u32[]{:S(2)}, u32[]{:S(2)}) collective-permute-start(bf16[197,768]{0,1:T(8,128)(2,1)S(1)} %get-tuple-element.250), channel_id=1, source_target_pairs={{0,1},{1,2},{2,3},{4,5},{5,6},{6,7},{8,9},{9,10},{10,11},{12,13},{... | collective-permute-start | bytes 907784 | tf_op jit(solution)/shard_map/ppermute | solution.py:32
  415.2 11.0 %collective-permute-start.3 = (bf16[197,768]{0,1:T(8,128)(2,1)S(1)}, bf16[197,768]{0,1:T(8,128)(2,1)S(1)}, u32[]{:S(2)}, u32[]{:S(2)}) collective-permute-start(bf16[197,768]{0,1:T(8,128)(2,1)S(1)} %get-tuple-element.251), channel_id=1, source_target_pairs={{1,0},{2,1},{3,2},{5,4},{6,5},{7,6},{9,8},{10,9},{11,10},{13,12},{... | collective-permute-start | bytes 907784 | tf_op jit(solution)/shard_map/ppermute | solution.py:32
  418.3 12.1 %copy-start.3 = (bf16[2048,384]{0,1:T(8,128)(2,1)S(1)}, bf16[2048,384]{0,1:T(8,128)(2,1)}, u32[]{:S(2)}) copy-start(bf16[2048,384]{0,1:T(8,128)(2,1)} %copy-done.2) | copy-start | bytes 4718596
  418.3 12.1 %copy-start.23 = (f32[2048]{0:T(1024)S(1)}, f32[2048]{0:T(1024)}, u32[]{:S(2)}) copy-start(f32[2048]{0:T(1024)} %copy-done.22) | copy-start | bytes 24580
  418.3 12.1 %copy-start.26 = (f32[2048]{0:T(1024)S(1)}, f32[2048]{0:T(1024)}, u32[]{:S(2)}) copy-start(f32[2048]{0:T(1024)} %copy-done.25) | copy-start | bytes 24580
  418.4 12.1 %copy-start.31 = (f32[384]{0:T(512)S(1)}, f32[384]{0:T(512)}, u32[]{:S(2)}) copy-start(f32[384]{0:T(512)} %param.22) | copy-start | bytes 4612
  418.4 12.1 %copy-start.43 = (f32[384]{0:T(512)S(1)}, f32[384]{0:T(512)}, u32[]{:S(2)}) copy-start(f32[384]{0:T(512)} %param.23) | copy-start | bytes 4612
  (36 other events, 95.5 us)
Sparse Core Ops, SparseCore 0:
  434.3 163.0 all-reduce.6
where the time goes:
time: 619 us; the launch traced here: 611 us
  local copies, waits for them, and re-layouts  204 us (33%)
  matrix products  172 us (28%)
  blocking collectives  68.6 us (11%)
  other arithmetic  67.8 us (11%)
  waiting for transfers between devices  67.6 us (11%)
  between operations  14.8 us (2%)
  starting transfers between devices  11 us (2%)
    psum x1, blocking collectives, body(): lax.psum((grads[0], grads[1], grads[2], grads[3], grads[4], grads[5], gra...  68.6 us
    psum x1, waiting for transfers between devices, body(): lax.psum((grads[0], grads[1], grads[2], grads[3], grads[4], grads[5], gra...  59.8 us
    dynamic_update_slice x4, local copies, waits for them, and re-layouts, backward_tile(): lax.dynamic_update_slice_in_dim(pair_grads, current + addition, begin, 0)  58.3 us
    dot_general x1, matrix products, body(): jnp.dot(normed2_low, expand_weight, preferred_element_type=jnp.float32)  33.8 us
    dot_general x4, matrix products, contract_cols(): lax.dot_general(left, right, (((1,), (1,)), ((), ())), preferred_element_...  28.1 us
    unnamed x102, local copies, waits for them, and re-layouts  25 us
    dot_general x4, matrix products, backward_tile(): jnp.einsum('hqk,qhd->khd', probs_low, grad_tile, preferred_element_type=j...  20.3 us
    dot_general x4, matrix products, backward_tile(): jnp.einsum('qhd,khd->hqk', grad_tile, value_tile, preferred_element_type=...  19.2 us
  transfers between devices with their start and end apart: 5, of which 3 were waited for; matrix products, arithmetic and copies ran while one was open for 8% of the time, Pallas kernels for 0%

commit v1 on v0

v1 whole, which is shorter than its diff:
```python
from functools import partial

import jax
import jax.numpy as jnp
from jax import lax
from jax.experimental import pallas as pl
from jax.experimental.pallas import tpu as pltpu
from jax.sharding import PartitionSpec as P

HD = 64
SEQ = 198
EPSILON = 1e-06
MASKED = -1000000000.0
WIN = 256
TILE = 256
HALO = 208
GROUPS = 24
LANES = 128
BIG = 1 << 20
F32 = jnp.float32
BF16 = jnp.bfloat16
NT = (((1,), (1,)), ((), ()))
TN = (((0,), (0,)), ((), ()))


def dot(a, b):
    return jnp.dot(a, b, preferred_element_type=F32)


def dot_nt(a, b):
    return lax.dot_general(a, b, NT, preferred_element_type=F32)


def dot_tn(a, b):
    return lax.dot_general(a, b, TN, preferred_element_type=F32)


def normalize(rows):
    center = jnp.mean(rows, axis=-1, keepdims=True)
    centred = rows - center
    spread = jnp.mean(centred * centred, axis=-1, keepdims=True)
    inverse = lax.rsqrt(spread + EPSILON)
    return centred * inverse, inverse


def normalize_back(upstream, scaled, inverse, gain):
    direct = upstream * gain
    first = jnp.mean(direct, axis=-1, keepdims=True)
    second = jnp.mean(direct * scaled, axis=-1, keepdims=True)
    return inverse * (direct - first - scaled * second)


def gelu_parts(v):
    size = jnp.abs(v)
    den = 1.0 + (0.3275911 * 0.7071067811865476) * size
    t = pl.reciprocal(den, approx=True)
    t = t * (2.0 - den * t)
    bell = jnp.exp(-0.5 * (v * v))
    poly = t * (
        0.5 * 0.254829592
        + t * (-0.5 * 0.284496736 + t * (0.5 * 1.421413741 + t * (-0.5 * 1.453152027 + t * (0.5 * 1.061405429))))
    )
    tail = poly * bell
    cdf = jnp.where(v >= 0.0, 1.0 - tail, tail)
    return v * cdf, cdf + v * (0.3989422804014327 * bell)


def find_next(seg_ref, start, ident, steps, low, high):
    def step(_, pair):
        lo, hi = pair
        mid = (lo + hi) // 2
        value = seg_ref[0, jnp.minimum(mid, seg_ref.shape[1] - 1)]
        above = jnp.logical_or(jnp.logical_or(value < 0, value > ident), mid >= seg_ref.shape[1])
        return jnp.where(above, lo, mid + 1), jnp.where(above, mid, hi)

    return lax.fori_loop(0, steps, step, (low, high))[0]


def plan_groups(seg_ref, position, last, rows, table):
    slots = seg_ref.shape[1]
    base = position * rows
    before_id = seg_ref[0, jnp.maximum(base - 1, 0)]
    first = find_next(seg_ref, base, before_id, 8, base, base + SEQ)
    first = jnp.where(position == 0, 0, first)
    end_id = seg_ref[0, base + rows - 1]
    last_end = find_next(seg_ref, base, end_id, 8, base + rows, jnp.minimum(base + rows + SEQ, slots))
    pad_start = find_next(seg_ref, base, BIG, 8, slots - SEQ, slots)
    end = jnp.where(last, pad_start, last_end) - base
    first = first - base

    def body(state):
        at, group, window, start, c1, c2 = state
        ident = seg_ref[0, base + at]
        after = find_next(seg_ref, base, ident, 8, base + at + SEQ // 3, base + at + SEQ + 1) - base
        after = jnp.minimum(after, end)
        fits = after - window <= WIN

        @pl.when(jnp.logical_not(fits))
        def _():
            write_group(table, group, window, start, c1, c2, at)

        group = jnp.where(fits, group, group + 1)
        new_c1 = jnp.where(fits, jnp.where(at == start, c1, jnp.where(c1 < 0, at, c1)), -1)
        new_c2 = jnp.where(fits, jnp.where(jnp.logical_and(at != start, c1 >= 0), jnp.where(c2 < 0, at, c2), c2), -1)
        start = jnp.where(fits, start, at)
        window = jnp.where(fits, window, (at // 16) * 16)
        return after, group, window, start, new_c1, new_c2

    init = (first, jnp.int32(0), (first // 16) * 16, first, jnp.int32(-1), jnp.int32(-1))
    at, group, window, start, c1, c2 = lax.while_loop(lambda s: s[0] < end, body, init)
    write_group(table, group, window, start, c1, c2, at)
    table[GROUPS, 0] = group + 1
    table[GROUPS, 1] = first
    table[GROUPS, 2] = end
    return group + 1, first, end


def write_group(table, group, window, start, c1, c2, end):
    table[group, 0] = window
    table[group, 1] = start - window
    table[group, 2] = jnp.where(c1 < 0, end, c1) - window
    table[group, 3] = jnp.where(c2 < 0, end, c2) - window
    table[group, 4] = end - window


def group_bias(table, group):
    bounds = [table[group, i] for i in range(1, 5)]
    row = lax.broadcasted_iota(jnp.int32, (WIN, WIN), 0)
    col = lax.broadcasted_iota(jnp.int32, (WIN, WIN), 1)

    def ident(index):
        return sum((index >= b).astype(jnp.int32) for b in bounds)

    return jnp.where(ident(row) == ident(col), 0.0, MASKED)


def head_masks():
    lane = lax.broadcasted_iota(jnp.int32, (WIN, 2 * HD), 1)
    return lane < HD, lane >= HD


def keep_first(ref, window, begin, cols, value):
    head = pl.ds(window, 16)
    old = ref[head, cols]
    row = lax.broadcasted_iota(jnp.int32, (16, 2 * HD), 0)
    ref[head, cols] = jnp.where(row >= begin, value[:16].astype(F32), old.astype(F32)).astype(BF16)
    ref[pl.ds(window + 16, WIN - 16), cols] = value[16:].astype(BF16)


def attend_group(group, table, triple, attended, stats):
    width = attended.shape[1]
    window = pl.multiple_of(table[group, 0], 16)
    rows = pl.ds(window, WIN)
    begin = table[group, 1]
    bias = group_bias(table, group)
    masks = head_masks()
    for pair in range(width // (2 * HD)):
        cols = pl.ds(pair * 2 * HD, 2 * HD)
        query = triple[rows, pl.ds(pair * 2 * HD, 2 * HD)]
        key = triple[rows, pl.ds(width + pair * 2 * HD, 2 * HD)]
        value = triple[rows, pl.ds(2 * width + pair * 2 * HD, 2 * HD)]
        value_t = value.T
        outs = []
        for h in range(2):
            masked = jnp.where(masks[h], query, jnp.zeros_like(query))
            scores = dot_nt(key, masked) + bias
            highest = jnp.max(scores, axis=0, keepdims=True)
            raised = jnp.exp(scores - highest)
            total = jnp.sum(raised, axis=0, keepdims=True)
            out = dot(value_t[h * HD : (h + 1) * HD], raised.astype(BF16))
            outs.append(out * (1.0 / total))
            stats[group, pl.ds(2 * pair + h, 1), :] = highest + jnp.log(total)
        keep_first(attended, window, begin, cols, jnp.concatenate(outs, axis=0).T)


def attend_back_group(group, table, triple, attended, upstream, stats, triple_grad):
    width = attended.shape[1]
    window = pl.multiple_of(table[group, 0], 16)
    rows = pl.ds(window, WIN)
    begin = table[group, 1]
    bias = group_bias(table, group)
    masks = head_masks()
    for pair in range(width // (2 * HD)):
        cols = pl.ds(pair * 2 * HD, 2 * HD)
        query = triple[rows, pl.ds(pair * 2 * HD, 2 * HD)]
        key = triple[rows, pl.ds(width + pair * 2 * HD, 2 * HD)]
        value = triple[rows, pl.ds(2 * width + pair * 2 * HD, 2 * HD)]
        out_t = attended[rows, cols].T.astype(F32)
        up = upstream[rows, cols]
        up_t = up.T
        product = out_t * up_t.astype(F32)
        key_t = key.T
        query_grads = []
        key_grad = jnp.zeros((WIN, 2 * HD), F32)
        value_grad = jnp.zeros((WIN, 2 * HD), F32)
        for h in range(2):
            masked = jnp.where(masks[h], query, jnp.zeros_like(query))
            lse = stats[group, pl.ds(2 * pair + h, 1), :]
            probs = jnp.exp(dot_nt(key, masked) + bias - lse)
            up_masked = jnp.where(masks[h], up, jnp.zeros_like(up))
            probs_grad = dot_nt(value, up_masked)
            agreement = jnp.sum(product[h * HD : (h + 1) * HD], axis=0, keepdims=True)
            scores_grad = (probs * (probs_grad - agreement)).astype(BF16)
            value_grad = value_grad + dot(probs.astype(BF16), up_masked)
            key_grad = key_grad + dot(scores_grad, masked)
            query_grads.append(dot(key_t[h * HD : (h + 1) * HD], scores_grad) * HD ** (-0.5))
        keep_first(triple_grad, window, begin, cols, jnp.concatenate(query_grads, axis=0).T)
        keep_first(triple_grad, window, begin, pl.ds(width + pair * 2 * HD, 2 * HD), key_grad)
        keep_first(triple_grad, window, begin, pl.ds(2 * width + pair * 2 * HD, 2 * HD), value_grad)


def interval(tile, first, end):
    row = lax.broadcasted_iota(jnp.int32, (TILE, 1), 0) + tile * TILE
    return jnp.logical_and(row >= first, row < end)


def kernel_one(
    place, seg, x_ref, x_halo, cot_ref, cot_halo, gain1, shift1, w_in, b_in, w_out, b_out, gain2, shift2,
    w_ex, b_ex, w_sh, b_sh,
    result, result_halo, triple, attended, upstream, middle_grad, stats, table, mine, other,
    d_ex, d_sh, d_out, small,
):
    rows, width = x_ref.shape
    tiles = triple.shape[0] // TILE
    groups, first, end = plan_groups(seg, place[0], place[1] == 1, rows, table)
    attended[...] = jnp.zeros_like(attended)
    d_ex[...] = jnp.zeros_like(d_ex)
    d_sh[...] = jnp.zeros_like(d_sh)
    d_out[...] = jnp.zeros_like(d_out)
    small[...] = jnp.zeros_like(small)

    def load(ref, halo, tile):
        spot = pl.ds(pl.multiple_of(jnp.minimum(tile, tiles - 2) * TILE, TILE), TILE)
        return jnp.where(tile == tiles - 1, halo[...].astype(F32), ref[spot, :].astype(F32))

    def project(tile, _):
        scaled, _inverse = normalize(load(x_ref, x_halo, tile))
        normed = (scaled * gain1[...] + shift1[...]).astype(BF16)
        spot = pl.ds(pl.multiple_of(tile * TILE, TILE), TILE)
        q = dot(normed, w_in[:, :width]) + b_in[0:1, :]
        triple[spot, :width] = (q.astype(BF16).astype(F32) * HD ** (-0.5)).astype(BF16)
        triple[spot, width : 2 * width] = dot(normed, w_in[:, width : 2 * width]).astype(BF16)
        triple[spot, 2 * width :] = (dot(normed, w_in[:, 2 * width :]) + b_in[1:2, :]).astype(BF16)
        return 0

    lax.fori_loop(0, tiles, project, 0)

    def attend(group, _):
        attend_group(group, table, triple, attended, stats)
        return 0

    lax.fori_loop(0, groups, attend, 0)

    hidden_width = w_ex.shape[1]
    chunk = 512

    def feed(tile, _):
        spot = pl.ds(pl.multiple_of(tile * TILE, TILE), TILE)
        keep = interval(tile, first, end)
        att = attended[spot, :]
        middle = load(x_ref, x_halo, tile) + dot(att, w_out[...]) + b_out[...]
        scaled, inverse = normalize(middle)
        normed = (scaled * gain2[...] + shift2[...]).astype(BF16)
        back = jnp.where(keep, load(cot_ref, cot_halo, tile), 0.0)
        back_low = back.astype(BF16)
        branch = jnp.zeros((TILE, width), F32)
        normed_grad = jnp.zeros((TILE, width), F32)
        for begin in range(0, hidden_width, chunk):
            cols = slice(begin, begin + chunk)
            before = dot(normed, w_ex[:, cols]) + b_ex[:, cols]
            value, slope = gelu_parts(before)
            hidden = value.astype(BF16)
            branch = branch + dot(hidden, w_sh[cols, :])
            before_grad = (dot_nt(back_low, w_sh[cols, :]) * slope)
            before_low = before_grad.astype(BF16)
            normed_grad = normed_grad + dot_nt(before_low, w_ex[:, cols])
            d_sh[:, cols] += dot_tn(back_low, hidden)
            d_ex[:, cols] += dot_tn(normed, before_low)
            small[8:9, cols] += jnp.sum(before_low.astype(F32), axis=0, keepdims=True)
        out = jnp.where(keep, middle + branch + b_sh[...], 0.0).astype(BF16)

        @pl.when(tile < tiles - 1)
        def _():
            result[pl.ds(pl.multiple_of(jnp.minimum(tile, tiles - 2) * TILE, TILE), TILE), :] = out

        @pl.when(tile == tiles - 1)
        def _():
            result_halo[...] = out

        small[0:1, :width] += jnp.sum(back, axis=0, keepdims=True)
        small[1:2, :width] += jnp.sum(normed_grad * scaled, axis=0, keepdims=True)
        small[2:3, :width] += jnp.sum(normed_grad, axis=0, keepdims=True)
        grad = back + normalize_back(normed_grad, scaled, inverse, gain2[...])
        small[3:4, :width] += jnp.sum(grad, axis=0, keepdims=True)
        middle_grad[spot, :] = grad
        grad_low = grad.astype(BF16)
        d_out[...] += dot_tn(att, grad_low)
        upstream[spot, :] = dot_nt(grad_low, w_out[...]).astype(BF16)
        return 0

    lax.fori_loop(0, tiles, feed, 0)
    pack((d_ex, d_sh, d_out), small, place[2], mine, other)


def pack(grads, small, core, mine, other):
    half = grads[0].shape[0] // 2
    at = 0
    for grad in grads:
        for begin in range(0, grad.shape[1], LANES):
            cols = slice(begin, begin + LANES)
            mine[pl.ds(at, half), :] = grad[pl.ds(pl.multiple_of(core * half, half), half), cols].astype(BF16)
            other[pl.ds(at, half), :] = grad[pl.ds(pl.multiple_of((1 - core) * half, half), half), cols].astype(BF16)
            at += half
    rest = mine.shape[0] - at
    mine[pl.ds(at, rest), :] = jnp.zeros((rest, LANES), BF16)
    other[pl.ds(at, rest), :] = jnp.zeros((rest, LANES), BF16)
    count = small.shape[1] // LANES
    for index in range(count):
        cols = slice(index * LANES, (index + 1) * LANES)
        spot = pl.ds(at + (index // 2) * 16, 16)

        @pl.when(core == index % 2)
        def _():
            mine[spot, :] = small[:, cols].astype(BF16)

        @pl.when(core != index % 2)
        def _():
            other[spot, :] = small[:, cols].astype(BF16)


def kernel_two(
    place, table, x_ref, x_halo, gain1, shift1, w_in, triple, attended, upstream, middle_grad, stats,
    input_grad, input_halo, mine, other, triple_grad, d_in, small,
):
    rows, width = x_ref.shape
    tiles = triple.shape[0] // TILE
    triple_grad[...] = jnp.zeros_like(triple_grad)
    d_in[...] = jnp.zeros_like(d_in)
    small[...] = jnp.zeros_like(small)

    def attend(group, _):
        attend_back_group(group, table, triple, attended, upstream, stats, triple_grad)
        return 0

    lax.fori_loop(0, table[GROUPS, 0], attend, 0)

    def load(ref, halo, tile):
        spot = pl.ds(pl.multiple_of(jnp.minimum(tile, tiles - 2) * TILE, TILE), TILE)
        return jnp.where(tile == tiles - 1, halo[...].astype(F32), ref[spot, :].astype(F32))

    def project(tile, _):
        spot = pl.ds(pl.multiple_of(tile * TILE, TILE), TILE)
        scaled, inverse = normalize(load(x_ref, x_halo, tile))
        normed = (scaled * gain1[...] + shift1[...]).astype(BF16)
        grad = triple_grad[spot, :]
        d_in[...] += dot_tn(normed, grad)
        small[4:5, : 3 * width] += jnp.sum(grad.astype(F32), axis=0, keepdims=True)
        normed_grad = dot_nt(grad, w_in[...])
        small[5:6, :width] += jnp.sum(normed_grad * scaled, axis=0, keepdims=True)
        small[6:7, :width] += jnp.sum(normed_grad, axis=0, keepdims=True)
        out = middle_grad[spot, :] + normalize_back(normed_grad, scaled, inverse, gain1[...])

        @pl.when(tile < tiles - 1)
        def _():
            input_grad[pl.ds(pl.multiple_of(jnp.minimum(tile, tiles - 2) * TILE, TILE), TILE), :] = out

        @pl.when(tile == tiles - 1)
        def _():
            input_halo[...] = out

        return 0

    lax.fori_loop(0, tiles, project, 0)
    pack((d_in,), small, place[2], mine, other)


VMEM = pl.BlockSpec(memory_space=pltpu.VMEM)
SMEM = pl.BlockSpec(memory_space=pltpu.SMEM)


def packed_rows(columns, small, pieces):
    half = columns // LANES * 192 + (small // LANES + 1) // 2 * 16
    return pieces * (-(-half // (8 * pieces)) * 8)


def forward_one(place, segments, x, x_halo, cot, cot_halo, weights, pieces):
    rows, width = x.shape
    total = rows + TILE
    hidden = weights[8].shape[1]
    packed = packed_rows(2 * hidden + width, hidden, pieces)
    shapes = (
        jax.ShapeDtypeStruct((rows, width), BF16),
        jax.ShapeDtypeStruct((TILE, width), BF16),
        jax.ShapeDtypeStruct((total, 3 * width), BF16),
        jax.ShapeDtypeStruct((total, width), BF16),
        jax.ShapeDtypeStruct((total, width), BF16),
        jax.ShapeDtypeStruct((total, width), F32),
        jax.ShapeDtypeStruct((GROUPS, 8, WIN), F32),
        jax.ShapeDtypeStruct((GROUPS + 1, 8), jnp.int32),
        jax.ShapeDtypeStruct((packed, LANES), BF16),
        jax.ShapeDtypeStruct((packed, LANES), BF16),
    )
    return pl.pallas_call(
        kernel_one,
        out_shape=shapes,
        in_specs=[SMEM, SMEM] + [VMEM] * 16,
        out_specs=tuple([VMEM] * 7 + [SMEM] + [VMEM] * 2),
        scratch_shapes=[
            pltpu.VMEM((width, hidden), F32),
            pltpu.VMEM((width, hidden), F32),
            pltpu.VMEM((width, width), F32),
            pltpu.VMEM((16, hidden), F32),
        ],
        compiler_params=pltpu.CompilerParams(vmem_limit_bytes=60 * 1024 * 1024),
        name="forward_one",
    )(place, segments, x, x_halo, cot, cot_halo, *weights)


def backward_two(place, table, x, x_halo, gain1, shift1, w_in, kept, pieces):
    rows, width = x.shape
    total = rows + TILE
    packed = packed_rows(3 * width, 3 * width, pieces)
    shapes = (
        jax.ShapeDtypeStruct((rows, width), F32),
        jax.ShapeDtypeStruct((TILE, width), F32),
        jax.ShapeDtypeStruct((packed, LANES), BF16),
        jax.ShapeDtypeStruct((packed, LANES), BF16),
    )
    return pl.pallas_call(
        kernel_two,
        out_shape=shapes,
        in_specs=[SMEM] * 2 + [VMEM] * 10,
        out_specs=tuple([VMEM] * 4),
        scratch_shapes=[
            pltpu.VMEM((total, 3 * width), BF16),
            pltpu.VMEM((width, 3 * width), F32),
            pltpu.VMEM((16, 3 * width), F32),
        ],
        compiler_params=pltpu.CompilerParams(vmem_limit_bytes=60 * 1024 * 1024),
        name="backward_two",
    )(place, table, x, x_halo, gain1, shift1, w_in, *kept)


def same_core_groups():
    packs, parts = lax.axis_size("dp"), lax.axis_size("mp")
    return [[d * parts + m for d in range(c, packs, 2) for m in range(parts)] for c in range(2)]


def swap_cores(block):
    packs = lax.axis_size("dp")
    return lax.ppermute(block, "dp", [(i, i ^ 1) for i in range(packs)])


def scatter_sum(mine, other, pieces):
    both = (mine.astype(F32) + swap_cores(other).astype(F32)).astype(BF16)
    parts = lax.all_to_all(both.reshape(pieces, -1, LANES), ("dp", "mp"), 0, 0, axis_index_groups=same_core_groups())
    return jnp.sum(parts.astype(F32), axis=0).astype(BF16)


def gather_sum(piece, core, pieces):
    sent = jnp.broadcast_to(piece[None], (pieces,) + piece.shape)
    mine = lax.all_to_all(sent, ("dp", "mp"), 0, 0, axis_index_groups=same_core_groups()).reshape(-1, LANES)
    other = swap_cores(mine)
    return jnp.where(core == 0, mine, other), jnp.where(core == 0, other, mine)


def unpack(halves, at, columns):
    low, high = halves
    count = columns // LANES
    blocks = [h[at : at + count * 192].reshape(count, 192, LANES).transpose(1, 0, 2) for h in (low, high)]
    return jnp.concatenate(blocks, axis=0).reshape(384, columns).astype(F32)


def unpack_small(halves, at, columns):
    count = columns // LANES
    rows = [halves[i % 2][at + (i // 2) * 16 : at + (i // 2) * 16 + 16] for i in range(count)]
    return jnp.concatenate(rows, axis=1).astype(F32)


def passed(block, distance):
    count = lax.axis_size("mp")
    route = [(i, i + distance) for i in range(count) if 0 <= i + distance < count]
    return lax.ppermute(block, "mp", route)


def take_over(own, other, first):
    row = lax.broadcasted_iota(jnp.int32, (HALO, 1), 0)
    return lax.dynamic_update_slice(own, jnp.where(row < first, other, own[:HALO]), (0, 0))


def body(
    layer_input, segments, cotangent, first_gain, first_shift, inward_weight, inward_bias, outward_weight,
    outward_bias, second_gain, second_shift, expand_weight, expand_bias, shrink_weight, shrink_bias,
):
    rows, width = layer_input.shape
    position = lax.axis_index("mp")
    core = lax.axis_index("dp") % 2
    pieces = lax.axis_size("dp") * lax.axis_size("mp") // 2
    place = jnp.stack([position, (position == lax.axis_size("mp") - 1).astype(jnp.int32), core]).astype(jnp.int32)
    pad = ((0, TILE - HALO), (0, 0))
    x_halo = jnp.pad(passed(layer_input[:HALO], -1), pad)
    cot_halo = jnp.pad(passed(cotangent[:HALO], -1), pad)
    weights = (
        first_gain[None], first_shift[None], inward_weight, inward_bias, outward_weight, outward_bias[None],
        second_gain[None], second_shift[None], expand_weight, expand_bias[None], shrink_weight, shrink_bias[None],
    )
    outs = forward_one(place, segments, layer_input, x_halo, cotangent, cot_halo, weights, pieces)
    result, result_halo, triple, attended, upstream, middle_grad, stats, table, mine, other = outs
    feed_piece = scatter_sum(mine, other, pieces)
    input_grad, input_halo, mine, other = backward_two(
        place, table, layer_input, x_halo, first_gain[None], first_shift[None], inward_weight,
        (triple, attended, upstream, middle_grad, stats), pieces,
    )
    first = table[GROUPS, 1]
    result = take_over(result, passed(result_halo[:HALO], 1), first)
    input_grad = take_over(input_grad, passed(input_halo[:HALO], 1), first)
    inward_piece = scatter_sum(mine, other, pieces)
    feed_sums = gather_sum(feed_piece, core, pieces)
    inward_sums = gather_sum(inward_piece, core, pieces)
    hidden = expand_weight.shape[1]
    d_ex = unpack(feed_sums, 0, hidden)
    d_sh = unpack(feed_sums, 192 * hidden // LANES, hidden).T
    d_out = unpack(feed_sums, 192 * 2 * hidden // LANES, width)
    d_in = unpack(inward_sums, 0, 3 * width)
    small = unpack_small(feed_sums, 192 * (2 * hidden + width) // LANES, hidden)
    small2 = unpack_small(inward_sums, 192 * 3 * width // LANES, 3 * width)
    return (
        result, input_grad, small2[5, :width], small2[6, :width], d_in,
        jnp.stack([small2[4, :width], small2[4, 2 * width : 3 * width]]),
        d_out, small[3, :width], small[1, :width], small[2, :width], d_ex, small[8], d_sh, small[0, :width],
    )


def solution(mesh):
    rows = P(("dp", "mp"), None)
    in_specs = (rows, P("dp", None), rows) + (P(),) * 12
    out_specs = (rows, rows) + (P(),) * 12
    return jax.shard_map(body, mesh=mesh, in_specs=in_specs, out_specs=out_specs, check_vma=False)
```

time: 619 us -> 276 us (0.45)
  local copies, waits for them, and re-layouts: 204 us -> 31.2 us
  matrix products: 172 us -> 0 us
  Pallas kernels: 0 us -> 126 us
  other arithmetic: 67.8 us -> 14.2 us
  blocking collectives: 68.6 us -> 29.3 us
  waiting for transfers between devices: 67.6 us -> 30.6 us
  starting transfers between devices: 11 us -> 41.1 us
  between operations: 14.8 us -> 0.97 us
    dot_general x40 -> x0, matrix products: 172 us -> none  [the longest x1 33.8 us: body(): jnp.dot(normed2_low, expand_weight, preferred_element_type=jnp.float32)]
    pallas_call x0 -> x2, Pallas kernels: none -> 126 us  [the longest x1 87.7 us: forward_one(): pl.pallas_call(kernel_one, out_shape=shapes, in_specs=[SMEM, SMEM] + [VME...]
    dynamic_update_slice x20 -> x0, local copies, waits for them, and re-layouts: 73.2 us -> none  [the longest x4 58.3 us: backward_tile(): lax.dynamic_update_slice_in_dim(pair_grads, current + addition, begin, 0)]
    psum x1 -> x0, blocking collectives: 68.6 us -> none  [body(): lax.psum((grads[0], grads[1], grads[2], grads[3], grads[4], grads[5], gra...]
    psum x1 -> x0, waiting for transfers between devices: 59.8 us -> none  [body(): lax.psum((grads[0], grads[1], grads[2], grads[3], grads[4], grads[5], gra...]
    all_to_all x0 -> x1, blocking collectives: none -> 29.3 us  [scatter_sum(): lax.all_to_all(both.reshape(pieces, -1, LANES), ('dp', 'mp'), 0, 0, axis_...]
    dynamic_slice x33 -> x0, local copies, waits for them, and re-layouts: 28.3 us -> none  [the longest x8 8.17 us: tile_scores(): lax.dynamic_slice_in_dim(queries, begin, tile, 0).reshape(tile, heads, HD)]
    all_to_all x0 -> x3, waiting for transfers between devices: none -> 25.2 us  [the longest x2 23 us: gather_sum(): lax.all_to_all(sent, ('dp', 'mp'), 0, 0, axis_index_groups=same_core_grou...]
  transfers between devices with their start and end apart: 5 -> 11, of which waited for: 3 -> 5; matrix products, arithmetic and copies ran while one was open for 8% -> 10% of each run, Pallas kernels for 0% -> 0%
where the time goes in v1:
time: 276 us; the launch traced here: 274 us
  Pallas kernels  126 us (46%)
  starting transfers between devices  41.1 us (15%)
  local copies, waits for them, and re-layouts  31.2 us (11%)
  waiting for transfers between devices  30.6 us (11%)
  blocking collectives  29.3 us (11%)
  other arithmetic  14.2 us (5%)
    pallas_call x1, Pallas kernels, forward_one(): pl.pallas_call(kernel_one, out_shape=shapes, in_specs=[SMEM, SMEM] + [VME...  87.7 us
    pallas_call x1, Pallas kernels, backward_two(): pl.pallas_call(kernel_two, out_shape=shapes, in_specs=[SMEM] * 2 + [VMEM]...  38.5 us
    all_to_all x1, blocking collectives, scatter_sum(): lax.all_to_all(both.reshape(pieces, -1, LANES), ('dp', 'mp'), 0, 0, axis_...  29.3 us
    all_to_all x2, waiting for transfers between devices, gather_sum(): lax.all_to_all(sent, ('dp', 'mp'), 0, 0, axis_index_groups=same_core_grou...  23 us
    all_to_all x2, starting transfers between devices, gather_sum(): lax.all_to_all(sent, ('dp', 'mp'), 0, 0, axis_index_groups=same_core_grou...  14.3 us
    ppermute x4, starting transfers between devices, swap_cores(): return lax.ppermute(block, 'dp', [(i, i ^ 1) for i in range(packs)])  13.3 us
    ppermute x4, starting transfers between devices, passed(): return lax.ppermute(block, 'mp', route)  8.61 us
    unnamed x32, local copies, waits for them, and re-layouts  6.16 us
  transfers between devices with their start and end apart: 11, of which 5 were waited for; matrix products, arithmetic and copies ran while one was open for 10% of the time, Pallas kernels for 0%

profile of v1, /device:TPU:1, one launch (start us, length us, event | category | flops | bytes accessed | tf_op | source)
XLA Modules:
  0.0 273.7 jit_solution(3721324308752409)
XLA Ops:
  15.9 87.7 %forward_one.1 = (bf16[2048,384]{1,0:T(8,128)(2,1)}, bf16[256,384]{1,0:T(8,128)(2,1)}, bf16[2304,1152]{1,0:T(8,128)(2,1)}, bf16[2304,384]{1,0:T(8,128)(2,1)}, bf...) custom-call(s32[3]{0:T(128)} %pad_add_fusion.place, ...), custom_call_target="tpu_custom_call" | custom-call | tf_op jit(solution)/shard_map/forward_one/pallas_call | solution.py:403
  103.6 38.5 %backward_two.1 = (f32[2048,384]{1,0:T(8,128)}, f32[256,384]{1,0:T(8,128)}, bf16[2048,128]{1,0:T(8,128)(2,1)}, bf16[2048,128]{1,0:T(8,128)(2,1)}) custom-call(s32[3]{0:T(128)} %pad_add_fusion.place, s32[25,8]{1,0:T(8,128)} %get-tuple-element.29.table, bf16[2048,384]{1,0:T(8,128)(2,1)} %x_ref.3, bf16[256,384]{1,0:T(8,128)(2,1)} %pad.7.x_halo, ...), custom_call_target="tpu_custom_call" | custom-call | tf_op jit(solution)/shard_map/backward_two/pallas_call | solution.py:429
  142.2 1.9 collective-permute-start.4
  144.2 1.7 collective-permute-done.4
  147.1 29.3 %all_to_all.20 = bf16[64,32,128]{2,1,0:T(8,128)(2,1)S(1)} all-to-all(bf16[64,32,128]{2,1,0:T(8,128)(2,1)S(1)} %bitcast.51), channel_id=1, replica_groups={{0,1,2,3,8,9,10,11,16,17,18,19,24,25,26,27,32,33,34,35,40,41,42,43,48,4..., dimensions={0} | all-to-all | bytes 1048576 | tf_op jit(solution)/shard_map/all_to_all | solution.py:456
  177.3 4.6 %all-to-all-start.1 = ((bf16[64,32,128]{2,1,0:T(8,128)(2,1)}), bf16[64,32,128]{2,1,0:T(8,128)(2,1)S(1)}, u32[]{:S(2)}, u32[]{:S(2)}) async-start(bf16[64,32,128]{2,1,0:T(8,128)(2,1)} %broadcast_in_dim.57), calls=%async_computation.1 | async-start | bytes 1048576 | tf_op jit(solution)/shard_map/all_to_all | solution.py:462
  182.0 2.8 %add_convert_fusion = bf16[5632,128]{1,0:T(8,128)(2,1)} fusion(bf16[5632,128]{1,0:T(8,128)(2,1)} %collective-permute-done.6, bf16[5632,128]{1,0:T(8,128)(2,1)S(1)} %copy-done), kind=kLoop, calls=%fused_computation | loop fusion | flops 2883584 | bytes 4325376 | tf_op jit(solution)/shard_map/convert_element_type | solution.py:455
  184.8 8.3 %all-to-all-done.1 = bf16[64,32,128]{2,1,0:T(8,128)(2,1)S(1)} async-done(((bf16[64,32,128]{2,1,0:T(8,128)(2,1)}), bf16[64,32,128]{2,1,0:T(8,128)(2,1)S(1)}, u32[]{:S(2)}, u32[]{:S(2)}) %all-to-all-start.1) | async-done | bytes 524320 | tf_op jit(solution)/shard_map/all_to_all | solution.py:462
  193.2 4.9 %all-to-all-start.2 = ((bf16[64,88,128]{2,1,0:T(8,128)(2,1)}), bf16[64,88,128]{2,1,0:T(8,128)(2,1)S(1)}, u32[]{:S(2)}, u32[]{:S(2)}) async-start(bf16[64,88,128]{2,1,0:T(8,128)(2,1)} %bitcast.11), calls=%async_computation.2 | async-start | bytes 2883584 | tf_op jit(solution)/shard_map/all_to_all | solution.py:456
  198.2 2.9 %collective-permute-start.2 = (bf16[208,384]{1,0:T(8,128)(2,1)S(1)}, bf16[208,384]{1,0:T(8,128)(2,1)S(1)}, u32[]{:S(2)}, u32[]{:S(2)}) collective-permute-start(bf16[208,384]{1,0:T(8,128)(2,1)S(1)} %slice.138), channel_id=1, source_target_pairs={{0,1},{1,2},{2,3},{4,5},{5,6},{6,7},{8,9},{9,10},{10,11},{12,13},{... | collective-permute-start | bytes 479240 | tf_op jit(solution)/shard_map/ppermute | solution.py:483
  202.4 3.1 %collective-permute-start.3 = (f32[208,384]{1,0:T(8,128)S(1)}, f32[208,384]{1,0:T(8,128)S(1)}, u32[]{:S(2)}, u32[]{:S(2)}) collective-permute-start(f32[208,384]{1,0:T(8,128)S(1)} %slice.140), channel_id=1, source_target_pairs={{0,1},{1,2},{2,3},{4,5},{5,6},{6,7},{8,9},{9,10},{10,11},{12,13},{... | collective-permute-start | bytes 958472 | tf_op jit(solution)/shard_map/ppermute | solution.py:483
  205.5 4.0 %collective-permute-start.5 = (bf16[2048,128]{1,0:T(8,128)(2,1)S(1)}, bf16[2048,128]{1,0:T(8,128)(2,1)S(1)}, u32[]{:S(2)}, u32[]{:S(2)}) collective-permute-start(bf16[2048,128]{1,0:T(8,128)(2,1)S(1)} %bitcast.50), channel_id=1, source_target_pairs={{0,4},{4,0},{8,12},{12,8},{16,20},{20,16},{24,28},{28,24},{32,36},... | collective-permute-start | bytes 1572872 | tf_op jit(solution)/shard_map/ppermute | solution.py:451
  210.1 3.8 %collective-permute-done.2 = bf16[208,384]{1,0:T(8,128)(2,1)S(1)} collective-permute-done((bf16[208,384]{1,0:T(8,128)(2,1)S(1)}, bf16[208,384]{1,0:T(8,128)(2,1)S(1)}, u32[]{:S(2)}, u32[]{:S(2)}) %collective-permute-start.2) | collective-permute-done | bytes 159776 | tf_op jit(solution)/shard_map/ppermute | solution.py:483
  213.9 1.7 select_dynamic-update-slice_fusion.1
  215.6 2.2 all-to-all-done.2
  219.3 9.7 %all-to-all-start.3 = ((bf16[64,88,128]{2,1,0:T(8,128)(2,1)}), bf16[64,88,128]{2,1,0:T(8,128)(2,1)}, u32[]{:S(2)}, u32[]{:S(2)}) async-start(bf16[64,88,128]{2,1,0:T(8,128)(2,1)} %broadcast_in_dim.58), calls=%async_computation.3 | async-start | bytes 2883584 | tf_op jit(solution)/shard_map/all_to_all | solution.py:462
  229.0 1.8 select_dynamic-update-slice_fusion
  230.9 14.7 %all-to-all-done.3 = bf16[64,88,128]{2,1,0:T(8,128)(2,1)} async-done(((bf16[64,88,128]{2,1,0:T(8,128)(2,1)}), bf16[64,88,128]{2,1,0:T(8,128)(2,1)}, u32[]{:S(2)}, u32[]{:S(2)}) %all-to-all-start.3) | async-done | bytes 1441824 | tf_op jit(solution)/shard_map/all_to_all | solution.py:462
  245.6 7.3 %collective-permute-start.7 = (bf16[5632,128]{1,0:T(8,128)(2,1)}, bf16[5632,128]{1,0:T(8,128)(2,1)}, u32[]{:S(2)}, u32[]{:S(2)}) collective-permute-start(bf16[5632,128]{1,0:T(8,128)(2,1)} %bitcast.12), channel_id=1, source_target_pairs={{0,4},{4,0},{8,12},{12,8},{16,20},{20,16},{24,28},{28,24},{32,36},... | collective-permute-start | bytes 4325384 | tf_op jit(solution)/shard_map/ppermute | solution.py:451
  255.2 1.9 copy.39
  258.4 2.0 broadcast_select_fusion.1
  266.5 2.0 copy.37
  268.5 3.0 %copy.41 = f32[384,1536]{1,0:T(8,128)} copy(f32[384,1536]{0,1:T(8,128)} %bitcast.42) | data formatting | bytes 4718592
  271.7 2.0 copy.38
  (80 shorter events, 30.9 us)
Async XLA Ops:
  1.6 12.9 %collective-permute-start = (bf16[208,384]{1,0:T(8,128)(2,1)S(1)}, bf16[208,384]{1,0:T(8,128)(2,1)S(1)}, u32[]{:S(2)}, u32[]{:S(2)}) collective-permute-start(bf16[208,384]{1,0:T(8,128)(2,1)S(1)} %slice.135), channel_id=1, source_target_pairs={{1,0},{2,1},{3,2},{5,4},{6,5},{7,6},{9,8},{10,9},{11,10},{13,12},{... | collective-permute-start | bytes 479240 | tf_op jit(solution)/shard_map/ppermute | solution.py:483
  3.8 11.4 %collective-permute-start.1 = (bf16[208,384]{1,0:T(8,128)(2,1)S(1)}, bf16[208,384]{1,0:T(8,128)(2,1)S(1)}, u32[]{:S(2)}, u32[]{:S(2)}) collective-permute-start(bf16[208,384]{1,0:T(8,128)(2,1)S(1)} %slice.136), channel_id=1, source_target_pairs={{1,0},{2,1},{3,2},{5,4},{6,5},{7,6},{9,8},{10,9},{11,10},{13,12},{... | collective-permute-start | bytes 479240 | tf_op jit(solution)/shard_map/ppermute | solution.py:483
  103.6 40.5 %copy-start.4 = (bf16[5632,128]{1,0:T(8,128)(2,1)S(1)}, bf16[5632,128]{1,0:T(8,128)(2,1)}, u32[]{:S(2)}) copy-start(bf16[5632,128]{1,0:T(8,128)(2,1)} %get-tuple-element.41) | copy-start | bytes 4325380
  142.2 3.7 %collective-permute-start.4 = (bf16[2048,128]{1,0:T(8,128)(2,1)}, bf16[2048,128]{1,0:T(8,128)(2,1)S(1)}, u32[]{:S(2)}, u32[]{:S(2)}) collective-permute-start(bf16[2048,128]{1,0:T(8,128)(2,1)} %get-tuple-element.39), channel_id=1, source_target_pairs={{0,4},{4,0},{8,12},{12,8},{16,20},{20,16},{24,28},{28,24},{32,36},... | collective-permute-start | bytes 1572872 | tf_op jit(solution)/shard_map/ppermute | solution.py:451
  144.1 37.9 %collective-permute-start.6 = (bf16[5632,128]{1,0:T(8,128)(2,1)S(1)}, bf16[5632,128]{1,0:T(8,128)(2,1)}, u32[]{:S(2)}, u32[]{:S(2)}) collective-permute-start(bf16[5632,128]{1,0:T(8,128)(2,1)S(1)} %copy-done.4), channel_id=1, source_target_pairs={{0,4},{4,0},{8,12},{12,8},{16,20},{20,16},{24,28},{28,24},{32,36},... | collective-permute-start | bytes 4325384 | tf_op jit(solution)/shard_map/ppermute | solution.py:451
  147.0 34.9 %copy-start = (bf16[5632,128]{1,0:T(8,128)(2,1)S(1)}, bf16[5632,128]{1,0:T(8,128)(2,1)}, u32[]{:S(2)}) copy-start(bf16[5632,128]{1,0:T(8,128)(2,1)} %get-tuple-element.40) | copy-start | bytes 4325380
  177.3 15.8 %all-to-all-start.1 = ((bf16[64,32,128]{2,1,0:T(8,128)(2,1)}), bf16[64,32,128]{2,1,0:T(8,128)(2,1)S(1)}, u32[]{:S(2)}, u32[]{:S(2)}) async-start(bf16[64,32,128]{2,1,0:T(8,128)(2,1)} %broadcast_in_dim.57), calls=%async_computation.1 | async-start | bytes 1048576 | tf_op jit(solution)/shard_map/all_to_all | solution.py:462
  184.8 13.3 %copy-start.2 = (bf16[256,384]{1,0:T(8,128)(2,1)S(1)}, bf16[256,384]{1,0:T(8,128)(2,1)}, u32[]{:S(2)}) copy-start(bf16[256,384]{1,0:T(8,128)(2,1)} %get-tuple-element.30) | copy-start | bytes 589828
  193.2 9.2 %copy-start.1 = (f32[256,384]{1,0:T(8,128)S(1)}, f32[256,384]{1,0:T(8,128)}, u32[]{:S(2)}) copy-start(f32[256,384]{1,0:T(8,128)} %get-tuple-element.37) | copy-start | bytes 1179652
  193.2 24.6 %all-to-all-start.2 = ((bf16[64,88,128]{2,1,0:T(8,128)(2,1)}), bf16[64,88,128]{2,1,0:T(8,128)(2,1)S(1)}, u32[]{:S(2)}, u32[]{:S(2)}) async-start(bf16[64,88,128]{2,1,0:T(8,128)(2,1)} %bitcast.11), calls=%async_computation.2 | async-start | bytes 2883584 | tf_op jit(solution)/shard_map/all_to_all | solution.py:456
  198.2 15.7 %collective-permute-start.2 = (bf16[208,384]{1,0:T(8,128)(2,1)S(1)}, bf16[208,384]{1,0:T(8,128)(2,1)S(1)}, u32[]{:S(2)}, u32[]{:S(2)}) collective-permute-start(bf16[208,384]{1,0:T(8,128)(2,1)S(1)} %slice.138), channel_id=1, source_target_pairs={{0,1},{1,2},{2,3},{4,5},{5,6},{6,7},{8,9},{9,10},{10,11},{12,13},{... | collective-permute-start | bytes 479240 | tf_op jit(solution)/shard_map/ppermute | solution.py:483
  202.4 26.6 %collective-permute-start.3 = (f32[208,384]{1,0:T(8,128)S(1)}, f32[208,384]{1,0:T(8,128)S(1)}, u32[]{:S(2)}, u32[]{:S(2)}) collective-permute-start(f32[208,384]{1,0:T(8,128)S(1)} %slice.140), channel_id=1, source_target_pairs={{0,1},{1,2},{2,3},{4,5},{5,6},{6,7},{8,9},{9,10},{10,11},{12,13},{... | collective-permute-start | bytes 958472 | tf_op jit(solution)/shard_map/ppermute | solution.py:483
  205.5 25.3 %collective-permute-start.5 = (bf16[2048,128]{1,0:T(8,128)(2,1)S(1)}, bf16[2048,128]{1,0:T(8,128)(2,1)S(1)}, u32[]{:S(2)}, u32[]{:S(2)}) collective-permute-start(bf16[2048,128]{1,0:T(8,128)(2,1)S(1)} %bitcast.50), channel_id=1, source_target_pairs={{0,4},{4,0},{8,12},{12,8},{16,20},{20,16},{24,28},{28,24},{32,36},... | collective-permute-start | bytes 1572872 | tf_op jit(solution)/shard_map/ppermute | solution.py:451
  219.3 26.3 %all-to-all-start.3 = ((bf16[64,88,128]{2,1,0:T(8,128)(2,1)}), bf16[64,88,128]{2,1,0:T(8,128)(2,1)}, u32[]{:S(2)}, u32[]{:S(2)}) async-start(bf16[64,88,128]{2,1,0:T(8,128)(2,1)} %broadcast_in_dim.58), calls=%async_computation.3 | async-start | bytes 2883584 | tf_op jit(solution)/shard_map/all_to_all | solution.py:462
  245.6 12.8 %collective-permute-start.7 = (bf16[5632,128]{1,0:T(8,128)(2,1)}, bf16[5632,128]{1,0:T(8,128)(2,1)}, u32[]{:S(2)}, u32[]{:S(2)}) collective-permute-start(bf16[5632,128]{1,0:T(8,128)(2,1)} %bitcast.12), channel_id=1, source_target_pairs={{0,4},{4,0},{8,12},{12,8},{16,20},{20,16},{24,28},{28,24},{32,36},... | collective-permute-start | bytes 4325384 | tf_op jit(solution)/shard_map/ppermute | solution.py:451
  253.0 0.7 copy-start.3

commit v2 on v1

v2 whole, which is shorter than its diff:
```python
from functools import partial

import jax
import jax.numpy as jnp
from jax import lax
from jax.experimental import pallas as pl
from jax.experimental.pallas import tpu as pltpu
from jax.sharding import PartitionSpec as P

HD = 64
SEQ = 198
EPSILON = 1e-06
MASKED = -1000000000.0
WIN = 256
TILE = 256
HALO = 208
WIDE = 768
OWN = 512
GROUPS = 24
LANES = 128
CHUNK = 256
FEED = 768
BIG = 1 << 20
F32 = jnp.float32
BF16 = jnp.bfloat16
NT = (((1,), (1,)), ((), ()))
TN = (((0,), (0,)), ((), ()))


def row_of(ref):
    return ref[...].reshape(1, -1)


def dot(a, b):
    return jnp.dot(a, b, preferred_element_type=F32)


def dot_nt(a, b):
    return lax.dot_general(a, b, NT, preferred_element_type=F32)


def dot_tn(a, b):
    return lax.dot_general(a, b, TN, preferred_element_type=F32)


def normalize(rows):
    center = jnp.mean(rows, axis=-1, keepdims=True)
    centred = rows - center
    spread = jnp.mean(centred * centred, axis=-1, keepdims=True)
    inverse = lax.rsqrt(spread + EPSILON)
    return centred * inverse, inverse


def normalize_back(upstream, scaled, inverse, gain):
    direct = upstream * gain
    first = jnp.mean(direct, axis=-1, keepdims=True)
    second = jnp.mean(direct * scaled, axis=-1, keepdims=True)
    return inverse * (direct - first - scaled * second)


def gelu_parts(v, half_upstream):
    scaled = v * 0.7071067811865476
    double = 1.0 + lax.erf(scaled)
    bell = jnp.exp2((scaled * scaled) * -1.4426950408889634)
    return (0.5 * v) * double, half_upstream * (double + (v * 0.7978845608028654) * bell)


def image_ends(seg, base, work):
    ident = lax.broadcasted_iota(jnp.int32, (LANES, LANES), 0)
    below = jnp.zeros((LANES, LANES), F32)
    for begin in range(0, seg.shape[1], LANES):
        row = seg[0:1, begin : begin + LANES]
        row = jnp.where(row < 0, BIG, row)
        below = below + jnp.where(row <= ident, 1.0, 0.0)
    ends = jnp.broadcast_to(jnp.sum(below, axis=1, keepdims=True), (LANES, LANES))
    started = jnp.sum(jnp.where(ends < base.astype(F32), 1.0, 0.0), axis=0, keepdims=True)
    work[0:1, :] = ends.T[0:1].astype(jnp.int32)
    work[1:2, :] = started.astype(jnp.int32)


def plan_groups(ends, position, rows, table):
    base = position * rows
    limit = jnp.minimum(base + rows, ends[0, LANES - 1]) - base
    image = jnp.where(position == 0, 0, ends[1, 0] + 1)
    first = jnp.where(position == 0, 0, ends[0, jnp.maximum(image - 1, 0)]) - base

    def body(state):
        at, image, group, window, start, c1, c2 = state
        after = ends[0, jnp.minimum(image, LANES - 1)] - base
        fits = after - window <= WIN

        @pl.when(jnp.logical_not(fits))
        def _():
            write_group(table, group, window, start, c1, c2, at)

        group = jnp.where(fits, group, group + 1)
        new_c1 = jnp.where(fits, jnp.where(at == start, c1, jnp.where(c1 < 0, at, c1)), -1)
        new_c2 = jnp.where(fits, jnp.where(jnp.logical_and(at != start, c1 >= 0), jnp.where(c2 < 0, at, c2), c2), -1)
        start = jnp.where(fits, start, at)
        window = jnp.where(fits, window, (at // 16) * 16)
        return after, image + 1, group, window, start, new_c1, new_c2

    init = (first, image, jnp.int32(0), (first // 16) * 16, first, jnp.int32(-1), jnp.int32(-1))
    at, image, group, window, start, c1, c2 = lax.while_loop(lambda s: s[0] < limit, body, init)
    write_group(table, group, window, start, c1, c2, at)
    table[GROUPS, 0] = group + 1
    table[GROUPS, 1] = first
    table[GROUPS, 2] = at


def write_group(table, group, window, start, c1, c2, end):
    table[group, 0] = window
    table[group, 1] = start - window
    table[group, 2] = jnp.where(c1 < 0, end, c1) - window
    table[group, 3] = jnp.where(c2 < 0, end, c2) - window
    table[group, 4] = end - window


def group_bias(table, group):
    bounds = [table[group, i] for i in range(1, 5)]
    row = lax.broadcasted_iota(jnp.int32, (WIN, LANES), 0)
    col = lax.broadcasted_iota(jnp.int32, (1, WIN), 1)

    def ident(index):
        return sum((index >= b).astype(jnp.int32) for b in bounds)

    row, col = ident(row), ident(col)
    return jnp.concatenate(
        [jnp.where(row == col[:, at : at + LANES], 0.0, MASKED) for at in range(0, WIN, LANES)], axis=1
    )


def head_masks():
    lane = lax.broadcasted_iota(jnp.int32, (WIN, 2 * HD), 1)
    return lane < HD, lane >= HD


def keep_first(ref, window, begin, cols, value):
    head = pl.ds(window, 16)
    old = ref[head, cols]
    row = lax.broadcasted_iota(jnp.int32, (16, 2 * HD), 0)
    ref[head, cols] = jnp.where(row >= begin, value[:16].astype(F32), old.astype(F32)).astype(BF16)
    ref[pl.ds(window + 16, WIN - 16), cols] = value[16:].astype(BF16)


def block_diagonal(pair_t):
    zero = jnp.zeros((HD, pair_t.shape[1]), pair_t.dtype)
    return jnp.concatenate(
        [jnp.concatenate([pair_t[:HD], zero], axis=1), jnp.concatenate([zero, pair_t[HD:]], axis=1)], axis=0
    )


def pipelined(groups, first, second, third, arrive=lambda group, have: have):
    def clamped(group):
        return jnp.minimum(group, groups - 1)

    def half(group, slot):
        first(clamped(group), slot)
        second(clamped(group - 1), 1 - slot)
        third(clamped(group - 2), slot)

    have = arrive(clamped(1), jnp.int32(0))
    first(0, 0)
    first(clamped(1), 1)
    second(0, 0)

    def both(step, have):
        have = arrive(clamped(2 * step + 3), have)
        half(2 * step + 2, 0)
        half(2 * step + 3, 1)
        return have

    have = lax.fori_loop(0, (groups + 1) // 2, both, have)
    arrive(None, have)


def group_rows(table, group, shifted=0):
    return pl.ds(pl.multiple_of(table[group, 0] - shifted, 16), WIN)


def attend_groups(groups, table, triple, attended, stats, scores, peaks, raised, scales, alone=None, shifted=0):
    width = attended.shape[1]
    pairs = range(width // (2 * HD))

    def first(group, slot):
        rows = group_rows(table, group, shifted)
        bias = group_bias(table, group)
        bias = jnp.concatenate([bias, bias], axis=1)
        for pair in pairs:
            query_t = triple[rows, pl.ds(pair * 2 * HD, 2 * HD)].T
            key = triple[rows, pl.ds(width + pair * 2 * HD, 2 * HD)]
            value = dot(key, block_diagonal(query_t)) + bias
            scores[slot][pair] = value
            peaks[slot][pair : pair + 1, :] = jnp.max(value, axis=0, keepdims=True)

    def second(group, slot):
        for pair in pairs:
            peak = peaks[slot][pair : pair + 1, :]
            value = jnp.exp(scores[slot][pair] - peak)
            total = jnp.sum(value, axis=0, keepdims=True)
            raised[slot][pair, :WIN] = value[:, :WIN].astype(BF16)
            raised[slot][pair, WIN:] = value[:, WIN:].astype(BF16)
            scales[slot][pair : pair + 1, :] = 1.0 / total
            lse = peak + jnp.log(total)
            stats[group, pl.ds(2 * pair, 1), :] = lse[:, :WIN]
            stats[group, pl.ds(2 * pair + 1, 1), :] = lse[:, WIN:]

    def third(group, slot):
        rows = group_rows(table, group, shifted)
        for pair in pairs:
            value_t = block_diagonal(triple[rows, pl.ds(2 * width + pair * 2 * HD, 2 * HD)].T)
            out = dot(value_t, raised[slot][pair])
            scale = scales[slot][pair : pair + 1, :]
            out = jnp.concatenate([out[:HD] * scale[:, :WIN], out[HD:] * scale[:, WIN:]], axis=0)
            keep_first(attended, group_rows(table, group).start, table[group, 1], pl.ds(pair * 2 * HD, 2 * HD), out.T)

    if alone is None:
        pipelined(groups, first, second, third)
    else:
        for part in (first, second, third):
            part(alone, 0)


def attend_back_groups(
    groups, table, triple, attended, upstream, stats, triple_grad, scores, agreements, probs_grads, probs, scores_grads,
):
    width = attended.shape[1]
    pairs = range(width // (2 * HD))
    masks = head_masks()

    def columns(pair, block):
        return pl.ds(block * width + pair * 2 * HD, 2 * HD)

    def first(group, slot):
        rows = group_rows(table, group)
        bias = group_bias(table, group)
        bias = jnp.concatenate([bias, bias], axis=1)
        for pair in pairs:
            lse = jnp.concatenate(
                [stats[group, pl.ds(2 * pair, 1), :], stats[group, pl.ds(2 * pair + 1, 1), :]], axis=1
            )
            query_t = triple[rows, columns(pair, 0)].T
            scores[slot][pair] = dot(triple[rows, columns(pair, 1)], block_diagonal(query_t)) + bias - lse
            up_t = upstream[rows, columns(pair, 0)].T
            probs_grads[slot][pair] = dot(triple[rows, columns(pair, 2)], block_diagonal(up_t))
            product = attended[rows, columns(pair, 0)].T.astype(F32) * up_t.astype(F32)
            agreements[slot][pair : pair + 1, :] = jnp.concatenate(
                [jnp.sum(product[:HD], axis=0, keepdims=True), jnp.sum(product[HD:], axis=0, keepdims=True)], axis=1
            )

    def second(group, slot):
        for pair in pairs:
            prob = jnp.exp(scores[slot][pair])
            probs[slot][pair] = prob.astype(BF16)
            agreement = agreements[slot][pair : pair + 1, :]
            scores_grads[slot][pair] = (prob * (probs_grads[slot][pair] - agreement)).astype(BF16)

    def stacked(pair_rows):
        zero = jnp.zeros_like(pair_rows)
        return jnp.concatenate([jnp.where(mask, pair_rows, zero) for mask in masks], axis=0)

    def third(group, slot):
        rows = group_rows(table, group)
        window, begin = rows.start, table[group, 1]
        for pair in pairs:
            scores_grad = scores_grads[slot][pair]
            value_grad = dot(probs[slot][pair], stacked(upstream[rows, columns(pair, 0)]))
            key_grad = dot(scores_grad, stacked(triple[rows, columns(pair, 0)]))
            key_t = block_diagonal(triple[rows, columns(pair, 1)].T)
            query_grad = dot(key_t, jnp.concatenate([scores_grad[:, :WIN], scores_grad[:, WIN:]], axis=0))
            keep_first(triple_grad, window, begin, columns(pair, 0), (query_grad * HD ** (-0.5)).T)
            keep_first(triple_grad, window, begin, columns(pair, 1), key_grad)
            keep_first(triple_grad, window, begin, columns(pair, 2), value_grad)

    pipelined(groups, first, second, third)


def interval(tile, first, end, size=TILE):
    row = lax.broadcasted_iota(jnp.int32, (size, 1), 0) + tile * size
    return jnp.logical_and(row >= first, row < end)


class Mover:
    def __init__(self, sems):
        self.sems = sems
        self.count = 0

    def start(self, source, target):
        copy = pltpu.make_async_copy(source, target, self.sems.at[self.count])
        self.count += 1
        copy.start()
        return copy


def project_rows(rows, gain1, shift1, w_in, b_in, target, spot):
    width = rows.shape[1]
    scaled, _inverse = normalize(rows)
    normed = (scaled * row_of(gain1) + row_of(shift1)).astype(BF16)
    q = dot(normed, w_in[:, :width]) + b_in[0:1, :]
    target[spot, :width] = (q.astype(BF16).astype(F32) * HD ** (-0.5)).astype(BF16)
    target[spot, width : 2 * width] = dot(normed, w_in[:, width : 2 * width]).astype(BF16)
    target[spot, 2 * width :] = (dot(normed, w_in[:, 2 * width :]) + b_in[1:2, :]).astype(BF16)


def kernel_own(
    place, seg, gain1, shift1, b_in, x_in, w_in_in,
    triple_out, attended_out, stats, table,
    x, w_in, triple, attended, work, ends, scores, peaks, raised, scales, sems, tile_sems,
):
    rows, width = x_in.shape
    move = Mover(sems)
    early = [move.start(w_in_in, w_in), move.start(x_in, x)]
    image_ends(seg, place[0] * rows, work)
    end_copy = move.start(work, ends)
    attended[...] = jnp.zeros_like(attended)
    spare = pl.ds(rows, triple.shape[0] - rows)
    triple[spare, :] = jnp.zeros((triple.shape[0] - rows, 3 * width), BF16)
    end_copy.wait()
    plan_groups(ends, place[0], rows, table)
    for copy in early:
        copy.wait()

    def step_copy(step):
        spot = pl.ds(pl.multiple_of(step * OWN, OWN), OWN)
        return pltpu.make_async_copy(triple.at[spot], triple_out.at[spot], tile_sems.at[step])

    def step_rows(step, _):
        spot = pl.ds(pl.multiple_of(step * OWN, OWN), OWN)
        project_rows(x[spot, :].astype(F32), gain1, shift1, w_in, b_in, triple, spot)
        step_copy(step).start()
        return 0

    lax.fori_loop(0, rows // OWN, step_rows, 0)
    attend_groups(jnp.maximum(table[GROUPS, 0] - 1, 1), table, triple, attended, stats, scores, peaks, raised, scales)
    leaving = move.start(attended, attended_out)
    for step in range(rows // OWN):
        step_copy(step).wait()
    leaving.wait()


def kernel_rest(
    place, table, gain1, shift1, b_in, b_out, gain2, shift2, b_ex,
    x_in, cot_in, halo_in, triple_in, attended_in, stats_in, w_in_in, w_out_in, w_ex_in, w_sh_in,
    middle_out, middle_grad_out, hidden_out, triple_grad_out, mine, other,
    x, back, w_in, w_out, w_ex, w_sh, triple, attended, middle, middle_grad, upstream, hidden, triple_grad, stats,
    d_ex, d_sh, d_out, product, sums, small, scores, peaks, raised, scales, probs_grads, probs, scores_grads,
    sems, tile_sems,
):
    rows, width = x_in.shape
    total = x.shape[0]
    tiles = total // FEED
    normed2, normed_grad = upstream, middle_grad
    move = Mover(sems)
    own, over = pl.ds(0, rows), pl.ds(rows, HALO)
    early = [
        move.start(halo_in.at[:, pl.ds(0, width)], x.at[over]),
        move.start(w_in_in, w_in),
        move.start(stats_in, stats),
        move.start(triple_in, triple.at[own]),
        move.start(attended_in, attended),
    ]
    late = [
        move.start(w_out_in, w_out),
        move.start(x_in, x.at[own]),
        move.start(cot_in, back.at[own]),
        move.start(halo_in.at[:, pl.ds(width, width)], back.at[over]),
        move.start(w_ex_in, w_ex),
        move.start(w_sh_in, w_sh),
    ]
    rest = pl.ds(rows + HALO, total - rows - HALO)
    x[rest, :] = jnp.zeros((total - rows - HALO, width), BF16)
    back[rest, :] = jnp.zeros((total - rows - HALO, width), BF16)
    for ref in (d_ex, d_sh, d_out, product, sums, small, triple_grad):
        ref[...] = jnp.zeros_like(ref)
    groups, first, end = table[GROUPS, 0], table[GROUPS, 1], table[GROUPS, 2]
    for copy in early:
        copy.wait()
    tail = pl.ds(rows, TILE)
    project_rows(x[tail, :].astype(F32), gain1, shift1, w_in, b_in, triple, tail)
    attend_groups(groups, table, triple, attended, stats, scores, peaks, raised, scales, alone=groups - 1)
    for copy in late:
        copy.wait()
    leaving = []

    hidden_width = w_ex.shape[1]
    begins = list(range(0, hidden_width, CHUNK))

    def wide_rows(step):
        return pl.ds(pl.multiple_of(step * WIDE, WIDE), WIDE)

    def before_feed(step, _):
        spot = wide_rows(step)
        value = x[spot, :].astype(F32) + dot(attended[spot, :], w_out[...]) + row_of(b_out)
        scaled, _inverse = normalize(value)
        middle[spot, :] = value
        normed2[spot, :] = (scaled * row_of(gain2) + row_of(shift2)).astype(BF16)
        keep = interval(step, first, end, WIDE)
        back[spot, :] = jnp.where(keep, back[spot, :].astype(F32), 0.0).astype(BF16)
        return 0

    def feed(tile, _):
        spot = pl.ds(pl.multiple_of(tile * FEED, FEED), FEED)
        normed = normed2[spot, :]
        back_low = back[spot, :]
        back_half = (0.5 * back_low.astype(F32)).astype(BF16)

        def first_part(begin):
            cols = slice(begin, begin + CHUNK)
            before = dot(normed, w_ex[:, cols]) + b_ex[cols].reshape(1, -1)
            return before, dot_nt(back_half, w_sh[cols, :])

        held = [first_part(begins[0])]
        total_grad = jnp.zeros((FEED, width), F32)
        for index, begin in enumerate(begins):
            cols = slice(begin, begin + CHUNK)
            if index + 1 < len(begins):
                held.append(first_part(begins[index + 1]))
            value, grad = gelu_parts(*held[index])
            value, grad = value.astype(BF16), grad.astype(BF16)
            hidden[spot, cols] = value
            total_grad = total_grad + dot_nt(grad, w_ex[:, cols])
            d_sh[:, cols] += dot_tn(back_low, value)
            d_ex[:, cols] += dot_tn(normed, grad)
            small[4:5, cols] += jnp.sum(grad.astype(F32), axis=0, keepdims=True)
        normed_grad[spot, :] = total_grad
        pltpu.make_async_copy(hidden.at[spot], hidden_out.at[spot], tile_sems.at[0]).start()
        return 0

    def after_feed(step, _):
        spot = wide_rows(step)
        back32 = back[spot, :].astype(F32)
        scaled, inverse = normalize(middle[spot, :])
        upstream2 = normed_grad[spot, :]
        small[0:1, :width] += jnp.sum(back32, axis=0, keepdims=True)
        small[1:2, :width] += jnp.sum(upstream2 * scaled, axis=0, keepdims=True)
        small[2:3, :width] += jnp.sum(upstream2, axis=0, keepdims=True)
        grad = back32 + normalize_back(upstream2, scaled, inverse, row_of(gain2))
        small[3:4, :width] += jnp.sum(grad, axis=0, keepdims=True)
        middle_grad[spot, :] = grad
        grad_low = grad.astype(BF16)
        d_out[...] += dot_tn(attended[spot, :], grad_low)
        upstream[spot, :] = dot_nt(grad_low, w_out[...]).astype(BF16)
        pltpu.make_async_copy(middle_grad.at[spot], middle_grad_out.at[spot], tile_sems.at[1]).start()
        return 0

    lax.fori_loop(0, total // WIDE, before_feed, 0)
    leaving.append(move.start(middle, middle_out))
    lax.fori_loop(0, tiles, feed, 0)
    lax.fori_loop(0, total // WIDE, after_feed, 0)
    attend_back_groups(
        groups, table, triple, attended, upstream, stats, triple_grad, scores, peaks, probs_grads, probs, scores_grads,
    )
    leaving.append(move.start(triple_grad, triple_grad_out))
    ones = jnp.ones((16, WIDE), BF16)

    def multiply(step, _):
        spot = wide_rows(step)
        scaled, _inverse = normalize(x[spot, :].astype(F32))
        grad = triple_grad[spot, :]
        product[...] += dot_tn(scaled.astype(BF16), grad)
        sums[...] += dot(ones, grad)
        return 0

    lax.fori_loop(0, total // WIDE, multiply, 0)
    gain = jnp.broadcast_to(row_of(gain1), (LANES, width)).T
    shift = jnp.broadcast_to(row_of(shift1), (LANES, width)).T
    by_gain = jnp.zeros((width, LANES), F32)
    by_shift = jnp.zeros((width, LANES), F32)
    for begin in range(0, 3 * width, LANES):
        cols = slice(begin, begin + LANES)
        block, sum_row = product[:, cols], sums[0:1, cols]
        weight = w_in[:, cols].astype(F32)
        by_gain = by_gain + weight * block
        by_shift = by_shift + weight * sum_row
        product[:, cols] = gain * block + shift * sum_row
    small[5:6, : 3 * width] = sums[0:1, :]
    by_gain = jnp.broadcast_to(jnp.sum(by_gain, axis=1, keepdims=True), (width, LANES)).T
    by_shift = jnp.broadcast_to(jnp.sum(by_shift, axis=1, keepdims=True), (width, LANES)).T
    small[6:7, :width] = by_gain[0:1]
    small[7:8, :width] = by_shift[0:1]
    pack((d_ex, d_sh, d_out, product), small, place[2], mine, other)
    for copy in leaving:
        copy.wait()
    pltpu.make_async_copy(hidden, hidden_out, tile_sems.at[0]).wait()
    pltpu.make_async_copy(middle_grad, middle_grad_out, tile_sems.at[1]).wait()


def pack(grads, small, core, mine, other):
    half = grads[0].shape[0] // 2
    at = 0
    for grad in grads:
        for begin in range(0, grad.shape[1], LANES):
            cols = slice(begin, begin + LANES)
            mine[pl.ds(at, half), :] = grad[pl.ds(pl.multiple_of(core * half, half), half), cols].astype(BF16)
            other[pl.ds(at, half), :] = grad[pl.ds(pl.multiple_of((1 - core) * half, half), half), cols].astype(BF16)
            at += half
    rest = mine.shape[0] - at
    mine[pl.ds(at, rest), :] = jnp.zeros((rest, LANES), BF16)
    other[pl.ds(at, rest), :] = jnp.zeros((rest, LANES), BF16)
    count = small.shape[1] // LANES
    for index in range(count):
        cols = slice(index * LANES, (index + 1) * LANES)
        spot = pl.ds(at + (index // 2) * 16, 16)

        @pl.when(core == index % 2)
        def _():
            mine[spot, :] = small[:, cols].astype(BF16)

        @pl.when(core != index % 2)
        def _():
            other[spot, :] = small[:, cols].astype(BF16)


def step_copies(arrays, step, sems):
    spot = pl.ds(step * WIDE, WIDE)
    return [
        pltpu.make_async_copy(source.at[spot], target.at[spot], sems.at[step, at])
        for at, (source, target) in enumerate(arrays)
    ]


def leave(value_ref, own_out, halo_out, step, sems):
    rows = own_out.shape[0]
    begin, end = step * WIDE, (step + 1) * WIDE
    own = pl.ds(begin, min(rows, end) - begin)
    copies = [pltpu.make_async_copy(value_ref.at[own], own_out.at[own], sems.at[step, 6])]
    if end > rows:
        copies.append(pltpu.make_async_copy(value_ref.at[pl.ds(rows, end - rows)], halo_out, sems.at[step, 7]))
    for copy in copies:
        copy.start()
    return copies


def kernel_input(
    after, gain1, x_in, halo_in, w_in_in, triple_grad_in, middle_grad_in, out, out_halo,
    x, w_in, triple_grad, middle_grad, sems, step_sems,
):
    rows, width = x_in.shape
    total = x.shape[0]
    move = Mover(sems)
    early = [
        move.start(w_in_in, w_in),
        move.start(x_in, x.at[pl.ds(0, rows)]),
        move.start(halo_in.at[:, pl.ds(0, width)], x.at[pl.ds(rows, HALO)]),
    ]
    arrays = ((triple_grad_in, triple_grad), (middle_grad_in, middle_grad))
    steps = range(total // WIDE)
    parts = [step_copies(arrays, step, step_sems) for step in steps]
    for part in parts:
        for copy in part:
            copy.start()
    x[pl.ds(rows + HALO, total - rows - HALO), :] = jnp.zeros((total - rows - HALO, width), BF16)
    for copy in early:
        copy.wait()
    leaving = []
    for step in steps:
        for copy in parts[step]:
            copy.wait()
        spot = pl.ds(step * WIDE, WIDE)
        scaled, inverse = normalize(x[spot, :].astype(F32))
        normed_grad = dot_nt(triple_grad[spot, :], w_in[...])
        middle_grad[spot, :] = middle_grad[spot, :] + normalize_back(normed_grad, scaled, inverse, row_of(gain1))
        leaving += leave(middle_grad, out, out_halo, step, step_sems)
    for copy in leaving:
        copy.wait()


def kernel_result(
    after, table, b_sh, middle_in, hidden_in, w_sh_in, out, out_halo, middle, hidden, w_sh, value, sems, step_sems,
):
    total = middle.shape[0]
    move = Mover(sems)
    weight_copy = move.start(w_sh_in, w_sh)
    arrays = ((middle_in, middle), (hidden_in, hidden))
    steps = range(total // WIDE)
    parts = [step_copies(arrays, step, step_sems) for step in steps]
    for part in parts:
        for copy in part:
            copy.start()
    weight_copy.wait()
    leaving = []
    for step in steps:
        for copy in parts[step]:
            copy.wait()
        spot = pl.ds(step * WIDE, WIDE)
        keep = interval(step, table[GROUPS, 1], table[GROUPS, 2], WIDE)
        row = middle[spot, :] + row_of(b_sh) + dot(hidden[spot, :], w_sh[...])
        value[spot, :] = jnp.where(keep, row, 0.0).astype(BF16)
        leaving += leave(value, out, out_halo, step, step_sems)
    for copy in leaving:
        copy.wait()


def kernel_add(mine, other, out):
    out[...] = (mine[...].astype(F32) + other[...].astype(F32)).astype(BF16)


def kernel_sum(extra, *refs):
    parts_in, out, parts, piece, sems = refs[extra:]
    count = parts.shape[0]
    quarter = max(count // 4, 1)
    copies = []
    for index, begin in enumerate(range(0, count, quarter)):
        spot = pl.ds(begin, quarter)
        copies.append(pltpu.make_async_copy(parts_in.at[spot], parts.at[spot], sems.at[index]))
        copies[-1].start()
    total = jnp.zeros(piece.shape, F32)
    for index, copy in enumerate(copies):
        copy.wait()
        for part in range(index * quarter, (index + 1) * quarter):
            total = total + parts[part].astype(F32)
    piece[...] = total.astype(BF16)
    for part in range(count):
        pltpu.make_async_copy(piece, out.at[part], sems.at[4]).start()
    pltpu.make_async_copy(parts, out, sems.at[4]).wait()


def halves_of(place, mine, other):
    def both(at, count):
        first, second = mine[pl.ds(at, count), :].astype(F32), other[pl.ds(at, count), :].astype(F32)
        swap = place[2] == 1
        return jnp.where(swap, second, first), jnp.where(swap, first, second)

    return both


def unpack(both, at, out):
    for begin in range(0, out.shape[1], LANES):
        low, high = both(at, 192)
        out[:192, begin : begin + LANES] = low
        out[192:, begin : begin + LANES] = high
        at += 192
    return at


def small_blocks(both, at, columns):
    blocks = []
    for index in range(columns // LANES):
        blocks.append(both(at + index // 2 * 16, 16)[index % 2])
    return jnp.concatenate(blocks, axis=1)


def kernel_unpack(
    place, mine, other, d_ex, d_sh, d_out, d_in, b_in, b_sh, gain2, shift2, b_out, b_ex, gain1, shift1
):
    both = halves_of(place, mine, other)
    width = d_out.shape[0]
    at = unpack(both, 0, d_ex)
    for begin in range(0, d_sh.shape[0], LANES):
        low, high = both(at, 192)
        d_sh[begin : begin + LANES, :] = jnp.concatenate([low, high], axis=0).T
        at += 192
    small = small_blocks(both, unpack(both, unpack(both, at, d_out), d_in), d_ex.shape[1])
    for row, ref in ((0, b_sh), (1, gain2), (2, shift2), (3, b_out), (6, gain1), (7, shift1)):
        ref[...] = small[row, :width]
    b_ex[...] = small[4]
    b_in[0:1, :] = small[5:6, :width]
    b_in[1:2, :] = small[5:6, 2 * width : 3 * width]


VMEM = pl.BlockSpec(memory_space=pltpu.VMEM)
SMEM = pl.BlockSpec(memory_space=pltpu.SMEM)
ANY = pl.BlockSpec(memory_space=pl.ANY)


def params(mib):
    return pltpu.CompilerParams(vmem_limit_bytes=mib * 1024 * 1024)


def cost(flops, moved):
    return pl.CostEstimate(flops=int(flops), bytes_accessed=int(moved), transcendentals=0)


def shape(dims, dtype):
    return jax.ShapeDtypeStruct(dims, dtype)


def packed_rows(columns, small, pieces):
    half = columns // LANES * 192 + (small // LANES + 1) // 2 * 16
    return pieces * (-(-half // (8 * pieces)) * 8)


def attention_scratch(pairs):
    return [
        [pltpu.VMEM((pairs, WIN, 2 * WIN), F32)] * 2,
        [pltpu.VMEM((8, 2 * WIN), F32)] * 2,
        [pltpu.VMEM((pairs, 2 * WIN, WIN), BF16)] * 2,
        [pltpu.VMEM((8, 2 * WIN), F32)] * 2,
    ]


def own_part(place, segments, gain1, shift1, b_in, x, w_in):
    rows, width = x.shape
    total = rows + TILE
    vmem = pltpu.VMEM
    return pl.pallas_call(
        kernel_own,
        out_shape=(
            shape((rows, 3 * width), BF16),
            shape((total, width), BF16),
            shape((GROUPS, 8, WIN), F32),
            shape((GROUPS + 1, 8), jnp.int32),
        ),
        in_specs=[SMEM] + [VMEM] * 4 + [ANY] * 2,
        out_specs=(ANY, ANY, VMEM, SMEM),
        scratch_shapes=[
            vmem((rows, width), BF16),
            vmem(w_in.shape, BF16),
            vmem((total, 3 * width), BF16),
            vmem((total, width), BF16),
            vmem((8, LANES), jnp.int32),
            pltpu.SMEM((8, LANES), jnp.int32),
            *attention_scratch(width // (2 * HD)),
            pltpu.SemaphoreType.DMA((8,)),
            pltpu.SemaphoreType.DMA((rows // OWN,)),
        ],
        compiler_params=params(58),
        cost_estimate=cost(2 * 6 * rows * width * 3 * width, 1e7),
        name="own_part",
    )(place, segments, gain1, shift1, b_in, x, w_in)


def rest_part(place, table, vectors, x, cot, halo, triple, attended, stats, w_in, w_out, w_ex, w_sh, pieces):
    rows, width = x.shape
    total = rows + TILE
    hidden = w_ex.shape[1]
    packed = packed_rows(2 * hidden + 4 * width, hidden, pieces)
    vmem = pltpu.VMEM
    pairs = width // (2 * HD)
    square, row = vmem((pairs, WIN, 2 * WIN), F32), vmem((8, 2 * WIN), F32)
    low = vmem((pairs, WIN, 2 * WIN), BF16)
    return pl.pallas_call(
        kernel_rest,
        out_shape=(
            shape((total, width), F32),
            shape((total, width), F32),
            shape((total, hidden), BF16),
            shape((total, 3 * width), BF16),
            shape((packed, LANES), BF16),
            shape((packed, LANES), BF16),
        ),
        in_specs=[SMEM, SMEM] + [VMEM] * 7 + [ANY] * 10,
        out_specs=tuple([ANY] * 4 + [VMEM] * 2),
        scratch_shapes=[
            vmem((total, width), BF16),
            vmem((total, width), BF16),
            vmem(w_in.shape, BF16),
            vmem(w_out.shape, BF16),
            vmem(w_ex.shape, BF16),
            vmem(w_sh.shape, BF16),
            vmem((total, 3 * width), BF16),
            vmem((total, width), BF16),
            vmem((total, width), F32),
            vmem((total, width), F32),
            vmem((total, width), BF16),
            vmem((total, hidden), BF16),
            vmem((total, 3 * width), BF16),
            vmem((GROUPS, 8, WIN), F32),
            vmem((width, hidden), F32),
            vmem((width, hidden), F32),
            vmem((width, width), F32),
            vmem((width, 3 * width), F32),
            vmem((16, 3 * width), F32),
            vmem((16, hidden), F32),
            [square] * 2,
            [row] * 2,
            [vmem((pairs, 2 * WIN, WIN), BF16)],
            [row],
            [square] * 2,
            [low] * 2,
            [low] * 2,
            pltpu.SemaphoreType.DMA((16,)),
            pltpu.SemaphoreType.DMA((2,)),
        ],
        compiler_params=params(62),
        cost_estimate=cost(2 * 9 * rows * width * (3 * width + 8 * width), 3e7),
        name="rest_part",
    )(place, table, *vectors, x, cot, halo, triple, attended, stats, w_in, w_out, w_ex, w_sh)


def input_gradient(after, gain1, x, halo, w_in, triple_grad, middle_grad):
    rows, width = x.shape
    total = triple_grad.shape[0]
    vmem = pltpu.VMEM
    return pl.pallas_call(
        kernel_input,
        out_shape=(shape((rows, width), F32), shape((TILE, width), F32)),
        in_specs=[ANY, VMEM] + [ANY] * 5,
        out_specs=(ANY, ANY),
        scratch_shapes=[
            vmem((total, width), BF16),
            vmem(w_in.shape, BF16),
            vmem((total, 3 * width), BF16),
            vmem((total, width), F32),
            pltpu.SemaphoreType.DMA((4,)),
            pltpu.SemaphoreType.DMA((total // WIDE, 8)),
        ],
        compiler_params=params(58),
        cost_estimate=cost(2 * rows * width * 9 * width, 1.4e7),
        name="input_gradient",
    )(after, gain1, x, halo, w_in, triple_grad, middle_grad)


def layer_result(after, table, b_sh, middle, hidden, w_sh):
    total, width = middle.shape
    vmem = pltpu.VMEM
    return pl.pallas_call(
        kernel_result,
        out_shape=(shape((total - TILE, width), BF16), shape((TILE, width), BF16)),
        in_specs=[ANY, SMEM, VMEM] + [ANY] * 3,
        out_specs=(ANY, ANY),
        scratch_shapes=[
            vmem(middle.shape, F32),
            vmem(hidden.shape, BF16),
            vmem(w_sh.shape, BF16),
            vmem(middle.shape, BF16),
            pltpu.SemaphoreType.DMA((2,)),
            pltpu.SemaphoreType.DMA((total // WIDE, 8)),
        ],
        compiler_params=params(58),
        cost_estimate=cost(2 * total * width * 8 * width, 1.3e7),
        name="layer_result",
    )(after, table, b_sh, middle, hidden, w_sh)


def add_halves(mine, other):
    return pl.pallas_call(
        kernel_add,
        out_shape=shape(mine.shape, BF16),
        in_specs=[VMEM, VMEM],
        out_specs=VMEM,
        compiler_params=params(58),
        cost_estimate=cost(mine.size, mine.size * 6),
        name="add_halves",
    )(mine, other)


def sum_parts(after, parts):
    return pl.pallas_call(
        partial(kernel_sum, len(after)),
        out_shape=shape(parts.shape, BF16),
        in_specs=[ANY] * (len(after) + 1),
        out_specs=ANY,
        scratch_shapes=[
            pltpu.VMEM(parts.shape, BF16),
            pltpu.VMEM(parts.shape[1:], BF16),
            pltpu.SemaphoreType.DMA((5,)),
        ],
        compiler_params=params(58),
        cost_estimate=cost(parts.size, parts.size * 4),
        name="sum_parts",
    )(*after, parts)


def unpack_call(kernel, name, place, mine, other, shapes):
    return pl.pallas_call(
        kernel,
        out_shape=tuple(shape(dims, F32) for dims in shapes),
        in_specs=[SMEM, VMEM, VMEM],
        out_specs=tuple([VMEM] * len(shapes)),
        compiler_params=params(58),
        cost_estimate=cost(mine.size, mine.size * 12),
        name=name,
    )(place, mine, other)


def same_core_groups():
    packs, parts = lax.axis_size("dp"), lax.axis_size("mp")
    return [[d * parts + m for d in range(c, packs, 2) for m in range(parts)] for c in range(2)]


def swap_cores(block):
    packs = lax.axis_size("dp")
    return lax.ppermute(block, "dp", [(i, i ^ 1) for i in range(packs)])


def exchange(parts):
    return lax.all_to_all(parts, ("dp", "mp"), 0, 0, axis_index_groups=same_core_groups())


def passed(block, distance):
    count = lax.axis_size("mp")
    route = [(i, i + distance) for i in range(count) if 0 <= i + distance < count]
    return lax.ppermute(block, "mp", route)


def take_over(own, other, first):
    row = lax.broadcasted_iota(jnp.int32, (HALO, 1), 0)
    return lax.dynamic_update_slice(own, jnp.where(row < first, other, own[:HALO]), (0, 0))


def body(
    layer_input, segments, cotangent, first_gain, first_shift, inward_weight, inward_bias, outward_weight,
    outward_bias, second_gain, second_shift, expand_weight, expand_bias, shrink_weight, shrink_bias,
):
    rows, width = layer_input.shape
    hidden_width = expand_weight.shape[1]
    position = lax.axis_index("mp")
    core = lax.axis_index("dp") % 2
    pieces = lax.axis_size("dp") * lax.axis_size("mp") // 2
    place = jnp.stack([position, position, core]).astype(jnp.int32)
    gain1, shift1, b_out, gain2, shift2, b_ex, b_sh = (
        first_gain, first_shift, outward_bias, second_gain, second_shift, expand_bias, shrink_bias
    )
    halo = passed(jnp.concatenate([layer_input[:HALO], cotangent[:HALO]], axis=1), -1)
    triple, attended, stats, table = own_part(
        place, segments, gain1, shift1, inward_bias, layer_input, inward_weight
    )
    middle, middle_grad, hidden, triple_grad, mine, other = rest_part(
        place, table, (gain1, shift1, inward_bias, b_out, gain2, shift2, b_ex), layer_input, cotangent, halo, triple,
        attended, stats, inward_weight, outward_weight, expand_weight, shrink_weight, pieces,
    )
    both = add_halves(mine, swap_cores(other))
    parts = exchange(both.reshape(pieces, -1, LANES))
    input_grad, input_halo = input_gradient(both, gain1, layer_input, halo, inward_weight, triple_grad, middle_grad)
    result, result_halo = layer_result(input_halo, table, b_sh, middle, hidden, shrink_weight)
    first = table[GROUPS, 1]
    input_grad = take_over(input_grad, passed(input_halo[:HALO], 1), first)
    result = take_over(result, passed(result_halo[:HALO], 1), first)
    mine = exchange(sum_parts((input_grad, result), parts)).reshape(-1, LANES)
    square, row = (width, width), (width,)
    d_ex, d_sh, d_out, d_in, d_b_in, d_b_sh, d_gain2, d_shift2, d_b_out, d_b_ex, d_gain1, d_shift1 = unpack_call(
        kernel_unpack, "unpack", place, mine, swap_cores(mine),
        ((width, hidden_width), (hidden_width, width), square, (width, 3 * width), (2, width)) + (row,) * 4
        + ((hidden_width,), row, row),
    )
    return (
        result, input_grad, d_gain1, d_shift1, d_in, d_b_in, d_out, d_b_out, d_gain2, d_shift2, d_ex, d_b_ex, d_sh,
        d_b_sh,
    )


def solution(mesh):
    rows = P(("dp", "mp"), None)
    in_specs = (rows, P("dp", None), rows) + (P(),) * 12
    out_specs = (rows, rows) + (P(),) * 12
    return jax.shard_map(body, mesh=mesh, in_specs=in_specs, out_specs=out_specs, check_vma=False)
```

time: 276 us -> 198 us (0.72)
  local copies, waits for them, and re-layouts: 31.2 us -> 8.49 us
  waiting for transfers between devices: 30.6 us -> 10.5 us
  Pallas kernels: 126 us -> 110 us
  starting transfers between devices: 41.1 us -> 26.9 us
  other arithmetic: 14.2 us -> 4.75 us
  blocking collectives: 29.3 us -> 35.7 us
    all_to_all x3 -> x1, waiting for transfers between devices: 25.2 us -> 0.01 us  [exchange(): lax.all_to_all(parts, ('dp', 'mp'), 0, 0, axis_index_groups=same_core_gro...]
    pallas_call x2 -> x7, Pallas kernels: 126 us -> 110 us  [the longest x1 58.7 us: rest_part(): pl.pallas_call(kernel_rest, out_shape=(shape((total, width), F32), shape(...]
    broadcast_in_dim x9 -> x0, local copies, waits for them, and re-layouts: 10.9 us -> none  [the longest x2 2.15 us: gather_sum(): sent = jnp.broadcast_to(piece[None], (pieces,) + piece.shape)]
    all_to_all x3 -> x1, starting transfers between devices: 19.2 us -> 10.6 us  [exchange(): lax.all_to_all(parts, ('dp', 'mp'), 0, 0, axis_index_groups=same_core_gro...]
    all_to_all x1, blocking collectives: 29.3 us -> 35.7 us  [exchange(): lax.all_to_all(parts, ('dp', 'mp'), 0, 0, axis_index_groups=same_core_gro...]
    convert_element_type x7 -> x0, other arithmetic: 6.28 us -> none  [the longest x2 4.01 us: scatter_sum(): both = (mine.astype(F32) + swap_cores(other).astype(F32)).astype(BF16)]
    ppermute x4 -> x2, waiting for transfers between devices: 1.66 us -> 7.03 us  [swap_cores(): return lax.ppermute(block, 'dp', [(i, i ^ 1) for i in range(packs)])]
    ppermute x4 -> x2, starting transfers between devices: 13.3 us -> 9.27 us  [swap_cores(): return lax.ppermute(block, 'dp', [(i, i ^ 1) for i in range(packs)])]
  transfers between devices with their start and end apart: 11 -> 6, of which waited for: 5 -> 3; matrix products, arithmetic and copies ran while one was open for 10% -> 4% of each run, Pallas kernels for 0% -> 20%
where the time goes in v2:
time: 198 us; the launch traced here: 197 us
  Pallas kernels  110 us (56%)
  blocking collectives  35.7 us (18%)
  starting transfers between devices  26.9 us (14%)
  waiting for transfers between devices  10.5 us (5%)
  local copies, waits for them, and re-layouts  8.49 us (4%)
  other arithmetic  4.75 us (2%)
    pallas_call x1, Pallas kernels, rest_part(): pl.pallas_call(kernel_rest, out_shape=(shape((total, width), F32), shape(...  58.7 us
    all_to_all x1, blocking collectives, exchange(): lax.all_to_all(parts, ('dp', 'mp'), 0, 0, axis_index_groups=same_core_gro...  35.7 us
    pallas_call x1, Pallas kernels, own_part(): pl.pallas_call(kernel_own, out_shape=(shape((rows, 3 * width), BF16), sha...  19.3 us
    all_to_all x1, starting transfers between devices, exchange(): lax.all_to_all(parts, ('dp', 'mp'), 0, 0, axis_index_groups=same_core_gro...  10.6 us
    pallas_call x1, Pallas kernels, layer_result(): pl.pallas_call(kernel_result, out_shape=(shape((total - TILE, width), BF1...  10 us
    pallas_call x1, Pallas kernels, input_gradient(): pl.pallas_call(kernel_input, out_shape=(shape((rows, width), F32), shape(...  9.71 us
    ppermute x2, starting transfers between devices, swap_cores(): return lax.ppermute(block, 'dp', [(i, i ^ 1) for i in range(packs)])  9.27 us
    ppermute x3, starting transfers between devices, passed(): return lax.ppermute(block, 'mp', route)  7.06 us
  transfers between devices with their start and end apart: 6, of which 3 were waited for; matrix products, arithmetic and copies ran while one was open for 4% of the time, Pallas kernels for 20%

profile of v2, /device:TPU:1, one launch (start us, length us, event | category | flops | bytes accessed | tf_op | source)
XLA Modules:
  0.0 197.0 jit_solution(3026616189268777159)
XLA Ops:
  0.6 0.9 slice.21
  2.6 1.3 collective-permute-start
  4.4 19.3 %own_part.1 = (bf16[2048,1152]{1,0:T(8,128)(2,1)}, bf16[2304,384]{1,0:T(8,128)(2,1)}, f32[24,8,256]{2,1,0:T(8,128)}, s32[25,8]{1,0:T(8,128)}) custom-call(s32[3]{0:T(128)} %pad_add_fusion.place, s32[1,8192]{1,0:T(1,128)} %seg.1, f32[384]{0:T(512)} %gain1.5, f32[384]{0:T(512)} %shift1.3, f32[2,384]{1,0:T(2,128)} %b_in.3, bf16[2048,384]{1,0:T(8,128)(2,1)} %x_in.5, ...), custom_call_target="tpu_custom_call" | custom-call | flops 10871635968 | bytes 10000000 | tf_op jit(solution)/shard_map/own_part/pallas_call | solution.py:696
  24.5 58.7 %rest_part.1 = (f32[2304,384]{1,0:T(8,128)}, f32[2304,384]{1,0:T(8,128)}, bf16[2304,1536]{1,0:T(8,128)(2,1)}, bf16[2304,1152]{1,0:T(8,128)(2,1)}, bf16[7168,128]{1,0:T(8,128)(2,1)}, /*index=5*/bf16[7168,128]{1,0:T(8,128)(2,1)}) custom-call(s32[3]{0:T(128)} %pad_add_fusion.place, s32[25,8]{1,0:T(8,128)} %get-tuple-element.40.table, f32[384]{0:T(512)} %gain1.5, ...), custom_call_target="tpu_custom_call" | custom-call | flops 59793997824 | bytes 30000000 | tf_op jit(solution)/shard_map/rest_part/pallas_call | solution.py:732
  83.2 5.9 %collective-permute-start.1 = (bf16[7168,128]{1,0:T(8,128)(2,1)}, bf16[7168,128]{1,0:T(8,128)(2,1)S(1)}, u32[]{:S(2)}, u32[]{:S(2)}) collective-permute-start(bf16[7168,128]{1,0:T(8,128)(2,1)} %get-tuple-element.45), channel_id=1, source_target_pairs={{0,4},{4,0},{8,12},{12,8},{16,20},{20,16},{24,28},{28,24},{32,36},... | collective-permute-start | bytes 5505032 | tf_op jit(solution)/shard_map/ppermute | solution.py:874
  89.1 3.6 %collective-permute-done.1.other = bf16[7168,128]{1,0:T(8,128)(2,1)S(1)} collective-permute-done((bf16[7168,128]{1,0:T(8,128)(2,1)}, bf16[7168,128]{1,0:T(8,128)(2,1)S(1)}, u32[]{:S(2)}, u32[]{:S(2)}) %collective-permute-start.1) | collective-permute-done | bytes 1835040 | tf_op jit(solution)/shard_map/ppermute | solution.py:874
  92.7 1.2 copy-done.3
  94.0 3.7 %add_halves.1.after = bf16[7168,128]{1,0:T(8,128)(2,1)} custom-call(bf16[7168,128]{1,0:T(8,128)(2,1)} %get-tuple-element.44.mine, bf16[7168,128]{1,0:T(8,128)(2,1)} %copy-done.3), custom_call_target="tpu_custom_call" | custom-call | flops 917504 | bytes 5505024 | tf_op jit(solution)/shard_map/add_halves/pallas_call | solution.py:827
  97.7 10.6 %all-to-all-start = ((bf16[64,112,128]{2,1,0:T(8,128)(2,1)}), bf16[64,112,128]{2,1,0:T(8,128)(2,1)S(1)}, u32[]{:S(2)}, u32[]{:S(2)}) async-start(bf16[64,112,128]{2,1,0:T(8,128)(2,1)} %bitcast.7), calls=%async_computation | async-start | bytes 3670016 | tf_op jit(solution)/shard_map/all_to_all | solution.py:878
  108.2 9.7 %input_gradient.1 = (f32[2048,384]{1,0:T(8,128)}, f32[256,384]{1,0:T(8,128)}) custom-call(bf16[7168,128]{1,0:T(8,128)(2,1)} %add_halves.1.after, f32[384]{0:T(512)} %gain1.5, bf16[2048,384]{1,0:T(8,128)(2,1)} %x_in.5, bf16[208,768]{1,0:T(8,128)(2,1)} %copy-done.5, bf16[384,1152]{1,0:T(8,128)(2,1)} %w_in_in.5, ...), custom_call_target="tpu_custom_call" | custom-call | flops 5435817984 | bytes 14000000 | tf_op jit(solution)/shard_map/input_gradient/pallas_call | solution.py:785
  118.0 10.0 %layer_result.1 = (bf16[2048,384]{1,0:T(8,128)(2,1)}, bf16[256,384]{1,0:T(8,128)(2,1)}) custom-call(f32[256,384]{1,0:T(8,128)} %get-tuple-element.48.after, s32[25,8]{1,0:T(8,128)} %get-tuple-element.40.table, f32[384]{0:T(512)} %b_sh.1, f32[2304,384]{1,0:T(8,128)} %get-tuple-element.49.middle_in, bf16[2304,1536]{1,0:T(8,128)(2,1)} %get-tuple-element.50.hidden_in, ...), custom_call_target="tpu_custom_call" | custom-call | flops 5435817984 | bytes 13000000 | tf_op jit(solution)/shard_map/layer_result/pallas_call | solution.py:807
  129.0 2.7 %collective-permute-start.2 = (bf16[208,384]{1,0:T(8,128)(2,1)S(1)}, bf16[208,384]{1,0:T(8,128)(2,1)S(1)}, u32[]{:S(2)}, u32[]{:S(2)}) collective-permute-start(bf16[208,384]{1,0:T(8,128)(2,1)S(1)} %slice.24), channel_id=1, source_target_pairs={{0,1},{1,2},{2,3},{4,5},{5,6},{6,7},{8,9},{9,10},{10,11},{12,13},{... | collective-permute-start | bytes 479240 | tf_op jit(solution)/shard_map/ppermute | solution.py:884
  131.6 1.3 slice.23
  132.9 3.1 %collective-permute-start.3 = (f32[208,384]{1,0:T(8,128)S(1)}, f32[208,384]{1,0:T(8,128)S(1)}, u32[]{:S(2)}, u32[]{:S(2)}) collective-permute-start(f32[208,384]{1,0:T(8,128)S(1)} %slice.26), channel_id=1, source_target_pairs={{0,1},{1,2},{2,3},{4,5},{5,6},{6,7},{8,9},{9,10},{10,11},{12,13},{... | collective-permute-start | bytes 958472 | tf_op jit(solution)/shard_map/ppermute | solution.py:884
  136.7 1.7 select_dynamic-update-slice_fusion.1.refs_1_
  138.4 3.4 %collective-permute-done.3 = f32[208,384]{1,0:T(8,128)S(1)} collective-permute-done((f32[208,384]{1,0:T(8,128)S(1)}, f32[208,384]{1,0:T(8,128)S(1)}, u32[]{:S(2)}, u32[]{:S(2)}) %collective-permute-start.3) | collective-permute-done | bytes 319520 | tf_op jit(solution)/shard_map/ppermute | solution.py:884
  141.8 1.8 select_dynamic-update-slice_fusion.refs_0_
  143.6 1.2 copy-done.1
  144.8 2.7 %sum_parts.1 = bf16[64,112,128]{2,1,0:T(8,128)(2,1)} custom-call(f32[2048,384]{1,0:T(8,128)} %select_dynamic-update-slice_fusion.refs_0_, bf16[2048,384]{1,0:T(8,128)(2,1)} %select_dynamic-update-slice_fusion.1.refs_1_, bf16[64,112,128]{2,1,0:T(8,128)(2,1)} %copy-done.1), custom_call_target="tpu_custom_call" | custom-call | flops 917504 | bytes 3670016 | tf_op jit(solution)/shard_map/sum_parts/pallas_call | solution.py:839
  147.6 35.7 %all_to_all.10 = bf16[64,112,128]{2,1,0:T(8,128)(2,1)S(1)} all-to-all(bf16[64,112,128]{2,1,0:T(8,128)(2,1)} %sum_parts.1), channel_id=1, replica_groups={{0,1,2,3,8,9,10,11,16,17,18,19,24,25,26,27,32,33,34,35,40,41,42,43,48,4..., dimensions={0} | all-to-all | bytes 3670016 | tf_op jit(solution)/shard_map/all_to_all | solution.py:878
  183.3 3.4 %collective-permute-start.4 = (bf16[7168,128]{1,0:T(8,128)(2,1)S(1)}, bf16[7168,128]{1,0:T(8,128)(2,1)S(1)}, u32[]{:S(2)}, u32[]{:S(2)}) collective-permute-start(bf16[7168,128]{1,0:T(8,128)(2,1)S(1)} %bitcast.5), channel_id=1, source_target_pairs={{0,4},{4,0},{8,12},{12,8},{16,20},{20,16},{24,28},{28,24},{32,36},... | collective-permute-start | bytes 5505032 | tf_op jit(solution)/shard_map/ppermute | solution.py:874
  186.7 3.4 %collective-permute-done.4.other = bf16[7168,128]{1,0:T(8,128)(2,1)S(1)} collective-permute-done((bf16[7168,128]{1,0:T(8,128)(2,1)S(1)}, bf16[7168,128]{1,0:T(8,128)(2,1)S(1)}, u32[]{:S(2)}, u32[]{:S(2)}) %collective-permute-start.4) | collective-permute-done | bytes 1835040 | tf_op jit(solution)/shard_map/ppermute | solution.py:874
  190.1 1.2 copy-done.2
  191.3 5.5 %unpack.1 = (f32[384,1536]{1,0:T(8,128)}, f32[1536,384]{1,0:T(8,128)}, f32[384,384]{1,0:T(8,128)}, f32[384,1152]{1,0:T(8,128)}, f32[2,384]{1,0:T(2,128)}, /*inde...) custom-call(s32[3]{0:T(128)} %pad_add_fusion.place, ...), custom_call_target="tpu_custom_call" | custom-call | flops 917504 | bytes 11010048 | tf_op jit(solution)/shard_map/unpack/pallas_call | solution.py:856
  (18 shorter events, 3.9 us)
Async XLA Ops:
  2.6 21.2 %collective-permute-start = (bf16[208,768]{1,0:T(8,128)(2,1)S(1)}, bf16[208,768]{1,0:T(8,128)(2,1)S(1)}, u32[]{:S(2)}, u32[]{:S(2)}) collective-permute-start(bf16[208,768]{1,0:T(8,128)(2,1)S(1)} %pad_maximum_fusion), channel_id=1, source_target_pairs={{1,0},{2,1},{3,2},{5,4},{6,5},{7,6},{9,8},{10,9},{11,10},{13,12},{... | collective-permute-start | bytes 958472 | tf_op jit(solution)/shard_map/ppermute | solution.py:884
  23.7 0.7 copy-start.5
  83.2 9.5 %collective-permute-start.1 = (bf16[7168,128]{1,0:T(8,128)(2,1)}, bf16[7168,128]{1,0:T(8,128)(2,1)S(1)}, u32[]{:S(2)}, u32[]{:S(2)}) collective-permute-start(bf16[7168,128]{1,0:T(8,128)(2,1)} %get-tuple-element.45), channel_id=1, source_target_pairs={{0,4},{4,0},{8,12},{12,8},{16,20},{20,16},{24,28},{28,24},{32,36},... | collective-permute-start | bytes 5505032 | tf_op jit(solution)/shard_map/ppermute | solution.py:874
  92.7 1.2 copy-start.3
  97.7 45.9 %all-to-all-start = ((bf16[64,112,128]{2,1,0:T(8,128)(2,1)}), bf16[64,112,128]{2,1,0:T(8,128)(2,1)S(1)}, u32[]{:S(2)}, u32[]{:S(2)}) async-start(bf16[64,112,128]{2,1,0:T(8,128)(2,1)} %bitcast.7), calls=%async_computation | async-start | bytes 3670016 | tf_op jit(solution)/shard_map/all_to_all | solution.py:878
  118.0 14.9 %copy-start.4 = (f32[256,384]{1,0:T(8,128)S(1)}, f32[256,384]{1,0:T(8,128)}, u32[]{:S(2)}) copy-start(f32[256,384]{1,0:T(8,128)} %get-tuple-element.48.after) | copy-start | bytes 1179652
  129.0 7.7 %collective-permute-start.2 = (bf16[208,384]{1,0:T(8,128)(2,1)S(1)}, bf16[208,384]{1,0:T(8,128)(2,1)S(1)}, u32[]{:S(2)}, u32[]{:S(2)}) collective-permute-start(bf16[208,384]{1,0:T(8,128)(2,1)S(1)} %slice.24), channel_id=1, source_target_pairs={{0,1},{1,2},{2,3},{4,5},{5,6},{6,7},{8,9},{9,10},{10,11},{12,13},{... | collective-permute-start | bytes 479240 | tf_op jit(solution)/shard_map/ppermute | solution.py:884
  132.9 8.9 %collective-permute-start.3 = (f32[208,384]{1,0:T(8,128)S(1)}, f32[208,384]{1,0:T(8,128)S(1)}, u32[]{:S(2)}, u32[]{:S(2)}) collective-permute-start(f32[208,384]{1,0:T(8,128)S(1)} %slice.26), channel_id=1, source_target_pairs={{0,1},{1,2},{2,3},{4,5},{5,6},{6,7},{8,9},{9,10},{10,11},{12,13},{... | collective-permute-start | bytes 958472 | tf_op jit(solution)/shard_map/ppermute | solution.py:884
  143.6 1.2 copy-start.1
  183.3 6.8 %copy-start = (bf16[64,112,128]{2,1,0:T(8,128)(2,1)}, bf16[64,112,128]{2,1,0:T(8,128)(2,1)S(1)}, u32[]{:S(2)}) copy-start(bf16[64,112,128]{2,1,0:T(8,128)(2,1)S(1)} %all_to_all.10) | copy-start | bytes 5505028
  183.3 6.8 %collective-permute-start.4 = (bf16[7168,128]{1,0:T(8,128)(2,1)S(1)}, bf16[7168,128]{1,0:T(8,128)(2,1)S(1)}, u32[]{:S(2)}, u32[]{:S(2)}) collective-permute-start(bf16[7168,128]{1,0:T(8,128)(2,1)S(1)} %bitcast.5), channel_id=1, source_target_pairs={{0,4},{4,0},{8,12},{12,8},{16,20},{20,16},{24,28},{28,24},{32,36},... | collective-permute-start | bytes 5505032 | tf_op jit(solution)/shard_map/ppermute | solution.py:874
  190.1 1.2 copy-start.2

commit v3 on v2

--- a/solution.py
+++ b/solution.py
@@ -292,9 +292,10 @@
         return copy
 
 
-def project_rows(rows, gain1, shift1, w_in, b_in, target, spot):
+def project_rows(rows, gain1, shift1, w_in, b_in, target, spot, scaled_ref, scaled_spot):
     width = rows.shape[1]
     scaled, _inverse = normalize(rows)
+    scaled_ref[scaled_spot, :] = scaled.astype(BF16)
     normed = (scaled * row_of(gain1) + row_of(shift1)).astype(BF16)
     q = dot(normed, w_in[:, :width]) + b_in[0:1, :]
     target[spot, :width] = (q.astype(BF16).astype(F32) * HD ** (-0.5)).astype(BF16)
@@ -304,7 +305,7 @@
 
 def kernel_own(
     place, seg, gain1, shift1, b_in, x_in, w_in_in,
-    triple_out, attended_out, stats, table,
+    triple_out, attended_out, scaled_out, stats, table,
     x, w_in, triple, attended, work, ends, scores, peaks, raised, scales, sems, tile_sems,
 ):
     rows, width = x_in.shape
@@ -326,13 +327,15 @@
 
     def step_rows(step, _):
         spot = pl.ds(pl.multiple_of(step * OWN, OWN), OWN)
-        project_rows(x[spot, :].astype(F32), gain1, shift1, w_in, b_in, triple, spot)
+        project_rows(x[spot, :].astype(F32), gain1, shift1, w_in, b_in, triple, spot, x, spot)
         step_copy(step).start()
         return 0
 
     lax.fori_loop(0, rows // OWN, step_rows, 0)
+    scaled_copy = move.start(x, scaled_out)
     attend_groups(jnp.maximum(table[GROUPS, 0] - 1, 1), table, triple, attended, stats, scores, peaks, raised, scales)
     leaving = move.start(attended, attended_out)
+    scaled_copy.wait()
     for step in range(rows // OWN):
         step_copy(step).wait()
     leaving.wait()
@@ -340,11 +343,11 @@
 
 def kernel_rest(
     place, table, gain1, shift1, b_in, b_out, gain2, shift2, b_ex,
-    x_in, cot_in, halo_in, triple_in, attended_in, stats_in, w_in_in, w_out_in, w_ex_in, w_sh_in,
+    x_in, cot_in, halo_in, triple_in, attended_in, scaled_in, stats_in, w_in_in, w_out_in, w_ex_in, w_sh_in,
     middle_out, middle_grad_out, hidden_out, triple_grad_out, mine, other,
     x, back, w_in, w_out, w_ex, w_sh, triple, attended, middle, middle_grad, upstream, hidden, triple_grad, stats,
     d_ex, d_sh, d_out, product, sums, small, scores, peaks, raised, scales, probs_grads, probs, scores_grads,
-    sems, tile_sems,
+    edge, sems, tile_sems,
 ):
     rows, width = x_in.shape
     total = x.shape[0]
@@ -376,7 +379,7 @@
     for copy in early:
         copy.wait()
     tail = pl.ds(rows, TILE)
-    project_rows(x[tail, :].astype(F32), gain1, shift1, w_in, b_in, triple, tail)
+    project_rows(x[tail, :].astype(F32), gain1, shift1, w_in, b_in, triple, tail, edge, slice(None))
     attend_groups(groups, table, triple, attended, stats, scores, peaks, raised, scales, alone=groups - 1)
     for copy in late:
         copy.wait()
@@ -444,6 +447,8 @@
         return 0
 
     lax.fori_loop(0, total // WIDE, before_feed, 0)
+    scaled_copy = move.start(scaled_in, x.at[own])
+    x[tail, :] = edge[...]
     leaving.append(move.start(middle, middle_out))
     lax.fori_loop(0, tiles, feed, 0)
     lax.fori_loop(0, total // WIDE, after_feed, 0)
@@ -451,13 +456,13 @@
         groups, table, triple, attended, upstream, stats, triple_grad, scores, peaks, probs_grads, probs, scores_grads,
     )
     leaving.append(move.start(triple_grad, triple_grad_out))
+    scaled_copy.wait()
     ones = jnp.ones((16, WIDE), BF16)
 
     def multiply(step, _):
         spot = wide_rows(step)
-        scaled, _inverse = normalize(x[spot, :].astype(F32))
         grad = triple_grad[spot, :]
-        product[...] += dot_tn(scaled.astype(BF16), grad)
+        product[...] += dot_tn(x[spot, :], grad)
         sums[...] += dot(ones, grad)
         return 0
 
@@ -478,37 +483,45 @@
     by_shift = jnp.broadcast_to(jnp.sum(by_shift, axis=1, keepdims=True), (width, LANES)).T
     small[6:7, :width] = by_gain[0:1]
     small[7:8, :width] = by_shift[0:1]
-    pack((d_ex, d_sh, d_out, product), small, place[2], mine, other)
+    pack((d_ex, d_out, product), d_sh, small, place[2], mine, other)
     for copy in leaving:
         copy.wait()
     pltpu.make_async_copy(hidden, hidden_out, tile_sems.at[0]).wait()
     pltpu.make_async_copy(middle_grad, middle_grad_out, tile_sems.at[1]).wait()
 
 
-def pack(grads, small, core, mine, other):
-    half = grads[0].shape[0] // 2
-    at = 0
-    for grad in grads:
-        for begin in range(0, grad.shape[1], LANES):
-            cols = slice(begin, begin + LANES)
-            mine[pl.ds(at, half), :] = grad[pl.ds(pl.multiple_of(core * half, half), half), cols].astype(BF16)
-            other[pl.ds(at, half), :] = grad[pl.ds(pl.multiple_of((1 - core) * half, half), half), cols].astype(BF16)
-            at += half
+def pack(grads, turned, small, core, mine, other):
+    def fill(half, target):
+        at = 0
+        for grad in grads:
+            count = grad.shape[0] // 2
+            rows = pl.ds(pl.multiple_of(half * count, count), count)
+            for begin in range(0, grad.shape[1], LANES):
+                target[pl.ds(at, count), :] = grad[rows, begin : begin + LANES].astype(BF16)
+                at += count
+        count, columns = turned.shape[0], turned.shape[1] // 2
+        for begin in range(0, columns, LANES):
+            cols = pl.ds(pl.multiple_of(half * columns + begin, LANES), LANES)
+            target[pl.ds(at, count), :] = turned[:, cols].astype(BF16)
+            at += count
+        return at
+
+    fill(core, mine)
+    at = fill(1 - core, other)
     rest = mine.shape[0] - at
     mine[pl.ds(at, rest), :] = jnp.zeros((rest, LANES), BF16)
     other[pl.ds(at, rest), :] = jnp.zeros((rest, LANES), BF16)
-    count = small.shape[1] // LANES
-    for index in range(count):
-        cols = slice(index * LANES, (index + 1) * LANES)
+    for index in range(small.shape[1] // LANES):
+        value = small[:, index * LANES : (index + 1) * LANES].astype(BF16)
         spot = pl.ds(at + (index // 2) * 16, 16)
 
         @pl.when(core == index % 2)
         def _():
-            mine[spot, :] = small[:, cols].astype(BF16)
+            mine[spot, :] = value
 
         @pl.when(core != index % 2)
         def _():
-            other[spot, :] = small[:, cols].astype(BF16)
+            other[spot, :] = value
 
 
 def step_copies(arrays, step, sems):
@@ -591,8 +604,30 @@
         copy.wait()
 
 
-def kernel_add(mine, other, out):
-    out[...] = (mine[...].astype(F32) + other[...].astype(F32)).astype(BF16)
+def kernel_add(mine_in, other_in, out, mine, other, sems):
+    chunks = sems.shape[0]
+    size = mine.shape[0] // chunks
+
+    def copies(chunk):
+        spot = pl.ds(chunk * size, size)
+        return [
+            pltpu.make_async_copy(mine_in.at[spot], mine.at[spot], sems.at[chunk, 0]),
+            pltpu.make_async_copy(other_in.at[spot], other.at[spot], sems.at[chunk, 1]),
+            pltpu.make_async_copy(mine.at[spot], out.at[spot], sems.at[chunk, 2]),
+        ]
+
+    for chunk in range(chunks):
+        for copy in copies(chunk)[:2]:
+            copy.start()
+    for chunk in range(chunks):
+        spot = pl.ds(chunk * size, size)
+        arriving = copies(chunk)
+        for copy in arriving[:2]:
+            copy.wait()
+        mine[spot, :] = (mine[spot, :].astype(F32) + other[spot, :].astype(F32)).astype(BF16)
+        arriving[2].start()
+    for chunk in range(chunks):
+        copies(chunk)[2].wait()
 
 
 def kernel_sum(extra, *refs):
@@ -615,47 +650,76 @@
     pltpu.make_async_copy(parts, out, sems.at[4]).wait()
 
 
-def halves_of(place, mine, other):
-    def both(at, count):
-        first, second = mine[pl.ds(at, count), :].astype(F32), other[pl.ds(at, count), :].astype(F32)
-        swap = place[2] == 1
-        return jnp.where(swap, second, first), jnp.where(swap, first, second)
-
-    return both
-
-
-def unpack(both, at, out):
-    for begin in range(0, out.shape[1], LANES):
-        low, high = both(at, 192)
-        out[:192, begin : begin + LANES] = low
-        out[192:, begin : begin + LANES] = high
-        at += 192
-    return at
-
-
-def small_blocks(both, at, columns):
+def kernel_unpack_half(where, packed_in, d_ex, d_out, d_in, d_sh, packed, ex, out, inward, sh, sems):
+    arrays = ((ex, d_ex), (out, d_out), (inward, d_in), (sh, d_sh))
+    sizes = [value.shape[0] * value.shape[1] // LANES for value, _target in arrays]
+    begins = [sum(sizes[:index]) for index in range(4)]
+    arriving = []
+    for index in range(4):
+        spot = pl.ds(begins[index], sizes[index])
+        arriving.append(pltpu.make_async_copy(packed_in.at[spot], packed.at[spot], sems.at[index]))
+        arriving[-1].start()
+    half = where[0]
+    leaving = []
+    for index, (value, target) in enumerate(arrays):
+        arriving[index].wait()
+        at = begins[index]
+        if index < 3:
+            count = value.shape[0]
+            for begin in range(0, value.shape[1], LANES):
+                value[:, begin : begin + LANES] = packed[pl.ds(at, count), :].astype(F32)
+                at += count
+        else:
+            count = value.shape[1]
+            for begin in range(0, value.shape[0], LANES):
+                value[begin : begin + LANES, :] = packed[pl.ds(at, count), :].astype(F32).T
+                at += count
+        rows = pl.ds(pl.multiple_of(half * value.shape[0], value.shape[0]), value.shape[0])
+        leaving.append(pltpu.make_async_copy(value, target.at[rows], sems.at[4 + index]))
+        leaving[-1].start()
+    return leaving
+
+
+def kernel_first_half(where, packed_in, *refs):
+    for copy in kernel_unpack_half(where, packed_in, *refs):
+        copy.wait()
+
+
+def kernel_second_half(
+    where, packed_in, first_in, kept_ex, kept_out, kept_in, kept_sh,
+    d_ex, d_out, d_in, d_sh, b_in, b_sh, gain2, shift2, b_out, b_ex, gain1, shift1,
+    packed, ex, out, inward, sh, sems, mine, other, small_sems,
+):
+    del kept_ex, kept_out, kept_in, kept_sh
+    rows = pl.ds(first_in.shape[0] - mine.shape[0], mine.shape[0])
+    copies = [
+        pltpu.make_async_copy(first_in.at[rows], mine, small_sems.at[0]),
+        pltpu.make_async_copy(packed_in.at[rows], other, small_sems.at[1]),
+    ]
+    for copy in copies:
+        copy.start()
+    leaving = kernel_unpack_half(where, packed_in, d_ex, d_out, d_in, d_sh, packed, ex, out, inward, sh, sems)
+    for copy in copies:
+        copy.wait()
+    width, columns = b_sh.shape[0], b_ex.shape[0]
+    swap = where[0] == 0
     blocks = []
     for index in range(columns // LANES):
-        blocks.append(both(at + index // 2 * 16, 16)[index % 2])
-    return jnp.concatenate(blocks, axis=1)
-
-
-def kernel_unpack(
-    place, mine, other, d_ex, d_sh, d_out, d_in, b_in, b_sh, gain2, shift2, b_out, b_ex, gain1, shift1
-):
-    both = halves_of(place, mine, other)
-    width = d_out.shape[0]
-    at = unpack(both, 0, d_ex)
-    for begin in range(0, d_sh.shape[0], LANES):
-        low, high = both(at, 192)
-        d_sh[begin : begin + LANES, :] = jnp.concatenate([low, high], axis=0).T
-        at += 192
-    small = small_blocks(both, unpack(both, unpack(both, at, d_out), d_in), d_ex.shape[1])
+        spot = pl.ds(index // 2 * 16, 16)
+        pair = mine[spot, :].astype(F32), other[spot, :].astype(F32)
+        blocks.append(jnp.where(swap, pair[1 - index % 2], pair[index % 2]))
+    small = jnp.concatenate(blocks, axis=1)
     for row, ref in ((0, b_sh), (1, gain2), (2, shift2), (3, b_out), (6, gain1), (7, shift1)):
         ref[...] = small[row, :width]
     b_ex[...] = small[4]
     b_in[0:1, :] = small[5:6, :width]
     b_in[1:2, :] = small[5:6, 2 * width : 3 * width]
+    for copy in leaving:
+        copy.wait()
+
+
+def kernel_touch(*refs):
+    del refs
 
 
 VMEM = pl.BlockSpec(memory_space=pltpu.VMEM)
@@ -698,11 +762,12 @@
         out_shape=(
             shape((rows, 3 * width), BF16),
             shape((total, width), BF16),
+            shape((rows, width), BF16),
             shape((GROUPS, 8, WIN), F32),
             shape((GROUPS + 1, 8), jnp.int32),
         ),
         in_specs=[SMEM] + [VMEM] * 4 + [ANY] * 2,
-        out_specs=(ANY, ANY, VMEM, SMEM),
+        out_specs=(ANY, ANY, ANY, VMEM, SMEM),
         scratch_shapes=[
             vmem((rows, width), BF16),
             vmem(w_in.shape, BF16),
@@ -714,13 +779,13 @@
             pltpu.SemaphoreType.DMA((8,)),
             pltpu.SemaphoreType.DMA((rows // OWN,)),
         ],
-        compiler_params=params(58),
+        compiler_params=params(63),
         cost_estimate=cost(2 * 6 * rows * width * 3 * width, 1e7),
         name="own_part",
     )(place, segments, gain1, shift1, b_in, x, w_in)
 
 
-def rest_part(place, table, vectors, x, cot, halo, triple, attended, stats, w_in, w_out, w_ex, w_sh, pieces):
+def rest_part(place, table, vectors, x, cot, halo, triple, attended, scaled, stats, w_in, w_out, w_ex, w_sh, pieces):
     rows, width = x.shape
     total = rows + TILE
     hidden = w_ex.shape[1]
@@ -739,7 +804,7 @@
             shape((packed, LANES), BF16),
             shape((packed, LANES), BF16),
         ),
-        in_specs=[SMEM, SMEM] + [VMEM] * 7 + [ANY] * 10,
+        in_specs=[SMEM, SMEM] + [VMEM] * 7 + [ANY] * 11,
         out_specs=tuple([ANY] * 4 + [VMEM] * 2),
         scratch_shapes=[
             vmem((total, width), BF16),
@@ -769,13 +834,14 @@
             [square] * 2,
             [low] * 2,
             [low] * 2,
+            vmem((TILE, width), BF16),
             pltpu.SemaphoreType.DMA((16,)),
             pltpu.SemaphoreType.DMA((2,)),
         ],
         compiler_params=params(62),
         cost_estimate=cost(2 * 9 * rows * width * (3 * width + 8 * width), 3e7),
         name="rest_part",
-    )(place, table, *vectors, x, cot, halo, triple, attended, stats, w_in, w_out, w_ex, w_sh)
+    )(place, table, *vectors, x, cot, halo, triple, attended, scaled, stats, w_in, w_out, w_ex, w_sh)
 
 
 def input_gradient(after, gain1, x, halo, w_in, triple_grad, middle_grad):
@@ -795,7 +861,7 @@
             pltpu.SemaphoreType.DMA((4,)),
             pltpu.SemaphoreType.DMA((total // WIDE, 8)),
         ],
-        compiler_params=params(58),
+        compiler_params=params(63),
         cost_estimate=cost(2 * rows * width * 9 * width, 1.4e7),
         name="input_gradient",
     )(after, gain1, x, halo, w_in, triple_grad, middle_grad)
@@ -817,7 +883,7 @@
             pltpu.SemaphoreType.DMA((2,)),
             pltpu.SemaphoreType.DMA((total // WIDE, 8)),
         ],
-        compiler_params=params(58),
+        compiler_params=params(63),
         cost_estimate=cost(2 * total * width * 8 * width, 1.3e7),
         name="layer_result",
     )(after, table, b_sh, middle, hidden, w_sh)
@@ -827,9 +893,12 @@
     return pl.pallas_call(
         kernel_add,
         out_shape=shape(mine.shape, BF16),
-        in_specs=[VMEM, VMEM],
-        out_specs=VMEM,
-        compiler_params=params(58),
+        in_specs=[ANY, ANY],
+        out_specs=ANY,
+        scratch_shapes=[
+            pltpu.VMEM(mine.shape, BF16), pltpu.VMEM(mine.shape, BF16), pltpu.SemaphoreType.DMA((4, 3)),
+        ],
+        compiler_params=params(63),
         cost_estimate=cost(mine.size, mine.size * 6),
         name="add_halves",
     )(mine, other)
@@ -846,22 +915,61 @@
             pltpu.VMEM(parts.shape[1:], BF16),
             pltpu.SemaphoreType.DMA((5,)),
         ],
-        compiler_params=params(58),
+        compiler_params=params(63),
         cost_estimate=cost(parts.size, parts.size * 4),
         name="sum_parts",
     )(*after, parts)
 
 
-def unpack_call(kernel, name, place, mine, other, shapes):
+def half_shapes(width, hidden):
+    dims = ((width, hidden), (width, width), (width, 3 * width), (hidden, width))
+    scratch = [pltpu.VMEM((rows // 2, columns), F32) for rows, columns in dims]
+    return tuple(shape(dim, F32) for dim in dims), [*scratch, pltpu.SemaphoreType.DMA((8,))]
+
+
+def unpack_first(half, packed, width, hidden):
+    shapes, scratch = half_shapes(width, hidden)
     return pl.pallas_call(
-        kernel,
-        out_shape=tuple(shape(dims, F32) for dims in shapes),
-        in_specs=[SMEM, VMEM, VMEM],
-        out_specs=tuple([VMEM] * len(shapes)),
-        compiler_params=params(58),
-        cost_estimate=cost(mine.size, mine.size * 12),
-        name=name,
-    )(place, mine, other)
+        kernel_first_half,
+        out_shape=shapes,
+        in_specs=[SMEM, ANY],
+        out_specs=(ANY,) * 4,
+        scratch_shapes=[pltpu.VMEM(packed.shape, BF16), *scratch],
+        compiler_params=params(63),
+        cost_estimate=cost(packed.size, packed.size * 6),
+        name="unpack_first",
+    )(half, packed)
+
+
+def unpack_second(half, packed, first, kept, used, width, hidden):
+    shapes, scratch = half_shapes(width, hidden)
+    rows = first.shape[0] - used
+    small = tuple(shape(dims, F32) for dims in ((2, width),) + ((width,),) * 4 + ((hidden,), (width,), (width,)))
+    return pl.pallas_call(
+        kernel_second_half,
+        out_shape=shapes + small,
+        in_specs=[SMEM] + [ANY] * 6,
+        out_specs=(ANY,) * 4 + (VMEM,) * 8,
+        scratch_shapes=[
+            pltpu.VMEM(packed.shape, BF16), *scratch, pltpu.VMEM((rows, LANES), BF16), pltpu.VMEM((rows, LANES), BF16),
+            pltpu.SemaphoreType.DMA((2,)),
+        ],
+        input_output_aliases={3: 0, 4: 1, 5: 2, 6: 3},
+        compiler_params=params(63),
+        cost_estimate=cost(packed.size, packed.size * 6),
+        name="unpack_second",
+    )(half, packed, first, *kept)
+
+
+def touch(value, *after):
+    return pl.pallas_call(
+        kernel_touch,
+        out_shape=shape(value.shape, value.dtype),
+        in_specs=[ANY] * (1 + len(after)),
+        out_specs=ANY,
+        input_output_aliases={0: 0},
+        name="touch",
+    )(value, *after)
 
 
 def same_core_groups():
@@ -903,26 +1011,28 @@
         first_gain, first_shift, outward_bias, second_gain, second_shift, expand_bias, shrink_bias
     )
     halo = passed(jnp.concatenate([layer_input[:HALO], cotangent[:HALO]], axis=1), -1)
-    triple, attended, stats, table = own_part(
+    triple, attended, scaled, stats, table = own_part(
         place, segments, gain1, shift1, inward_bias, layer_input, inward_weight
     )
     middle, middle_grad, hidden, triple_grad, mine, other = rest_part(
         place, table, (gain1, shift1, inward_bias, b_out, gain2, shift2, b_ex), layer_input, cotangent, halo, triple,
-        attended, stats, inward_weight, outward_weight, expand_weight, shrink_weight, pieces,
+        attended, scaled, stats, inward_weight, outward_weight, expand_weight, shrink_weight, pieces,
     )
     both = add_halves(mine, swap_cores(other))
     parts = exchange(both.reshape(pieces, -1, LANES))
     input_grad, input_halo = input_gradient(both, gain1, layer_input, halo, inward_weight, triple_grad, middle_grad)
     result, result_halo = layer_result(input_halo, table, b_sh, middle, hidden, shrink_weight)
+    summed = sum_parts((input_halo, result_halo), parts)
+    mine = exchange(summed).reshape(-1, LANES)
     first = table[GROUPS, 1]
-    input_grad = take_over(input_grad, passed(input_halo[:HALO], 1), first)
-    result = take_over(result, passed(result_halo[:HALO], 1), first)
-    mine = exchange(sum_parts((input_grad, result), parts)).reshape(-1, LANES)
-    square, row = (width, width), (width,)
-    d_ex, d_sh, d_out, d_in, d_b_in, d_b_sh, d_gain2, d_shift2, d_b_out, d_b_ex, d_gain1, d_shift1 = unpack_call(
-        kernel_unpack, "unpack", place, mine, swap_cores(mine),
-        ((width, hidden_width), (hidden_width, width), square, (width, 3 * width), (2, width)) + (row,) * 4
-        + ((hidden_width,), row, row),
+    input_grad = take_over(input_grad, passed(touch(input_halo, summed)[:HALO], 1), first)
+    result = take_over(result, passed(touch(result_halo, summed)[:HALO], 1), first)
+    mine = touch(mine, input_grad, result)
+    other = swap_cores(mine)
+    used = 192 * (2 * hidden_width + 4 * width) // LANES
+    half = unpack_first(place[2:], mine, width, hidden_width)
+    d_ex, d_out, d_in, d_sh, d_b_in, d_b_sh, d_gain2, d_shift2, d_b_out, d_b_ex, d_gain1, d_shift1 = unpack_second(
+        1 - place[2:], other, mine, half, used, width, hidden_width
     )
     return (
         result, input_grad, d_gain1, d_shift1, d_in, d_b_in, d_out, d_b_out, d_gain2, d_shift2, d_ex, d_b_ex, d_sh,

time: 198 us -> 183 us (0.924)
  blocking collectives: 35.7 us -> 0 us
  waiting for transfers between devices: 10.5 us -> 27.5 us
  starting transfers between devices: 26.9 us -> 34.1 us
    all_to_all x1 -> x0, blocking collectives: 35.7 us -> none  [exchange(): lax.all_to_all(parts, ('dp', 'mp'), 0, 0, axis_index_groups=same_core_gro...]
    all_to_all x1 -> x2, starting transfers between devices: 10.6 us -> 24.1 us  [exchange(): lax.all_to_all(parts, ('dp', 'mp'), 0, 0, axis_index_groups=same_core_gro...]
    ppermute x3, waiting for transfers between devices: 3.42 us -> 16.8 us  [passed(): return lax.ppermute(block, 'mp', route)]
    ppermute x2, starting transfers between devices: 9.27 us -> 2.66 us  [swap_cores(): return lax.ppermute(block, 'dp', [(i, i ^ 1) for i in range(packs)])]
    all_to_all x1 -> x2, waiting for transfers between devices: 0.01 us -> 6.29 us  [exchange(): lax.all_to_all(parts, ('dp', 'mp'), 0, 0, axis_index_groups=same_core_gro...]
    ppermute x2, waiting for transfers between devices: 7.03 us -> 4.45 us  [swap_cores(): return lax.ppermute(block, 'dp', [(i, i ^ 1) for i in range(packs)])]
    unnamed x12 -> x4, local copies, waits for them, and re-layouts: 4.41 us -> 1.97 us
    pallas_call x2 -> x6, Pallas kernels: 9.19 us -> 9.71 us  [the longest x1 3.67 us: unpack_second(): pl.pallas_call(kernel_second_half, out_shape=shapes + small, in_specs=[SM...]
  transfers between devices with their start and end apart: 6 -> 7, of which waited for: 3 -> 5; matrix products, arithmetic and copies ran while one was open for 4% -> 4% of each run, Pallas kernels for 20% -> 23%
where the time goes in v3:
time: 183 us
  Pallas kernels  109 us (60%)
  starting transfers between devices  34.1 us (19%)
  waiting for transfers between devices  27.5 us (15%)
  local copies, waits for them, and re-layouts  7.02 us (4%)
  other arithmetic  4.77 us (3%)
    pallas_call x1, Pallas kernels, rest_part(): pl.pallas_call(kernel_rest, out_shape=(shape((total, width), F32), shape(...  57.6 us
    all_to_all x2, starting transfers between devices, exchange(): lax.all_to_all(parts, ('dp', 'mp'), 0, 0, axis_index_groups=same_core_gro...  24.1 us
    pallas_call x1, Pallas kernels, own_part(): pl.pallas_call(kernel_own, out_shape=(shape((rows, 3 * width), BF16), sha...  19.4 us
    ppermute x3, waiting for transfers between devices, passed(): return lax.ppermute(block, 'mp', route)  16.8 us
    pallas_call x1, Pallas kernels, layer_result(): pl.pallas_call(kernel_result, out_shape=(shape((total - TILE, width), BF1...  9.91 us
    pallas_call x1, Pallas kernels, input_gradient(): pl.pallas_call(kernel_input, out_shape=(shape((rows, width), F32), shape(...  9.7 us
    ppermute x3, starting transfers between devices, passed(): return lax.ppermute(block, 'mp', route)  7.32 us
    all_to_all x2, waiting for transfers between devices, exchange(): lax.all_to_all(parts, ('dp', 'mp'), 0, 0, axis_index_groups=same_core_gro...  6.29 us
  transfers between devices with their start and end apart: 7, of which 5 were waited for; matrix products, arithmetic and copies ran while one was open for 4% of the time, Pallas kernels for 23%

profile of v3, /device:TPU:1, one launch (start us, length us, event | category | flops | bytes accessed | tf_op | source)
XLA Modules:
  0.0 183.5 jit_solution(13872776542892892918)
XLA Ops:
  0.6 0.9 slice.21
  2.6 1.3 collective-permute-start
  4.5 19.4 %own_part.1 = (bf16[2048,1152]{1,0:T(8,128)(2,1)}, bf16[2304,384]{1,0:T(8,128)(2,1)}, bf16[2048,384]{1,0:T(8,128)(2,1)}, f32[24,8,256]{2,1,0:T(8,128)}, s32[25,8]{1,0:T(8,128)}) custom-call(s32[3]{0:T(128)} %pad_add_fusion.place, s32[1,8192]{1,0:T(1,128)} %seg.1, f32[384]{0:T(512)} %gain1.5, f32[384]{0:T(512)} %shift1.3, f32[2,384]{1,0:T(2,128)} %b_in.3, ...), custom_call_target="tpu_custom_call" | custom-call | flops 10871635968 | bytes 10000000 | tf_op jit(solution)/shard_map/own_part/pallas_call | solution.py:760
  24.5 57.6 %rest_part.1 = (f32[2304,384]{1,0:T(8,128)}, f32[2304,384]{1,0:T(8,128)}, bf16[2304,1536]{1,0:T(8,128)(2,1)}, bf16[2304,1152]{1,0:T(8,128)(2,1)}, bf16[7168,128]{1,0:T(8,128)(2,1)}, /*index=5*/bf16[7168,128]{1,0:T(8,128)(2,1)}) custom-call(s32[3]{0:T(128)} %pad_add_fusion.place, s32[25,8]{1,0:T(8,128)} %get-tuple-element.45.table, f32[384]{0:T(512)} %gain1.5, ...), custom_call_target="tpu_custom_call" | custom-call | flops 59793997824 | bytes 30000000 | tf_op jit(solution)/shard_map/rest_part/pallas_call | solution.py:797
  82.7 3.8 %collective-permute-done.1.other_in = bf16[7168,128]{1,0:T(8,128)(2,1)} collective-permute-done((bf16[7168,128]{1,0:T(8,128)(2,1)}, bf16[7168,128]{1,0:T(8,128)(2,1)}, u32[]{:S(2)}, u32[]{:S(2)}) %collective-permute-start.1) | collective-permute-done | bytes 1835040 | tf_op jit(solution)/shard_map/ppermute | solution.py:982
  86.5 3.0 %add_halves.1.after = bf16[7168,128]{1,0:T(8,128)(2,1)} custom-call(bf16[7168,128]{1,0:T(8,128)(2,1)} %get-tuple-element.50.mine_in, bf16[7168,128]{1,0:T(8,128)(2,1)} %collective-permute-done.1.other_in), custom_call_target="tpu_custom_call" | custom-call | flops 917504 | bytes 5505024 | tf_op jit(solution)/shard_map/add_halves/pallas_call | solution.py:893
  89.4 18.6 %all-to-all-start = ((bf16[64,112,128]{2,1,0:T(8,128)(2,1)}), bf16[64,112,128]{2,1,0:T(8,128)(2,1)}, u32[]{:S(2)}, u32[]{:S(2)}) async-start(bf16[64,112,128]{2,1,0:T(8,128)(2,1)} %bitcast.6), calls=%async_computation | async-start | bytes 3670016 | tf_op jit(solution)/shard_map/all_to_all | solution.py:986
  108.1 9.7 %input_gradient.1 = (f32[2048,384]{1,0:T(8,128)}, f32[256,384]{1,0:T(8,128)}) custom-call(bf16[7168,128]{1,0:T(8,128)(2,1)} %add_halves.1.after, f32[384]{0:T(512)} %gain1.5, bf16[2048,384]{1,0:T(8,128)(2,1)} %x_in.5, bf16[208,768]{1,0:T(8,128)(2,1)} %copy-done.1, bf16[384,1152]{1,0:T(8,128)(2,1)} %w_in_in.5, ...), custom_call_target="tpu_custom_call" | custom-call | flops 5435817984 | bytes 14000000 | tf_op jit(solution)/shard_map/input_gradient/pallas_call | solution.py:851
  117.8 9.9 %layer_result.1 = (bf16[2048,384]{1,0:T(8,128)(2,1)}, bf16[256,384]{1,0:T(8,128)(2,1)}) custom-call(f32[256,384]{1,0:T(8,128)} %get-tuple-element.54.after.refs_0_, s32[25,8]{1,0:T(8,128)} %get-tuple-element.45.table, f32[384]{0:T(512)} %b_sh.1, f32[2304,384]{1,0:T(8,128)} %get-tuple-element.55.middle_in, bf16[2304,1536]{1,0:T(8,128)(2,1)} %get-tuple-element.56.hidden_in, ...), custom_call_target="tpu_custom_call" | custom-call | flops 5435817984 | bytes 13000000 | tf_op jit(solution)/shard_map/layer_result/pallas_call | solution.py:873
  127.7 6.3 %all-to-all-done.refs_2_ = bf16[64,112,128]{2,1,0:T(8,128)(2,1)} async-done(((bf16[64,112,128]{2,1,0:T(8,128)(2,1)}), bf16[64,112,128]{2,1,0:T(8,128)(2,1)}, u32[]{:S(2)}, u32[]{:S(2)}) %all-to-all-start) | async-done | bytes 1835040 | tf_op jit(solution)/shard_map/all_to_all | solution.py:986
  134.0 2.7 %sum_parts.1.refs_1_ = bf16[64,112,128]{2,1,0:T(8,128)(2,1)} custom-call(f32[256,384]{1,0:T(8,128)} %get-tuple-element.54.after.refs_0_, bf16[256,384]{1,0:T(8,128)(2,1)} %get-tuple-element.58.refs_1_.refs_0_, bf16[64,112,128]{2,1,0:T(8,128)(2,1)} %all-to-all-done.refs_2_), custom_call_target="tpu_custom_call" | custom-call | flops 917504 | bytes 3670016 | tf_op jit(solution)/shard_map/sum_parts/pallas_call | solution.py:908
  136.7 5.5 %all-to-all-start.1 = ((bf16[64,112,128]{2,1,0:T(8,128)(2,1)}), bf16[64,112,128]{2,1,0:T(8,128)(2,1)S(1)}, u32[]{:S(2)}, u32[]{:S(2)}) async-start(bf16[64,112,128]{2,1,0:T(8,128)(2,1)} %sum_parts.1.refs_1_), calls=%async_computation.1 | async-start | bytes 3670016 | tf_op jit(solution)/shard_map/all_to_all | solution.py:986
  143.2 2.9 %collective-permute-start.2 = (bf16[208,384]{1,0:T(8,128)(2,1)S(1)}, bf16[208,384]{1,0:T(8,128)(2,1)S(1)}, u32[]{:S(2)}, u32[]{:S(2)}) collective-permute-start(bf16[208,384]{1,0:T(8,128)(2,1)S(1)} %slice.28), channel_id=1, source_target_pairs={{0,1},{1,2},{2,3},{4,5},{5,6},{6,7},{8,9},{9,10},{10,11},{12,13},{... | collective-permute-start | bytes 479240 | tf_op jit(solution)/shard_map/ppermute | solution.py:992
  146.1 1.3 slice.23
  147.3 1.0 slice.29
  148.3 3.1 %collective-permute-start.3 = (f32[208,384]{1,0:T(8,128)S(1)}, f32[208,384]{1,0:T(8,128)S(1)}, u32[]{:S(2)}, u32[]{:S(2)}) collective-permute-start(f32[208,384]{1,0:T(8,128)S(1)} %slice.29), channel_id=1, source_target_pairs={{0,1},{1,2},{2,3},{4,5},{5,6},{6,7},{8,9},{9,10},{10,11},{12,13},{... | collective-permute-start | bytes 958472 | tf_op jit(solution)/shard_map/ppermute | solution.py:992
  152.1 11.7 %collective-permute-done.2 = bf16[208,384]{1,0:T(8,128)(2,1)S(1)} collective-permute-done((bf16[208,384]{1,0:T(8,128)(2,1)S(1)}, bf16[208,384]{1,0:T(8,128)(2,1)S(1)}, u32[]{:S(2)}, u32[]{:S(2)}) %collective-permute-start.2) | collective-permute-done | bytes 159776 | tf_op jit(solution)/shard_map/ppermute | solution.py:992
  163.8 1.7 select_dynamic-update-slice_fusion.1.refs_2_
  165.5 5.1 %collective-permute-done.3 = f32[208,384]{1,0:T(8,128)S(1)} collective-permute-done((f32[208,384]{1,0:T(8,128)S(1)}, f32[208,384]{1,0:T(8,128)S(1)}, u32[]{:S(2)}, u32[]{:S(2)}) %collective-permute-start.3) | collective-permute-done | bytes 319520 | tf_op jit(solution)/shard_map/ppermute | solution.py:992
  170.6 1.8 select_dynamic-update-slice_fusion.refs_1_
  172.4 1.3 copy-done
  173.7 2.1 %collective-permute-start.4 = (bf16[7168,128]{1,0:T(8,128)(2,1)}, bf16[7168,128]{1,0:T(8,128)(2,1)}, u32[]{:S(2)}, u32[]{:S(2)}) collective-permute-start(bf16[7168,128]{1,0:T(8,128)(2,1)} %touch.5.packed_in.first_in), channel_id=1, source_target_pairs={{0,4},{4,0},{8,12},{12,8},{16,20},{20,16},{24,28},{28,24},{32,36},... | collective-permute-start | bytes 5505032 | tf_op jit(solution)/shard_map/ppermute | solution.py:982
  175.8 3.1 %unpack_first.1 = (f32[384,1536]{1,0:T(8,128)}, f32[384,384]{1,0:T(8,128)}, f32[384,1152]{1,0:T(8,128)}, f32[1536,384]{1,0:T(8,128)}) custom-call(s32[1]{0:T(128)} %bitcast.1.where, bf16[7168,128]{1,0:T(8,128)(2,1)} %touch.5.packed_in.first_in), custom_call_target="tpu_custom_call" | custom-call | flops 917504 | bytes 5505024 | tf_op jit(solution)/shard_map/unpack_first/pallas_call | solution.py:932
  179.6 3.7 %unpack_second.1 = (f32[384,1536]{1,0:T(8,128)}, f32[384,384]{1,0:T(8,128)}, f32[384,1152]{1,0:T(8,128)}, f32[1536,384]{1,0:T(8,128)}, f32[2,384]{1,0:T(2,128)},...) custom-call(s32[1]{0:T(128)S(6)} %sub.3.where, ...), custom_call_target="tpu_custom_call", output_to_operand_aliasing={{0}: (3, {}), {1}: (4, {}), {2}: (5, {}), {3}: (6, {})} | custom-call | flops 917504 | bytes 5505024 | tf_op jit(solution)/shard_map/unpack_second/pallas_call | solution.py:948
  (15 shorter events, 5.1 us)
Async XLA Ops:
  2.6 21.3 %collective-permute-start = (bf16[208,768]{1,0:T(8,128)(2,1)S(1)}, bf16[208,768]{1,0:T(8,128)(2,1)S(1)}, u32[]{:S(2)}, u32[]{:S(2)}) collective-permute-start(bf16[208,768]{1,0:T(8,128)(2,1)S(1)} %pad_maximum_fusion), channel_id=1, source_target_pairs={{1,0},{2,1},{3,2},{5,4},{6,5},{7,6},{9,8},{10,9},{11,10},{13,12},{... | collective-permute-start | bytes 958472 | tf_op jit(solution)/shard_map/ppermute | solution.py:992
  23.8 0.7 copy-start.1
  82.2 4.3 %collective-permute-start.1 = (bf16[7168,128]{1,0:T(8,128)(2,1)}, bf16[7168,128]{1,0:T(8,128)(2,1)}, u32[]{:S(2)}, u32[]{:S(2)}) collective-permute-start(bf16[7168,128]{1,0:T(8,128)(2,1)} %get-tuple-element.51), channel_id=1, source_target_pairs={{0,4},{4,0},{8,12},{12,8},{16,20},{20,16},{24,28},{28,24},{32,36},... | collective-permute-start | bytes 5505032 | tf_op jit(solution)/shard_map/ppermute | solution.py:982
  89.4 44.6 %all-to-all-start = ((bf16[64,112,128]{2,1,0:T(8,128)(2,1)}), bf16[64,112,128]{2,1,0:T(8,128)(2,1)}, u32[]{:S(2)}, u32[]{:S(2)}) async-start(bf16[64,112,128]{2,1,0:T(8,128)(2,1)} %bitcast.6), calls=%async_computation | async-start | bytes 3670016 | tf_op jit(solution)/shard_map/all_to_all | solution.py:986
  136.7 35.7 %all-to-all-start.1 = ((bf16[64,112,128]{2,1,0:T(8,128)(2,1)}), bf16[64,112,128]{2,1,0:T(8,128)(2,1)S(1)}, u32[]{:S(2)}, u32[]{:S(2)}) async-start(bf16[64,112,128]{2,1,0:T(8,128)(2,1)} %sum_parts.1.refs_1_), calls=%async_computation.1 | async-start | bytes 3670016 | tf_op jit(solution)/shard_map/all_to_all | solution.py:986
  143.2 20.6 %collective-permute-start.2 = (bf16[208,384]{1,0:T(8,128)(2,1)S(1)}, bf16[208,384]{1,0:T(8,128)(2,1)S(1)}, u32[]{:S(2)}, u32[]{:S(2)}) collective-permute-start(bf16[208,384]{1,0:T(8,128)(2,1)S(1)} %slice.28), channel_id=1, source_target_pairs={{0,1},{1,2},{2,3},{4,5},{5,6},{6,7},{8,9},{9,10},{10,11},{12,13},{... | collective-permute-start | bytes 479240 | tf_op jit(solution)/shard_map/ppermute | solution.py:992
  148.3 22.3 %collective-permute-start.3 = (f32[208,384]{1,0:T(8,128)S(1)}, f32[208,384]{1,0:T(8,128)S(1)}, u32[]{:S(2)}, u32[]{:S(2)}) collective-permute-start(f32[208,384]{1,0:T(8,128)S(1)} %slice.29), channel_id=1, source_target_pairs={{0,1},{1,2},{2,3},{4,5},{5,6},{6,7},{8,9},{9,10},{10,11},{12,13},{... | collective-permute-start | bytes 958472 | tf_op jit(solution)/shard_map/ppermute | solution.py:992
  172.4 1.3 copy-start
  173.7 5.9 %collective-permute-start.4 = (bf16[7168,128]{1,0:T(8,128)(2,1)}, bf16[7168,128]{1,0:T(8,128)(2,1)}, u32[]{:S(2)}, u32[]{:S(2)}) collective-permute-start(bf16[7168,128]{1,0:T(8,128)(2,1)} %touch.5.packed_in.first_in), channel_id=1, source_target_pairs={{0,4},{4,0},{8,12},{12,8},{16,20},{20,16},{24,28},{28,24},{32,36},... | collective-permute-start | bytes 5505032 | tf_op jit(solution)/shard_map/ppermute | solution.py:982

commit v4 on v3

--- a/solution.py
+++ b/solution.py
@@ -11,11 +11,12 @@
 SEQ = 198
 EPSILON = 1e-06
 MASKED = -1000000000.0
+LOG2E = 1.4426950408889634
 WIN = 256
 TILE = 256
 HALO = 208
 WIDE = 768
-OWN = 512
+OWN = 1024
 GROUPS = 24
 LANES = 128
 CHUNK = 256
@@ -130,6 +131,21 @@
     )
 
 
+def group_mask_factors(table, group):
+    bounds = [table[group, i] for i in range(1, 5)]
+
+    def ident(index):
+        return sum((index >= b).astype(jnp.int32) for b in bounds)
+
+    row = ident(lax.broadcasted_iota(jnp.int32, (WIN, LANES), 0))
+    left = jnp.where(row == lax.broadcasted_iota(jnp.int32, (WIN, LANES), 1), 1.0, 0.0).astype(BF16)
+    col = ident(lax.broadcasted_iota(jnp.int32, (1, WIN), 1))
+    kind = lax.broadcasted_iota(jnp.int32, (16, WIN), 0)
+    right = jnp.where(kind == col, 0.0, MASKED).astype(BF16)
+    right = jnp.concatenate([right, jnp.zeros((LANES - 16, WIN), BF16)], axis=0)
+    return left, jnp.concatenate([right, right], axis=1)
+
+
 def head_masks():
     lane = lax.broadcasted_iota(jnp.int32, (WIN, 2 * HD), 1)
     return lane < HD, lane >= HD
@@ -184,24 +200,25 @@
 
     def first(group, slot):
         rows = group_rows(table, group, shifted)
-        bias = group_bias(table, group)
-        bias = jnp.concatenate([bias, bias], axis=1)
+        left, right = group_mask_factors(table, group)
         for pair in pairs:
             query_t = triple[rows, pl.ds(pair * 2 * HD, 2 * HD)].T
             key = triple[rows, pl.ds(width + pair * 2 * HD, 2 * HD)]
-            value = dot(key, block_diagonal(query_t)) + bias
+            value = dot(
+                jnp.concatenate([key, left], axis=1), jnp.concatenate([block_diagonal(query_t), right], axis=0)
+            )
             scores[slot][pair] = value
             peaks[slot][pair : pair + 1, :] = jnp.max(value, axis=0, keepdims=True)
 
     def second(group, slot):
         for pair in pairs:
             peak = peaks[slot][pair : pair + 1, :]
-            value = jnp.exp(scores[slot][pair] - peak)
+            value = jnp.exp2(scores[slot][pair] - peak)
             total = jnp.sum(value, axis=0, keepdims=True)
             raised[slot][pair, :WIN] = value[:, :WIN].astype(BF16)
             raised[slot][pair, WIN:] = value[:, WIN:].astype(BF16)
             scales[slot][pair : pair + 1, :] = 1.0 / total
-            lse = peak + jnp.log(total)
+            lse = peak + LOG2E * jnp.log(total)
             stats[group, pl.ds(2 * pair, 1), :] = lse[:, :WIN]
             stats[group, pl.ds(2 * pair + 1, 1), :] = lse[:, WIN:]
 
@@ -221,9 +238,7 @@
             part(alone, 0)
 
 
-def attend_back_groups(
-    groups, table, triple, attended, upstream, stats, triple_grad, scores, agreements, probs_grads, probs, scores_grads,
-):
+def attend_back_groups(groups, table, triple, attended, upstream, stats, triple_grad, probs, scores_grads):
     width = attended.shape[1]
     pairs = range(width // (2 * HD))
     masks = head_masks()
@@ -240,26 +255,22 @@
                 [stats[group, pl.ds(2 * pair, 1), :], stats[group, pl.ds(2 * pair + 1, 1), :]], axis=1
             )
             query_t = triple[rows, columns(pair, 0)].T
-            scores[slot][pair] = dot(triple[rows, columns(pair, 1)], block_diagonal(query_t)) + bias - lse
             up_t = upstream[rows, columns(pair, 0)].T
-            probs_grads[slot][pair] = dot(triple[rows, columns(pair, 2)], block_diagonal(up_t))
             product = attended[rows, columns(pair, 0)].T.astype(F32) * up_t.astype(F32)
-            agreements[slot][pair : pair + 1, :] = jnp.concatenate(
+            agreement = jnp.concatenate(
                 [jnp.sum(product[:HD], axis=0, keepdims=True), jnp.sum(product[HD:], axis=0, keepdims=True)], axis=1
             )
-
-    def second(group, slot):
-        for pair in pairs:
-            prob = jnp.exp(scores[slot][pair])
+            scores = dot(triple[rows, columns(pair, 1)], block_diagonal(query_t))
+            probs_grad = dot(triple[rows, columns(pair, 2)], block_diagonal(up_t))
+            prob = jnp.exp2(scores + bias - lse)
             probs[slot][pair] = prob.astype(BF16)
-            agreement = agreements[slot][pair : pair + 1, :]
-            scores_grads[slot][pair] = (prob * (probs_grads[slot][pair] - agreement)).astype(BF16)
+            scores_grads[slot][pair] = (prob * (probs_grad - agreement)).astype(BF16)
 
     def stacked(pair_rows):
         zero = jnp.zeros_like(pair_rows)
         return jnp.concatenate([jnp.where(mask, pair_rows, zero) for mask in masks], axis=0)
 
-    def third(group, slot):
+    def second(group, slot):
         rows = group_rows(table, group)
         window, begin = rows.start, table[group, 1]
         for pair in pairs:
@@ -269,10 +280,24 @@
             key_t = block_diagonal(triple[rows, columns(pair, 1)].T)
             query_grad = dot(key_t, jnp.concatenate([scores_grad[:, :WIN], scores_grad[:, WIN:]], axis=0))
             keep_first(triple_grad, window, begin, columns(pair, 0), (query_grad * HD ** (-0.5)).T)
-            keep_first(triple_grad, window, begin, columns(pair, 1), key_grad)
+            keep_first(triple_grad, window, begin, columns(pair, 1), key_grad * (1.0 / LOG2E))
             keep_first(triple_grad, window, begin, columns(pair, 2), value_grad)
 
-    pipelined(groups, first, second, third)
+    def clamped(group):
+        return jnp.minimum(group, groups - 1)
+
+    def half(group, slot):
+        first(clamped(group), slot)
+        second(clamped(group - 1), 1 - slot)
+
+    first(0, 0)
+
+    def both(step, _):
+        half(2 * step + 1, 1)
+        half(2 * step + 2, 0)
+        return 0
+
+    lax.fori_loop(0, (groups + 1) // 2, both, 0)
 
 
 def interval(tile, first, end, size=TILE):
@@ -298,19 +323,24 @@
     scaled_ref[scaled_spot, :] = scaled.astype(BF16)
     normed = (scaled * row_of(gain1) + row_of(shift1)).astype(BF16)
     q = dot(normed, w_in[:, :width]) + b_in[0:1, :]
-    target[spot, :width] = (q.astype(BF16).astype(F32) * HD ** (-0.5)).astype(BF16)
+    target[spot, :width] = (q.astype(BF16).astype(F32) * (HD ** (-0.5) * LOG2E)).astype(BF16)
     target[spot, width : 2 * width] = dot(normed, w_in[:, width : 2 * width]).astype(BF16)
     target[spot, 2 * width :] = (dot(normed, w_in[:, 2 * width :]) + b_in[1:2, :]).astype(BF16)
 
 
 def kernel_own(
-    place, seg, gain1, shift1, b_in, x_in, w_in_in,
+    place, seg_in, gain1_in, shift1_in, b_in_in, x_in, w_in_in,
     triple_out, attended_out, scaled_out, stats, table,
-    x, w_in, triple, attended, work, ends, scores, peaks, raised, scales, sems, tile_sems,
+    seg, gain1, shift1, b_in, x, w_in, triple, attended, work, ends, scores, peaks, raised, scales, sems, tile_sems,
 ):
     rows, width = x_in.shape
     move = Mover(sems)
-    early = [move.start(w_in_in, w_in), move.start(x_in, x)]
+    seg_copy = move.start(seg_in, seg)
+    early = [
+        move.start(gain1_in, gain1), move.start(shift1_in, shift1), move.start(b_in_in, b_in),
+        move.start(x_in, x), move.start(w_in_in, w_in),
+    ]
+    seg_copy.wait()
     image_ends(seg, place[0] * rows, work)
     end_copy = move.start(work, ends)
     attended[...] = jnp.zeros_like(attended)
@@ -342,12 +372,20 @@
 
 
 def kernel_rest(
-    place, table, gain1, shift1, b_in, b_out, gain2, shift2, b_ex,
+    place, table, *refs
+):
+    vectors_in, refs = refs[:7], refs[7:]
+    vectors, refs = refs[-7:], refs[:-7]
+    rest_body(place, table, vectors_in, vectors, *refs)
+
+
+def rest_body(
+    place, table, vectors_in, vectors,
     x_in, cot_in, halo_in, triple_in, attended_in, scaled_in, stats_in, w_in_in, w_out_in, w_ex_in, w_sh_in,
-    middle_out, middle_grad_out, hidden_out, triple_grad_out, mine, other,
+    middle_out, middle_grad_out, hidden_out, triple_grad_out, mine_out, other_out,
     x, back, w_in, w_out, w_ex, w_sh, triple, attended, middle, middle_grad, upstream, hidden, triple_grad, stats,
-    d_ex, d_sh, d_out, product, sums, small, scores, peaks, raised, scales, probs_grads, probs, scores_grads,
-    edge, sems, tile_sems,
+    d_ex, d_sh, d_out, product, sums, small, scores, peaks, raised, scales, probs, scores_grads,
+    edge, mine, other, sems, tile_sems,
 ):
     rows, width = x_in.shape
     total = x.shape[0]
@@ -355,13 +393,16 @@
     normed2, normed_grad = upstream, middle_grad
     move = Mover(sems)
     own, over = pl.ds(0, rows), pl.ds(rows, HALO)
+    gain1, shift1, b_in, b_out, gain2, shift2, b_ex = vectors
+    vector_copies = [move.start(source, target) for source, target in zip(vectors_in, vectors)]
+    near, far = pl.ds(2 * WIDE, rows - 2 * WIDE), pl.ds(0, 2 * WIDE)
     early = [
         move.start(halo_in.at[:, pl.ds(0, width)], x.at[over]),
         move.start(w_in_in, w_in),
+        move.start(triple_in.at[near], triple.at[near]),
         move.start(stats_in, stats),
-        move.start(triple_in, triple.at[own]),
         move.start(attended_in, attended),
-    ]
+    ] + vector_copies
     late = [
         move.start(w_out_in, w_out),
         move.start(x_in, x.at[own]),
@@ -370,6 +411,7 @@
         move.start(w_ex_in, w_ex),
         move.start(w_sh_in, w_sh),
     ]
+    last = move.start(triple_in.at[far], triple.at[far])
     rest = pl.ds(rows + HALO, total - rows - HALO)
     x[rest, :] = jnp.zeros((total - rows - HALO, width), BF16)
     back[rest, :] = jnp.zeros((total - rows - HALO, width), BF16)
@@ -413,7 +455,7 @@
             return before, dot_nt(back_half, w_sh[cols, :])
 
         held = [first_part(begins[0])]
-        total_grad = jnp.zeros((FEED, width), F32)
+        total_grad = jnp.zeros((width, FEED), F32)
         for index, begin in enumerate(begins):
             cols = slice(begin, begin + CHUNK)
             if index + 1 < len(begins):
@@ -421,11 +463,11 @@
             value, grad = gelu_parts(*held[index])
             value, grad = value.astype(BF16), grad.astype(BF16)
             hidden[spot, cols] = value
-            total_grad = total_grad + dot_nt(grad, w_ex[:, cols])
+            total_grad = total_grad + dot_nt(w_ex[:, cols], grad)
             d_sh[:, cols] += dot_tn(back_low, value)
             d_ex[:, cols] += dot_tn(normed, grad)
             small[4:5, cols] += jnp.sum(grad.astype(F32), axis=0, keepdims=True)
-        normed_grad[spot, :] = total_grad
+        normed_grad[spot, :] = total_grad.T
         pltpu.make_async_copy(hidden.at[spot], hidden_out.at[spot], tile_sems.at[0]).start()
         return 0
 
@@ -452,8 +494,14 @@
     leaving.append(move.start(middle, middle_out))
     lax.fori_loop(0, tiles, feed, 0)
     lax.fori_loop(0, total // WIDE, after_feed, 0)
+    core = place[2]
+    for half, target in ((core, mine), (1 - core, other)):
+        at = pack((d_out,), half, target, pack_turned(d_sh, half, target, pack((d_ex,), half, target, 0)))
+    ready = pl.ds(0, at)
+    leaving += [move.start(mine.at[ready], mine_out.at[ready]), move.start(other.at[ready], other_out.at[ready])]
+    last.wait()
     attend_back_groups(
-        groups, table, triple, attended, upstream, stats, triple_grad, scores, peaks, probs_grads, probs, scores_grads,
+        groups, table, triple, attended, upstream, stats, triple_grad, probs, scores_grads
     )
     leaving.append(move.start(triple_grad, triple_grad_out))
     scaled_copy.wait()
@@ -483,31 +531,38 @@
     by_shift = jnp.broadcast_to(jnp.sum(by_shift, axis=1, keepdims=True), (width, LANES)).T
     small[6:7, :width] = by_gain[0:1]
     small[7:8, :width] = by_shift[0:1]
-    pack((d_ex, d_out, product), d_sh, small, place[2], mine, other)
+    begin = at
+    for half, target in ((core, mine), (1 - core, other)):
+        at = pack((product,), half, target, begin)
+    pack_small(small, core, mine, other, at)
+    ready = pl.ds(begin, mine.shape[0] - begin)
+    leaving += [move.start(mine.at[ready], mine_out.at[ready]), move.start(other.at[ready], other_out.at[ready])]
     for copy in leaving:
         copy.wait()
     pltpu.make_async_copy(hidden, hidden_out, tile_sems.at[0]).wait()
     pltpu.make_async_copy(middle_grad, middle_grad_out, tile_sems.at[1]).wait()
 
 
-def pack(grads, turned, small, core, mine, other):
-    def fill(half, target):
-        at = 0
-        for grad in grads:
-            count = grad.shape[0] // 2
-            rows = pl.ds(pl.multiple_of(half * count, count), count)
-            for begin in range(0, grad.shape[1], LANES):
-                target[pl.ds(at, count), :] = grad[rows, begin : begin + LANES].astype(BF16)
-                at += count
-        count, columns = turned.shape[0], turned.shape[1] // 2
-        for begin in range(0, columns, LANES):
-            cols = pl.ds(pl.multiple_of(half * columns + begin, LANES), LANES)
-            target[pl.ds(at, count), :] = turned[:, cols].astype(BF16)
+def pack(grads, half, target, at):
+    for grad in grads:
+        count = grad.shape[0] // 2
+        rows = pl.ds(pl.multiple_of(half * count, count), count)
+        for begin in range(0, grad.shape[1], LANES):
+            target[pl.ds(at, count), :] = grad[rows, begin : begin + LANES].astype(BF16)
             at += count
-        return at
-
-    fill(core, mine)
-    at = fill(1 - core, other)
+    return at
+
+
+def pack_turned(grad, half, target, at):
+    count, columns = grad.shape[0], grad.shape[1] // 2
+    for begin in range(0, columns, LANES):
+        cols = pl.ds(pl.multiple_of(half * columns + begin, LANES), LANES)
+        target[pl.ds(at, count), :] = grad[:, cols].astype(BF16)
+        at += count
+    return at
+
+
+def pack_small(small, core, mine, other, at):
     rest = mine.shape[0] - at
     mine[pl.ds(at, rest), :] = jnp.zeros((rest, LANES), BF16)
     other[pl.ds(at, rest), :] = jnp.zeros((rest, LANES), BF16)
@@ -651,7 +706,7 @@
 
 
 def kernel_unpack_half(where, packed_in, d_ex, d_out, d_in, d_sh, packed, ex, out, inward, sh, sems):
-    arrays = ((ex, d_ex), (out, d_out), (inward, d_in), (sh, d_sh))
+    arrays = ((ex, d_ex), (sh, d_sh), (out, d_out), (inward, d_in))
     sizes = [value.shape[0] * value.shape[1] // LANES for value, _target in arrays]
     begins = [sum(sizes[:index]) for index in range(4)]
     arriving = []
@@ -664,7 +719,7 @@
     for index, (value, target) in enumerate(arrays):
         arriving[index].wait()
         at = begins[index]
-        if index < 3:
+        if index != 1:
             count = value.shape[0]
             for begin in range(0, value.shape[1], LANES):
                 value[:, begin : begin + LANES] = packed[pl.ds(at, count), :].astype(F32)
@@ -766,9 +821,13 @@
             shape((GROUPS, 8, WIN), F32),
             shape((GROUPS + 1, 8), jnp.int32),
         ),
-        in_specs=[SMEM] + [VMEM] * 4 + [ANY] * 2,
+        in_specs=[SMEM] + [ANY] * 6,
         out_specs=(ANY, ANY, ANY, VMEM, SMEM),
         scratch_shapes=[
+            vmem(segments.shape, jnp.int32),
+            vmem(gain1.shape, F32),
+            vmem(shift1.shape, F32),
+            vmem(b_in.shape, F32),
             vmem((rows, width), BF16),
             vmem(w_in.shape, BF16),
             vmem((total, 3 * width), BF16),
@@ -776,7 +835,7 @@
             vmem((8, LANES), jnp.int32),
             pltpu.SMEM((8, LANES), jnp.int32),
             *attention_scratch(width // (2 * HD)),
-            pltpu.SemaphoreType.DMA((8,)),
+            pltpu.SemaphoreType.DMA((16,)),
             pltpu.SemaphoreType.DMA((rows // OWN,)),
         ],
         compiler_params=params(63),
@@ -804,8 +863,8 @@
             shape((packed, LANES), BF16),
             shape((packed, LANES), BF16),
         ),
-        in_specs=[SMEM, SMEM] + [VMEM] * 7 + [ANY] * 11,
-        out_specs=tuple([ANY] * 4 + [VMEM] * 2),
+        in_specs=[SMEM, SMEM] + [ANY] * 18,
+        out_specs=tuple([ANY] * 6),
         scratch_shapes=[
             vmem((total, width), BF16),
             vmem((total, width), BF16),
@@ -827,16 +886,18 @@
             vmem((width, 3 * width), F32),
             vmem((16, 3 * width), F32),
             vmem((16, hidden), F32),
-            [square] * 2,
-            [row] * 2,
+            [square],
+            [row],
             [vmem((pairs, 2 * WIN, WIN), BF16)],
             [row],
-            [square] * 2,
             [low] * 2,
             [low] * 2,
             vmem((TILE, width), BF16),
-            pltpu.SemaphoreType.DMA((16,)),
+            vmem((packed, LANES), BF16),
+            vmem((packed, LANES), BF16),
+            pltpu.SemaphoreType.DMA((40,)),
             pltpu.SemaphoreType.DMA((2,)),
+            *[vmem(v.shape, F32) for v in vectors],
         ],
         compiler_params=params(62),
         cost_estimate=cost(2 * 9 * rows * width * (3 * width + 8 * width), 3e7),
@@ -992,9 +1053,36 @@
     return lax.ppermute(block, "mp", route)
 
 
-def take_over(own, other, first):
+def kernel_take_over(table, own_in, other_in, own_out, own, other, sems):
+    rows = pl.ds(0, HALO)
+    copies = [
+        pltpu.make_async_copy(own_in.at[rows], own, sems.at[0]), pltpu.make_async_copy(other_in, other, sems.at[1])
+    ]
+    for copy in copies:
+        copy.start()
+    for copy in copies:
+        copy.wait()
     row = lax.broadcasted_iota(jnp.int32, (HALO, 1), 0)
-    return lax.dynamic_update_slice(own, jnp.where(row < first, other, own[:HALO]), (0, 0))
+    mixed = jnp.where(row < table[GROUPS, 1], other[...].astype(F32), own[...].astype(F32))
+    own[...] = mixed.astype(own.dtype)
+    copy = pltpu.make_async_copy(own, own_out.at[rows], sems.at[2])
+    copy.start()
+    copy.wait()
+
+
+def take_over(table, own, other):
+    return pl.pallas_call(
+        kernel_take_over,
+        out_shape=shape(own.shape, own.dtype),
+        in_specs=[SMEM, ANY, ANY],
+        out_specs=ANY,
+        scratch_shapes=[
+            pltpu.VMEM(other.shape, own.dtype), pltpu.VMEM(other.shape, own.dtype), pltpu.SemaphoreType.DMA((3,)),
+        ],
+        input_output_aliases={1: 0},
+        compiler_params=params(63),
+        name="take_over",
+    )(table, own, other)
 
 
 def body(
@@ -1022,11 +1110,11 @@
     parts = exchange(both.reshape(pieces, -1, LANES))
     input_grad, input_halo = input_gradient(both, gain1, layer_input, halo, inward_weight, triple_grad, middle_grad)
     result, result_halo = layer_result(input_halo, table, b_sh, middle, hidden, shrink_weight)
-    summed = sum_parts((input_halo, result_halo), parts)
+    input_other = passed(input_halo[:HALO], 1)
+    summed = sum_parts((input_other, result_halo), parts)
     mine = exchange(summed).reshape(-1, LANES)
-    first = table[GROUPS, 1]
-    input_grad = take_over(input_grad, passed(touch(input_halo, summed)[:HALO], 1), first)
-    result = take_over(result, passed(touch(result_halo, summed)[:HALO], 1), first)
+    input_grad = take_over(table, input_grad, touch(input_other, summed))
+    result = take_over(table, result, passed(touch(result_halo, summed)[:HALO], 1))
     mine = touch(mine, input_grad, result)
     other = swap_cores(mine)
     used = 192 * (2 * hidden_width + 4 * width) // LANES

time: 183 us -> 179 us (0.978)
  waiting for transfers between devices: 27.5 us -> 22.5 us
  other arithmetic: 4.77 us -> 0.62 us
  Pallas kernels: 109 us -> 112 us
  starting transfers between devices: 34.1 us -> 36.4 us
    all_to_all x2, waiting for transfers between devices: 6.29 us -> 0.79 us  [exchange(): lax.all_to_all(parts, ('dp', 'mp'), 0, 0, axis_index_groups=same_core_gro...]
    pallas_call x0 -> x2, Pallas kernels: none -> 5.42 us  [take_over(): pl.pallas_call(kernel_take_over, out_shape=shape(own.shape, own.dtype), i...]
    dynamic_update_slice x2 -> x0, other arithmetic: 3.5 us -> none  [take_over(): lax.dynamic_update_slice(own, jnp.where(row < first, other, own[:HALO]),...]
  transfers between devices with their start and end apart: 7 -> 7, of which waited for: 5 -> 6; matrix products, arithmetic and copies ran while one was open for 4% -> 1% of each run, Pallas kernels for 23% -> 26%
where the time goes in v4:
time: 179 us; the launch traced here: 178 us
  Pallas kernels  112 us (63%)
  starting transfers between devices  36.4 us (20%)
  waiting for transfers between devices  22.5 us (13%)
  local copies, waits for them, and re-layouts  5.42 us (3%)
    pallas_call x1, Pallas kernels, rest_part(): pl.pallas_call(kernel_rest, out_shape=(shape((total, width), F32), shape(...  56.5 us
    all_to_all x2, starting transfers between devices, exchange(): lax.all_to_all(parts, ('dp', 'mp'), 0, 0, axis_index_groups=same_core_gro...  24.7 us
    pallas_call x1, Pallas kernels, own_part(): pl.pallas_call(kernel_own, out_shape=(shape((rows, 3 * width), BF16), sha...  17.9 us
    ppermute x3, waiting for transfers between devices, passed(): return lax.ppermute(block, 'mp', route)  16.9 us
    pallas_call x1, Pallas kernels, layer_result(): pl.pallas_call(kernel_result, out_shape=(shape((total - TILE, width), BF1...  9.91 us
    pallas_call x1, Pallas kernels, input_gradient(): pl.pallas_call(kernel_input, out_shape=(shape((rows, width), F32), shape(...  9.69 us
    ppermute x3, starting transfers between devices, passed(): return lax.ppermute(block, 'mp', route)  7.29 us
    pallas_call x2, Pallas kernels, take_over(): pl.pallas_call(kernel_take_over, out_shape=shape(own.shape, own.dtype), i...  5.42 us
  transfers between devices with their start and end apart: 7, of which 6 were waited for; matrix products, arithmetic and copies ran while one was open for 1% of the time, Pallas kernels for 26%

profile of v4, /device:TPU:1, one launch (start us, length us, event | category | flops | bytes accessed | tf_op | source)
XLA Modules:
  0.0 177.8 jit_solution(1659841768337542488)
XLA Ops:
  0.6 0.9 slice.12
  1.6 0.9 slice.13
  2.6 1.3 collective-permute-start
  4.5 17.9 %own_part.1 = (bf16[2048,1152]{1,0:T(8,128)(2,1)}, bf16[2304,384]{1,0:T(8,128)(2,1)}, bf16[2048,384]{1,0:T(8,128)(2,1)}, f32[24,8,256]{2,1,0:T(8,128)}, s32[25,8]{1,0:T(8,128)}) custom-call(s32[3]{0:T(128)} %pad_add_fusion.place, s32[1,8192]{1,0:T(1,128)} %seg_in.1, f32[384]{0:T(512)} %gain1.1, f32[384]{0:T(512)} %refs_1_.1, f32[2,384]{1,0:T(2,128)} %refs_2_.1, ...), custom_call_target="tpu_custom_call" | custom-call | flops 10871635968 | bytes 10000000 | tf_op jit(solution)/shard_map/own_part/pallas_call | solution.py:815
  22.4 0.7 copy-done.2
  23.1 56.5 %rest_part.1 = (f32[2304,384]{1,0:T(8,128)}, f32[2304,384]{1,0:T(8,128)}, bf16[2304,1536]{1,0:T(8,128)(2,1)}, bf16[2304,1152]{1,0:T(8,128)(2,1)}, bf16[7168,128]{1,0:T(8,128)(2,1)}, /*index=5*/bf16[7168,128]{1,0:T(8,128)(2,1)}) custom-call(s32[3]{0:T(128)} %pad_add_fusion.place, s32[25,8]{1,0:T(8,128)} %get-tuple-element.45.table, f32[384]{0:T(512)} %gain1.1, ...), custom_call_target="tpu_custom_call" | custom-call | flops 59793997824 | bytes 30000000 | tf_op jit(solution)/shard_map/rest_part/pallas_call | solution.py:856
  79.7 4.1 %collective-permute-done.1.other_in = bf16[7168,128]{1,0:T(8,128)(2,1)} collective-permute-done((bf16[7168,128]{1,0:T(8,128)(2,1)}, bf16[7168,128]{1,0:T(8,128)(2,1)}, u32[]{:S(2)}, u32[]{:S(2)}) %collective-permute-start.1) | collective-permute-done | bytes 1835040 | tf_op jit(solution)/shard_map/ppermute | solution.py:1043
  83.8 3.0 %add_halves.1.after = bf16[7168,128]{1,0:T(8,128)(2,1)} custom-call(bf16[7168,128]{1,0:T(8,128)(2,1)} %get-tuple-element.50.mine_in, bf16[7168,128]{1,0:T(8,128)(2,1)} %collective-permute-done.1.other_in), custom_call_target="tpu_custom_call" | custom-call | flops 917504 | bytes 5505024 | tf_op jit(solution)/shard_map/add_halves/pallas_call | solution.py:954
  86.8 13.4 %all-to-all-start = ((bf16[64,112,128]{2,1,0:T(8,128)(2,1)}), bf16[64,112,128]{2,1,0:T(8,128)(2,1)}, u32[]{:S(2)}, u32[]{:S(2)}) async-start(bf16[64,112,128]{2,1,0:T(8,128)(2,1)} %bitcast.4), calls=%async_computation | async-start | bytes 3670016 | tf_op jit(solution)/shard_map/all_to_all | solution.py:1047
  100.2 9.7 %input_gradient.1 = (f32[2048,384]{1,0:T(8,128)}, f32[256,384]{1,0:T(8,128)}) custom-call(bf16[7168,128]{1,0:T(8,128)(2,1)} %add_halves.1.after, f32[384]{0:T(512)} %gain1.1, bf16[2048,384]{1,0:T(8,128)(2,1)} %x_in.3, bf16[208,768]{1,0:T(8,128)(2,1)} %copy-done.2, bf16[384,1152]{1,0:T(8,128)(2,1)} %w_in_in.3, ...), custom_call_target="tpu_custom_call" | custom-call | flops 5435817984 | bytes 14000000 | tf_op jit(solution)/shard_map/input_gradient/pallas_call | solution.py:912
  109.9 1.0 slice.14
  110.9 3.1 %collective-permute-start.2 = (f32[208,384]{1,0:T(8,128)S(1)}, f32[208,384]{1,0:T(8,128)S(1)}, u32[]{:S(2)}, u32[]{:S(2)}) collective-permute-start(f32[208,384]{1,0:T(8,128)S(1)} %slice.14), channel_id=1, source_target_pairs={{0,1},{1,2},{2,3},{4,5},{5,6},{6,7},{8,9},{9,10},{10,11},{12,13},{... | collective-permute-start | bytes 958472 | tf_op jit(solution)/shard_map/ppermute | solution.py:1053
  114.0 9.9 %layer_result.1 = (bf16[2048,384]{1,0:T(8,128)(2,1)}, bf16[256,384]{1,0:T(8,128)(2,1)}) custom-call(f32[256,384]{1,0:T(8,128)} %get-tuple-element.54.after, s32[25,8]{1,0:T(8,128)} %get-tuple-element.45.table, f32[384]{0:T(512)} %b_sh.1, f32[2304,384]{1,0:T(8,128)} %get-tuple-element.55.middle_in, bf16[2304,1536]{1,0:T(8,128)(2,1)} %get-tuple-element.56.hidden_in, ...), custom_call_target="tpu_custom_call" | custom-call | flops 5435817984 | bytes 13000000 | tf_op jit(solution)/shard_map/layer_result/pallas_call | solution.py:934
  123.9 1.9 %collective-permute-done.2.refs_0_ = f32[208,384]{1,0:T(8,128)S(1)} collective-permute-done((f32[208,384]{1,0:T(8,128)S(1)}, f32[208,384]{1,0:T(8,128)S(1)}, u32[]{:S(2)}, u32[]{:S(2)}) %collective-permute-start.2) | collective-permute-done | bytes 319520 | tf_op jit(solution)/shard_map/ppermute | solution.py:1053
  126.6 2.7 %sum_parts.1.refs_1_ = bf16[64,112,128]{2,1,0:T(8,128)(2,1)} custom-call(f32[208,384]{1,0:T(8,128)} %copy-done, bf16[256,384]{1,0:T(8,128)(2,1)} %get-tuple-element.58.refs_1_.refs_0_, bf16[64,112,128]{2,1,0:T(8,128)(2,1)} %all-to-all-done.refs_2_), custom_call_target="tpu_custom_call" | custom-call | flops 917504 | bytes 3670016 | tf_op jit(solution)/shard_map/sum_parts/pallas_call | solution.py:969
  129.3 11.3 %all-to-all-start.1 = ((bf16[64,112,128]{2,1,0:T(8,128)(2,1)}), bf16[64,112,128]{2,1,0:T(8,128)(2,1)}, u32[]{:S(2)}, u32[]{:S(2)}) async-start(bf16[64,112,128]{2,1,0:T(8,128)(2,1)} %sum_parts.1.refs_1_), calls=%async_computation.1 | async-start | bytes 3670016 | tf_op jit(solution)/shard_map/all_to_all | solution.py:1047
  140.7 0.9 slice.16
  141.6 2.9 %collective-permute-start.3 = (bf16[208,384]{1,0:T(8,128)(2,1)S(1)}, bf16[208,384]{1,0:T(8,128)(2,1)S(1)}, u32[]{:S(2)}, u32[]{:S(2)}) collective-permute-start(bf16[208,384]{1,0:T(8,128)(2,1)S(1)} %slice.16), channel_id=1, source_target_pairs={{0,1},{1,2},{2,3},{4,5},{5,6},{6,7},{8,9},{9,10},{10,11},{12,13},{... | collective-permute-start | bytes 479240 | tf_op jit(solution)/shard_map/ppermute | solution.py:1053
  144.5 2.8 %take_over.3.refs_1_ = f32[2048,384]{1,0:T(8,128)} custom-call(s32[25,8]{1,0:T(8,128)} %get-tuple-element.45.table, f32[2048,384]{1,0:T(8,128)} %get-tuple-element.59.own_in, f32[208,384]{1,0:T(8,128)} %touch.4.other_in), custom_call_target="tpu_custom_call", output_to_operand_aliasing={{}: (1, {})} | custom-call | tf_op jit(solution)/shard_map/take_over/pallas_call | solution.py:1074
  147.3 14.9 %collective-permute-done.3.other_in = bf16[208,384]{1,0:T(8,128)(2,1)S(1)} collective-permute-done((bf16[208,384]{1,0:T(8,128)(2,1)S(1)}, bf16[208,384]{1,0:T(8,128)(2,1)S(1)}, u32[]{:S(2)}, u32[]{:S(2)}) %collective-permute-start.3) | collective-permute-done | bytes 159776 | tf_op jit(solution)/shard_map/ppermute | solution.py:1053
  162.9 2.6 %take_over.2.refs_2_ = bf16[2048,384]{1,0:T(8,128)(2,1)} custom-call(s32[25,8]{1,0:T(8,128)} %get-tuple-element.45.table, bf16[2048,384]{1,0:T(8,128)(2,1)} %get-tuple-element.57.own_in, bf16[208,384]{1,0:T(8,128)(2,1)} %copy-done.1), custom_call_target="tpu_custom_call", output_to_operand_aliasing={{}: (1, {})} | custom-call | tf_op jit(solution)/shard_map/take_over/pallas_call | solution.py:1074
  165.8 4.3 %collective-permute-start.4 = (bf16[7168,128]{1,0:T(8,128)(2,1)}, bf16[7168,128]{1,0:T(8,128)(2,1)}, u32[]{:S(2)}, u32[]{:S(2)}) collective-permute-start(bf16[7168,128]{1,0:T(8,128)(2,1)} %touch.5.packed_in.first_in), channel_id=1, source_target_pairs={{0,4},{4,0},{8,12},{12,8},{16,20},{20,16},{24,28},{28,24},{32,36},... | collective-permute-start | bytes 5505032 | tf_op jit(solution)/shard_map/ppermute | solution.py:1043
  170.2 3.0 %unpack_first.1 = (f32[384,1536]{1,0:T(8,128)}, f32[384,384]{1,0:T(8,128)}, f32[384,1152]{1,0:T(8,128)}, f32[1536,384]{1,0:T(8,128)}) custom-call(s32[1]{0:T(128)} %bitcast.1.where, bf16[7168,128]{1,0:T(8,128)(2,1)} %touch.5.packed_in.first_in), custom_call_target="tpu_custom_call" | custom-call | flops 917504 | bytes 5505024 | tf_op jit(solution)/shard_map/unpack_first/pallas_call | solution.py:993
  173.9 3.7 %unpack_second.1 = (f32[384,1536]{1,0:T(8,128)}, f32[384,384]{1,0:T(8,128)}, f32[384,1152]{1,0:T(8,128)}, f32[1536,384]{1,0:T(8,128)}, f32[2,384]{1,0:T(2,128)},...) custom-call(s32[1]{0:T(128)S(6)} %sub.3.where, ...), custom_call_target="tpu_custom_call", output_to_operand_aliasing={{0}: (3, {}), {1}: (4, {}), {2}: (5, {}), {3}: (6, {})} | custom-call | flops 917504 | bytes 5505024 | tf_op jit(solution)/shard_map/unpack_second/pallas_call | solution.py:1009
  (15 shorter events, 3.1 us)
Async XLA Ops:
  2.6 19.8 %collective-permute-start = (bf16[208,768]{1,0:T(8,128)(2,1)S(1)}, bf16[208,768]{1,0:T(8,128)(2,1)S(1)}, u32[]{:S(2)}, u32[]{:S(2)}) collective-permute-start(bf16[208,768]{1,0:T(8,128)(2,1)S(1)} %pad_maximum_fusion), channel_id=1, source_target_pairs={{1,0},{2,1},{3,2},{5,4},{6,5},{7,6},{9,8},{10,9},{11,10},{13,12},{... | collective-permute-start | bytes 958472 | tf_op jit(solution)/shard_map/ppermute | solution.py:1053
  22.4 0.7 copy-start.2
  79.6 4.2 %collective-permute-start.1 = (bf16[7168,128]{1,0:T(8,128)(2,1)}, bf16[7168,128]{1,0:T(8,128)(2,1)}, u32[]{:S(2)}, u32[]{:S(2)}) collective-permute-start(bf16[7168,128]{1,0:T(8,128)(2,1)} %get-tuple-element.51), channel_id=1, source_target_pairs={{0,4},{4,0},{8,12},{12,8},{16,20},{20,16},{24,28},{28,24},{32,36},... | collective-permute-start | bytes 5505032 | tf_op jit(solution)/shard_map/ppermute | solution.py:1043
  86.8 39.5 %all-to-all-start = ((bf16[64,112,128]{2,1,0:T(8,128)(2,1)}), bf16[64,112,128]{2,1,0:T(8,128)(2,1)}, u32[]{:S(2)}, u32[]{:S(2)}) async-start(bf16[64,112,128]{2,1,0:T(8,128)(2,1)} %bitcast.4), calls=%async_computation | async-start | bytes 3670016 | tf_op jit(solution)/shard_map/all_to_all | solution.py:1047
  110.9 15.0 %collective-permute-start.2 = (f32[208,384]{1,0:T(8,128)S(1)}, f32[208,384]{1,0:T(8,128)S(1)}, u32[]{:S(2)}, u32[]{:S(2)}) collective-permute-start(f32[208,384]{1,0:T(8,128)S(1)} %slice.14), channel_id=1, source_target_pairs={{0,1},{1,2},{2,3},{4,5},{5,6},{6,7},{8,9},{9,10},{10,11},{12,13},{... | collective-permute-start | bytes 958472 | tf_op jit(solution)/shard_map/ppermute | solution.py:1053
  125.9 0.7 copy-start
  129.3 36.5 %all-to-all-start.1 = ((bf16[64,112,128]{2,1,0:T(8,128)(2,1)}), bf16[64,112,128]{2,1,0:T(8,128)(2,1)}, u32[]{:S(2)}, u32[]{:S(2)}) async-start(bf16[64,112,128]{2,1,0:T(8,128)(2,1)} %sum_parts.1.refs_1_), calls=%async_computation.1 | async-start | bytes 3670016 | tf_op jit(solution)/shard_map/all_to_all | solution.py:1047
  141.6 20.6 %collective-permute-start.3 = (bf16[208,384]{1,0:T(8,128)(2,1)S(1)}, bf16[208,384]{1,0:T(8,128)(2,1)S(1)}, u32[]{:S(2)}, u32[]{:S(2)}) collective-permute-start(bf16[208,384]{1,0:T(8,128)(2,1)S(1)} %slice.16), channel_id=1, source_target_pairs={{0,1},{1,2},{2,3},{4,5},{5,6},{6,7},{8,9},{9,10},{10,11},{12,13},{... | collective-permute-start | bytes 479240 | tf_op jit(solution)/shard_map/ppermute | solution.py:1053
  162.2 0.7 copy-start.1
  165.8 8.1 %collective-permute-start.4 = (bf16[7168,128]{1,0:T(8,128)(2,1)}, bf16[7168,128]{1,0:T(8,128)(2,1)}, u32[]{:S(2)}, u32[]{:S(2)}) collective-permute-start(bf16[7168,128]{1,0:T(8,128)(2,1)} %touch.5.packed_in.first_in), channel_id=1, source_target_pairs={{0,4},{4,0},{8,12},{12,8},{16,20},{20,16},{24,28},{28,24},{32,36},... | collective-permute-start | bytes 5505032 | tf_op jit(solution)/shard_map/ppermute | solution.py:1043

commit v5 on v4

--- a/solution.py
+++ b/solution.py
@@ -18,6 +18,7 @@
 WIDE = 768
 OWN = 1024
 GROUPS = 24
+SLOTS = 5
 LANES = 128
 CHUNK = 256
 FEED = 768
@@ -166,7 +167,7 @@
     )
 
 
-def pipelined(groups, first, second, third, arrive=lambda group, have: have):
+def pipelined(groups, first, second, third, keep_copy):
     def clamped(group):
         return jnp.minimum(group, groups - 1)
 
@@ -175,31 +176,42 @@
         second(clamped(group - 1), 1 - slot)
         third(clamped(group - 2), slot)
 
-    have = arrive(clamped(1), jnp.int32(0))
     first(0, 0)
     first(clamped(1), 1)
     second(0, 0)
-
-    def both(step, have):
-        have = arrive(clamped(2 * step + 3), have)
+    steps = (groups + 1) // 2
+
+    def both(step, _):
+        keep_copy(clamped(2 * step)).start()
+
+        @pl.when(step > 0)
+        def _():
+            keep_copy(clamped(2 * step - 1)).start()
+
         half(2 * step + 2, 0)
         half(2 * step + 3, 1)
-        return have
-
-    have = lax.fori_loop(0, (groups + 1) // 2, both, have)
-    arrive(None, have)
-
-
-def group_rows(table, group, shifted=0):
-    return pl.ds(pl.multiple_of(table[group, 0] - shifted, 16), WIN)
-
-
-def attend_groups(groups, table, triple, attended, stats, scores, peaks, raised, scales, alone=None, shifted=0):
+        return 0
+
+    lax.fori_loop(0, steps, both, 0)
+    keep_copy(clamped(2 * steps - 1)).start()
+
+    def settle(_, carry):
+        keep_copy(0).wait()
+        return carry
+
+    return lambda: lax.fori_loop(0, 2 * steps, settle, 0)
+
+
+def group_rows(table, group):
+    return pl.ds(pl.multiple_of(table[group, 0], 16), WIN)
+
+
+def attend_groups(groups, table, triple, attended, stats, scores, peaks, raised, scales, alone=None, kept=None, keep_copy=None):
     width = attended.shape[1]
     pairs = range(width // (2 * HD))
 
     def first(group, slot):
-        rows = group_rows(table, group, shifted)
+        rows = group_rows(table, group)
         left, right = group_mask_factors(table, group)
         for pair in pairs:
             query_t = triple[rows, pl.ds(pair * 2 * HD, 2 * HD)].T
@@ -215,30 +227,36 @@
             peak = peaks[slot][pair : pair + 1, :]
             value = jnp.exp2(scores[slot][pair] - peak)
             total = jnp.sum(value, axis=0, keepdims=True)
-            raised[slot][pair, :WIN] = value[:, :WIN].astype(BF16)
-            raised[slot][pair, WIN:] = value[:, WIN:].astype(BF16)
-            scales[slot][pair : pair + 1, :] = 1.0 / total
-            lse = peak + LOG2E * jnp.log(total)
-            stats[group, pl.ds(2 * pair, 1), :] = lse[:, :WIN]
-            stats[group, pl.ds(2 * pair + 1, 1), :] = lse[:, WIN:]
+            low = value.astype(BF16)
+            raised[slot][pair, :WIN] = low[:, :WIN]
+            raised[slot][pair, WIN:] = low[:, WIN:]
+            if kept is not None:
+                kept[group, pair, :WIN] = low[:, :WIN]
+                kept[group, pair, WIN:] = low[:, WIN:]
+            scale = 1.0 / total
+            scales[slot][pair : pair + 1, :] = scale
+            stats[group, pl.ds(2 * pair, 1), :] = scale[:, :WIN]
+            stats[group, pl.ds(2 * pair + 1, 1), :] = scale[:, WIN:]
 
     def third(group, slot):
-        rows = group_rows(table, group, shifted)
+        rows = group_rows(table, group)
         for pair in pairs:
             value_t = block_diagonal(triple[rows, pl.ds(2 * width + pair * 2 * HD, 2 * HD)].T)
             out = dot(value_t, raised[slot][pair])
             scale = scales[slot][pair : pair + 1, :]
             out = jnp.concatenate([out[:HD] * scale[:, :WIN], out[HD:] * scale[:, WIN:]], axis=0)
-            keep_first(attended, group_rows(table, group).start, table[group, 1], pl.ds(pair * 2 * HD, 2 * HD), out.T)
+            keep_first(attended, rows.start, table[group, 1], pl.ds(pair * 2 * HD, 2 * HD), out.T)
 
     if alone is None:
-        pipelined(groups, first, second, third)
-    else:
-        for part in (first, second, third):
-            part(alone, 0)
-
-
-def attend_back_groups(groups, table, triple, attended, upstream, stats, triple_grad, probs, scores_grads):
+        return pipelined(groups, first, second, third, keep_copy)
+    for part in (first, second, third):
+        part(alone, 0)
+    return None
+
+
+def attend_back_groups(
+    groups, table, triple, attended, upstream, stats, triple_grad, scores_grads, scaled_up, kept, kept_copy
+):
     width = attended.shape[1]
     pairs = range(width // (2 * HD))
     masks = head_masks()
@@ -246,36 +264,35 @@
     def columns(pair, block):
         return pl.ds(block * width + pair * 2 * HD, 2 * HD)
 
-    def first(group, slot):
+    def side_by_side(turn, pair):
+        low = kept[lax.rem(turn, SLOTS), pair]
+        return jnp.concatenate([low[:WIN], low[WIN:]], axis=1)
+
+    def first(turn, group, slot):
         rows = group_rows(table, group)
-        bias = group_bias(table, group)
-        bias = jnp.concatenate([bias, bias], axis=1)
         for pair in pairs:
-            lse = jnp.concatenate(
-                [stats[group, pl.ds(2 * pair, 1), :], stats[group, pl.ds(2 * pair + 1, 1), :]], axis=1
-            )
-            query_t = triple[rows, columns(pair, 0)].T
-            up_t = upstream[rows, columns(pair, 0)].T
-            product = attended[rows, columns(pair, 0)].T.astype(F32) * up_t.astype(F32)
+            scale = [jnp.broadcast_to(stats[group, pl.ds(2 * pair + h, 1), :], (HD, WIN)) for h in range(2)]
+            up_t = upstream[rows, columns(pair, 0)].T.astype(F32) * jnp.concatenate(scale, axis=0)
+            product = attended[rows, columns(pair, 0)].T.astype(F32) * up_t
             agreement = jnp.concatenate(
                 [jnp.sum(product[:HD], axis=0, keepdims=True), jnp.sum(product[HD:], axis=0, keepdims=True)], axis=1
             )
-            scores = dot(triple[rows, columns(pair, 1)], block_diagonal(query_t))
-            probs_grad = dot(triple[rows, columns(pair, 2)], block_diagonal(up_t))
-            prob = jnp.exp2(scores + bias - lse)
-            probs[slot][pair] = prob.astype(BF16)
+            up_low = up_t.astype(BF16)
+            scaled_up[slot][pair] = up_low
+            probs_grad = dot(triple[rows, columns(pair, 2)], block_diagonal(up_low))
+            prob = side_by_side(turn, pair).astype(F32)
             scores_grads[slot][pair] = (prob * (probs_grad - agreement)).astype(BF16)
 
     def stacked(pair_rows):
         zero = jnp.zeros_like(pair_rows)
         return jnp.concatenate([jnp.where(mask, pair_rows, zero) for mask in masks], axis=0)
 
-    def second(group, slot):
+    def second(turn, group, slot):
         rows = group_rows(table, group)
         window, begin = rows.start, table[group, 1]
         for pair in pairs:
             scores_grad = scores_grads[slot][pair]
-            value_grad = dot(probs[slot][pair], stacked(upstream[rows, columns(pair, 0)]))
+            value_grad = dot_nt(side_by_side(turn, pair), block_diagonal(scaled_up[slot][pair]))
             key_grad = dot(scores_grad, stacked(triple[rows, columns(pair, 0)]))
             key_t = block_diagonal(triple[rows, columns(pair, 1)].T)
             query_grad = dot(key_t, jnp.concatenate([scores_grad[:, :WIN], scores_grad[:, WIN:]], axis=0))
@@ -283,21 +300,37 @@
             keep_first(triple_grad, window, begin, columns(pair, 1), key_grad * (1.0 / LOG2E))
             keep_first(triple_grad, window, begin, columns(pair, 2), value_grad)
 
-    def clamped(group):
-        return jnp.minimum(group, groups - 1)
-
-    def half(group, slot):
-        first(clamped(group), slot)
-        second(clamped(group - 1), 1 - slot)
-
-    first(0, 0)
+    def clamped(turn):
+        return jnp.minimum(turn, groups - 1)
+
+    def half(turn, slot):
+        first(turn, clamped(turn), slot)
+        second(turn - 1, clamped(turn - 1), 1 - slot)
+
+    steps = (groups + 1) // 2
+
+    def fetch(turn):
+        kept_copy(clamped(turn), lax.rem(turn, SLOTS))
+
+    def arrived(turn):
+        kept_copy(None, lax.rem(turn, SLOTS))
+
+    arrived(jnp.int32(0))
+    first(jnp.int32(0), 0, 0)
 
     def both(step, _):
+        @pl.when(step + 1 < steps)
+        def _():
+            fetch(2 * step + 3)
+            fetch(2 * step + 4)
+
+        arrived(2 * step + 1)
+        arrived(2 * step + 2)
         half(2 * step + 1, 1)
         half(2 * step + 2, 0)
         return 0
 
-    lax.fori_loop(0, (groups + 1) // 2, both, 0)
+    lax.fori_loop(0, steps, both, 0)
 
 
 def interval(tile, first, end, size=TILE):
@@ -329,9 +362,9 @@
 
 
 def kernel_own(
-    place, seg_in, gain1_in, shift1_in, b_in_in, x_in, w_in_in,
-    triple_out, attended_out, scaled_out, stats, table,
-    seg, gain1, shift1, b_in, x, w_in, triple, attended, work, ends, scores, peaks, raised, scales, sems, tile_sems,
+    seg_in, gain1_in, shift1_in, b_in_in, x_in, w_in_in,
+    triple_out, attended_out, scaled_out, raised_out, stats, table,
+    seg, gain1, shift1, b_in, x, w_in, triple, attended, work, ends, scores, peaks, raised, scales, kept, sems, tile_sems,
 ):
     rows, width = x_in.shape
     move = Mover(sems)
@@ -341,13 +374,11 @@
         move.start(x_in, x), move.start(w_in_in, w_in),
     ]
     seg_copy.wait()
-    image_ends(seg, place[0] * rows, work)
+    image_ends(seg, lax.axis_index("mp") * rows, work)
     end_copy = move.start(work, ends)
     attended[...] = jnp.zeros_like(attended)
     spare = pl.ds(rows, triple.shape[0] - rows)
     triple[spare, :] = jnp.zeros((triple.shape[0] - rows, 3 * width), BF16)
-    end_copy.wait()
-    plan_groups(ends, place[0], rows, table)
     for copy in early:
         copy.wait()
 
@@ -363,29 +394,39 @@
 
     lax.fori_loop(0, rows // OWN, step_rows, 0)
     scaled_copy = move.start(x, scaled_out)
-    attend_groups(jnp.maximum(table[GROUPS, 0] - 1, 1), table, triple, attended, stats, scores, peaks, raised, scales)
+    end_copy.wait()
+    plan_groups(ends, lax.axis_index("mp"), rows, table)
+
+    def keep_copy(group):
+        return pltpu.make_async_copy(kept.at[group], raised_out.at[group], tile_sems.at[rows // OWN])
+
+    settle = attend_groups(
+        jnp.maximum(table[GROUPS, 0] - 1, 1), table, triple, attended, stats, scores, peaks, raised, scales,
+        kept=kept, keep_copy=keep_copy,
+    )
     leaving = move.start(attended, attended_out)
     scaled_copy.wait()
+    settle()
     for step in range(rows // OWN):
         step_copy(step).wait()
     leaving.wait()
 
 
 def kernel_rest(
-    place, table, *refs
+    table, *refs
 ):
     vectors_in, refs = refs[:7], refs[7:]
     vectors, refs = refs[-7:], refs[:-7]
-    rest_body(place, table, vectors_in, vectors, *refs)
+    rest_body(table, vectors_in, vectors, *refs)
 
 
 def rest_body(
-    place, table, vectors_in, vectors,
-    x_in, cot_in, halo_in, triple_in, attended_in, scaled_in, stats_in, w_in_in, w_out_in, w_ex_in, w_sh_in,
-    middle_out, middle_grad_out, hidden_out, triple_grad_out, mine_out, other_out,
+    table, vectors_in, vectors,
+    x_in, cot_in, halo_in, triple_in, attended_in, scaled_in, raised_in, stats_in, w_in_in, w_out_in, w_ex_in, w_sh_in,
+    middle_out, middle_grad_out, hidden_out, triple_grad_out, edge_out, mine_out, other_out,
     x, back, w_in, w_out, w_ex, w_sh, triple, attended, middle, middle_grad, upstream, hidden, triple_grad, stats,
-    d_ex, d_sh, d_out, product, sums, small, scores, peaks, raised, scales, probs, scores_grads,
-    edge, mine, other, sems, tile_sems,
+    d_ex, d_sh, d_out, product, sums, small, scores, peaks, raised, scales, scaled_up, scores_grads,
+    kept, edge, mine, other, sems, tile_sems, kept_sems,
 ):
     rows, width = x_in.shape
     total = x.shape[0]
@@ -394,23 +435,22 @@
     move = Mover(sems)
     own, over = pl.ds(0, rows), pl.ds(rows, HALO)
     gain1, shift1, b_in, b_out, gain2, shift2, b_ex = vectors
-    vector_copies = [move.start(source, target) for source, target in zip(vectors_in, vectors)]
     near, far = pl.ds(2 * WIDE, rows - 2 * WIDE), pl.ds(0, 2 * WIDE)
+    first_copies = [move.start(halo_in.at[:, pl.ds(0, width)], x.at[over])]
+    first_copies += [move.start(source, target) for source, target in zip(vectors_in, vectors)]
+    first_copies.append(move.start(w_in_in, w_in))
     early = [
-        move.start(halo_in.at[:, pl.ds(0, width)], x.at[over]),
-        move.start(w_in_in, w_in),
         move.start(triple_in.at[near], triple.at[near]),
         move.start(stats_in, stats),
         move.start(attended_in, attended),
-    ] + vector_copies
+    ]
     late = [
         move.start(w_out_in, w_out),
         move.start(x_in, x.at[own]),
         move.start(cot_in, back.at[own]),
         move.start(halo_in.at[:, pl.ds(width, width)], back.at[over]),
-        move.start(w_ex_in, w_ex),
-        move.start(w_sh_in, w_sh),
     ]
+    weight_copies = [move.start(w_ex_in, w_ex), move.start(w_sh_in, w_sh)]
     last = move.start(triple_in.at[far], triple.at[far])
     rest = pl.ds(rows + HALO, total - rows - HALO)
     x[rest, :] = jnp.zeros((total - rows - HALO, width), BF16)
@@ -418,11 +458,29 @@
     for ref in (d_ex, d_sh, d_out, product, sums, small, triple_grad):
         ref[...] = jnp.zeros_like(ref)
     groups, first, end = table[GROUPS, 0], table[GROUPS, 1], table[GROUPS, 2]
+    for copy in first_copies:
+        copy.wait()
+    tail = pl.ds(rows, TILE)
+    edge_copy = move.start(x.at[tail], edge_out)
+    project_rows(x[tail, :].astype(F32), gain1, shift1, w_in, b_in, triple, tail, edge, slice(None))
     for copy in early:
         copy.wait()
-    tail = pl.ds(rows, TILE)
-    project_rows(x[tail, :].astype(F32), gain1, shift1, w_in, b_in, triple, tail, edge, slice(None))
     attend_groups(groups, table, triple, attended, stats, scores, peaks, raised, scales, alone=groups - 1)
+    def kept_copy(group, slot):
+        if group is None:
+            pltpu.make_async_copy(raised[0], kept.at[slot], kept_sems.at[slot]).wait()
+            return
+
+        @pl.when(group == groups - 1)
+        def _():
+            pltpu.make_async_copy(raised[0], kept.at[slot], kept_sems.at[slot]).start()
+
+        @pl.when(group != groups - 1)
+        def _():
+            pltpu.make_async_copy(raised_in.at[group], kept.at[slot], kept_sems.at[slot]).start()
+
+    for turn in range(3):
+        kept_copy(jnp.int32(turn), turn)
     for copy in late:
         copy.wait()
     leaving = []
@@ -489,19 +547,22 @@
         return 0
 
     lax.fori_loop(0, total // WIDE, before_feed, 0)
+    for copy in weight_copies:
+        copy.wait()
+    edge_copy.wait()
     scaled_copy = move.start(scaled_in, x.at[own])
     x[tail, :] = edge[...]
     leaving.append(move.start(middle, middle_out))
     lax.fori_loop(0, tiles, feed, 0)
     lax.fori_loop(0, total // WIDE, after_feed, 0)
-    core = place[2]
+    core = lax.rem(lax.axis_index("dp"), 2)
     for half, target in ((core, mine), (1 - core, other)):
         at = pack((d_out,), half, target, pack_turned(d_sh, half, target, pack((d_ex,), half, target, 0)))
     ready = pl.ds(0, at)
     leaving += [move.start(mine.at[ready], mine_out.at[ready]), move.start(other.at[ready], other_out.at[ready])]
     last.wait()
     attend_back_groups(
-        groups, table, triple, attended, upstream, stats, triple_grad, probs, scores_grads
+        groups, table, triple, attended, upstream, stats, triple_grad, scores_grads, scaled_up, kept, kept_copy
     )
     leaving.append(move.start(triple_grad, triple_grad_out))
     scaled_copy.wait()
@@ -600,7 +661,7 @@
 
 
 def kernel_input(
-    after, gain1, x_in, halo_in, w_in_in, triple_grad_in, middle_grad_in, out, out_halo,
+    after, gain1, x_in, edge_in, w_in_in, triple_grad_in, middle_grad_in, out, out_halo,
     x, w_in, triple_grad, middle_grad, sems, step_sems,
 ):
     rows, width = x_in.shape
@@ -609,7 +670,7 @@
     early = [
         move.start(w_in_in, w_in),
         move.start(x_in, x.at[pl.ds(0, rows)]),
-        move.start(halo_in.at[:, pl.ds(0, width)], x.at[pl.ds(rows, HALO)]),
+        move.start(edge_in, x.at[pl.ds(rows, TILE)]),
     ]
     arrays = ((triple_grad_in, triple_grad), (middle_grad_in, middle_grad))
     steps = range(total // WIDE)
@@ -617,7 +678,6 @@
     for part in parts:
         for copy in part:
             copy.start()
-    x[pl.ds(rows + HALO, total - rows - HALO), :] = jnp.zeros((total - rows - HALO, width), BF16)
     for copy in early:
         copy.wait()
     leaving = []
@@ -705,7 +765,7 @@
     pltpu.make_async_copy(parts, out, sems.at[4]).wait()
 
 
-def kernel_unpack_half(where, packed_in, d_ex, d_out, d_in, d_sh, packed, ex, out, inward, sh, sems):
+def kernel_unpack_half(half, packed_in, d_ex, d_out, d_in, d_sh, packed, ex, out, inward, sh, sems):
     arrays = ((ex, d_ex), (sh, d_sh), (out, d_out), (inward, d_in))
     sizes = [value.shape[0] * value.shape[1] // LANES for value, _target in arrays]
     begins = [sum(sizes[:index]) for index in range(4)]
@@ -714,7 +774,6 @@
         spot = pl.ds(begins[index], sizes[index])
         arriving.append(pltpu.make_async_copy(packed_in.at[spot], packed.at[spot], sems.at[index]))
         arriving[-1].start()
-    half = where[0]
     leaving = []
     for index, (value, target) in enumerate(arrays):
         arriving[index].wait()
@@ -735,13 +794,17 @@
     return leaving
 
 
-def kernel_first_half(where, packed_in, *refs):
-    for copy in kernel_unpack_half(where, packed_in, *refs):
+def own_core():
+    return lax.rem(lax.axis_index("dp"), 2)
+
+
+def kernel_first_half(packed_in, *refs):
+    for copy in kernel_unpack_half(own_core(), packed_in, *refs):
         copy.wait()
 
 
 def kernel_second_half(
-    where, packed_in, first_in, kept_ex, kept_out, kept_in, kept_sh,
+    packed_in, first_in, kept_ex, kept_out, kept_in, kept_sh,
     d_ex, d_out, d_in, d_sh, b_in, b_sh, gain2, shift2, b_out, b_ex, gain1, shift1,
     packed, ex, out, inward, sh, sems, mine, other, small_sems,
 ):
@@ -753,11 +816,14 @@
     ]
     for copy in copies:
         copy.start()
-    leaving = kernel_unpack_half(where, packed_in, d_ex, d_out, d_in, d_sh, packed, ex, out, inward, sh, sems)
+    core = own_core()
+    leaving = kernel_unpack_half(
+        1 - core, packed_in, d_ex, d_out, d_in, d_sh, packed, ex, out, inward, sh, sems
+    )
     for copy in copies:
         copy.wait()
     width, columns = b_sh.shape[0], b_ex.shape[0]
-    swap = where[0] == 0
+    swap = core == 1
     blocks = []
     for index in range(columns // LANES):
         spot = pl.ds(index // 2 * 16, 16)
@@ -808,9 +874,10 @@
     ]
 
 
-def own_part(place, segments, gain1, shift1, b_in, x, w_in):
+def own_part(segments, gain1, shift1, b_in, x, w_in):
     rows, width = x.shape
     total = rows + TILE
+    pairs = width // (2 * HD)
     vmem = pltpu.VMEM
     return pl.pallas_call(
         kernel_own,
@@ -818,11 +885,12 @@
             shape((rows, 3 * width), BF16),
             shape((total, width), BF16),
             shape((rows, width), BF16),
+            shape((GROUPS, pairs, 2 * WIN, WIN), BF16),
             shape((GROUPS, 8, WIN), F32),
             shape((GROUPS + 1, 8), jnp.int32),
         ),
-        in_specs=[SMEM] + [ANY] * 6,
-        out_specs=(ANY, ANY, ANY, VMEM, SMEM),
+        in_specs=[ANY] * 6,
+        out_specs=(ANY, ANY, ANY, ANY, VMEM, SMEM),
         scratch_shapes=[
             vmem(segments.shape, jnp.int32),
             vmem(gain1.shape, F32),
@@ -834,17 +902,18 @@
             vmem((total, width), BF16),
             vmem((8, LANES), jnp.int32),
             pltpu.SMEM((8, LANES), jnp.int32),
-            *attention_scratch(width // (2 * HD)),
+            *attention_scratch(pairs),
+            vmem((GROUPS, pairs, 2 * WIN, WIN), BF16),
             pltpu.SemaphoreType.DMA((16,)),
-            pltpu.SemaphoreType.DMA((rows // OWN,)),
+            pltpu.SemaphoreType.DMA((rows // OWN + 1,)),
         ],
         compiler_params=params(63),
         cost_estimate=cost(2 * 6 * rows * width * 3 * width, 1e7),
         name="own_part",
-    )(place, segments, gain1, shift1, b_in, x, w_in)
-
-
-def rest_part(place, table, vectors, x, cot, halo, triple, attended, scaled, stats, w_in, w_out, w_ex, w_sh, pieces):
+    )(segments, gain1, shift1, b_in, x, w_in)
+
+
+def rest_part(table, vectors, x, cot, halo, triple, attended, scaled, raised, stats, w_in, w_out, w_ex, w_sh, pieces):
     rows, width = x.shape
     total = rows + TILE
     hidden = w_ex.shape[1]
@@ -860,11 +929,12 @@
             shape((total, width), F32),
             shape((total, hidden), BF16),
             shape((total, 3 * width), BF16),
+            shape((TILE, width), BF16),
             shape((packed, LANES), BF16),
             shape((packed, LANES), BF16),
         ),
-        in_specs=[SMEM, SMEM] + [ANY] * 18,
-        out_specs=tuple([ANY] * 6),
+        in_specs=[SMEM] + [ANY] * 19,
+        out_specs=tuple([ANY] * 7),
         scratch_shapes=[
             vmem((total, width), BF16),
             vmem((total, width), BF16),
@@ -890,19 +960,21 @@
             [row],
             [vmem((pairs, 2 * WIN, WIN), BF16)],
             [row],
+            [vmem((pairs, 2 * HD, WIN), BF16)] * 2,
             [low] * 2,
-            [low] * 2,
+            vmem((SLOTS, pairs, 2 * WIN, WIN), BF16),
             vmem((TILE, width), BF16),
             vmem((packed, LANES), BF16),
             vmem((packed, LANES), BF16),
             pltpu.SemaphoreType.DMA((40,)),
             pltpu.SemaphoreType.DMA((2,)),
+            pltpu.SemaphoreType.DMA((SLOTS,)),
             *[vmem(v.shape, F32) for v in vectors],
         ],
         compiler_params=params(62),
         cost_estimate=cost(2 * 9 * rows * width * (3 * width + 8 * width), 3e7),
         name="rest_part",
-    )(place, table, *vectors, x, cot, halo, triple, attended, scaled, stats, w_in, w_out, w_ex, w_sh)
+    )(table, *vectors, x, cot, halo, triple, attended, scaled, raised, stats, w_in, w_out, w_ex, w_sh)
 
 
 def input_gradient(after, gain1, x, halo, w_in, triple_grad, middle_grad):
@@ -988,38 +1060,38 @@
     return tuple(shape(dim, F32) for dim in dims), [*scratch, pltpu.SemaphoreType.DMA((8,))]
 
 
-def unpack_first(half, packed, width, hidden):
+def unpack_first(packed, width, hidden):
     shapes, scratch = half_shapes(width, hidden)
     return pl.pallas_call(
         kernel_first_half,
         out_shape=shapes,
-        in_specs=[SMEM, ANY],
+        in_specs=[ANY],
         out_specs=(ANY,) * 4,
         scratch_shapes=[pltpu.VMEM(packed.shape, BF16), *scratch],
         compiler_params=params(63),
         cost_estimate=cost(packed.size, packed.size * 6),
         name="unpack_first",
-    )(half, packed)
-
-
-def unpack_second(half, packed, first, kept, used, width, hidden):
+    )(packed)
+
+
+def unpack_second(packed, first, kept, used, width, hidden):
     shapes, scratch = half_shapes(width, hidden)
     rows = first.shape[0] - used
     small = tuple(shape(dims, F32) for dims in ((2, width),) + ((width,),) * 4 + ((hidden,), (width,), (width,)))
     return pl.pallas_call(
         kernel_second_half,
         out_shape=shapes + small,
-        in_specs=[SMEM] + [ANY] * 6,
+        in_specs=[ANY] * 6,
         out_specs=(ANY,) * 4 + (VMEM,) * 8,
         scratch_shapes=[
             pltpu.VMEM(packed.shape, BF16), *scratch, pltpu.VMEM((rows, LANES), BF16), pltpu.VMEM((rows, LANES), BF16),
             pltpu.SemaphoreType.DMA((2,)),
         ],
-        input_output_aliases={3: 0, 4: 1, 5: 2, 6: 3},
+        input_output_aliases={2: 0, 3: 1, 4: 2, 5: 3},
         compiler_params=params(63),
         cost_estimate=cost(packed.size, packed.size * 6),
         name="unpack_second",
-    )(half, packed, first, *kept)
+    )(packed, first, *kept)
 
 
 def touch(value, *after):
@@ -1091,24 +1163,21 @@
 ):
     rows, width = layer_input.shape
     hidden_width = expand_weight.shape[1]
-    position = lax.axis_index("mp")
-    core = lax.axis_index("dp") % 2
     pieces = lax.axis_size("dp") * lax.axis_size("mp") // 2
-    place = jnp.stack([position, position, core]).astype(jnp.int32)
     gain1, shift1, b_out, gain2, shift2, b_ex, b_sh = (
         first_gain, first_shift, outward_bias, second_gain, second_shift, expand_bias, shrink_bias
     )
     halo = passed(jnp.concatenate([layer_input[:HALO], cotangent[:HALO]], axis=1), -1)
-    triple, attended, scaled, stats, table = own_part(
-        place, segments, gain1, shift1, inward_bias, layer_input, inward_weight
+    triple, attended, scaled, raised, stats, table = own_part(
+        segments, gain1, shift1, inward_bias, layer_input, inward_weight
     )
-    middle, middle_grad, hidden, triple_grad, mine, other = rest_part(
-        place, table, (gain1, shift1, inward_bias, b_out, gain2, shift2, b_ex), layer_input, cotangent, halo, triple,
-        attended, scaled, stats, inward_weight, outward_weight, expand_weight, shrink_weight, pieces,
+    middle, middle_grad, hidden, triple_grad, edge, mine, other = rest_part(
+        table, (gain1, shift1, inward_bias, b_out, gain2, shift2, b_ex), layer_input, cotangent, halo, triple,
+        attended, scaled, raised, stats, inward_weight, outward_weight, expand_weight, shrink_weight, pieces,
     )
     both = add_halves(mine, swap_cores(other))
     parts = exchange(both.reshape(pieces, -1, LANES))
-    input_grad, input_halo = input_gradient(both, gain1, layer_input, halo, inward_weight, triple_grad, middle_grad)
+    input_grad, input_halo = input_gradient(both, gain1, layer_input, edge, inward_weight, triple_grad, middle_grad)
     result, result_halo = layer_result(input_halo, table, b_sh, middle, hidden, shrink_weight)
     input_other = passed(input_halo[:HALO], 1)
     summed = sum_parts((input_other, result_halo), parts)
@@ -1118,9 +1187,9 @@
     mine = touch(mine, input_grad, result)
     other = swap_cores(mine)
     used = 192 * (2 * hidden_width + 4 * width) // LANES
-    half = unpack_first(place[2:], mine, width, hidden_width)
+    half = unpack_first(mine, width, hidden_width)
     d_ex, d_out, d_in, d_sh, d_b_in, d_b_sh, d_gain2, d_shift2, d_b_out, d_b_ex, d_gain1, d_shift1 = unpack_second(
-        1 - place[2:], other, mine, half, used, width, hidden_width
+        other, mine, half, used, width, hidden_width
     )
     return (
         result, input_grad, d_gain1, d_shift1, d_in, d_b_in, d_out, d_b_out, d_gain2, d_shift2, d_ex, d_b_ex, d_sh,

time: 179 us -> 175 us (0.978)
  Pallas kernels: 112 us -> 106 us
  starting transfers between devices: 36.4 us -> 40 us
    pallas_call x1, Pallas kernels: 56.5 us -> 50.6 us  [rest_part(): pl.pallas_call(kernel_rest, out_shape=(shape((total, width), F32), shape(...]
    ppermute x2, starting transfers between devices: 4.43 us -> 7.88 us  [swap_cores(): return lax.ppermute(block, 'dp', [(i, i ^ 1) for i in range(packs)])]
  transfers between devices with their start and end apart: 7 -> 7, of which waited for: 6 -> 6; matrix products, arithmetic and copies ran while one was open for 1% -> 1% of each run, Pallas kernels for 26% -> 27%
where the time goes in v5:
time: 175 us; the launch traced here: 174 us
  Pallas kernels  106 us (61%)
  starting transfers between devices  40 us (23%)
  waiting for transfers between devices  21.8 us (12%)
  local copies, waits for them, and re-layouts  5.43 us (3%)
    pallas_call x1, Pallas kernels, rest_part(): pl.pallas_call(kernel_rest, out_shape=(shape((total, width), F32), shape(...  50.6 us
    all_to_all x2, starting transfers between devices, exchange(): lax.all_to_all(parts, ('dp', 'mp'), 0, 0, axis_index_groups=same_core_gro...  25.1 us
    pallas_call x1, Pallas kernels, own_part(): pl.pallas_call(kernel_own, out_shape=(shape((rows, 3 * width), BF16), sha...  17.7 us
    ppermute x3, waiting for transfers between devices, passed(): return lax.ppermute(block, 'mp', route)  16.6 us
    pallas_call x1, Pallas kernels, input_gradient(): pl.pallas_call(kernel_input, out_shape=(shape((rows, width), F32), shape(...  10.3 us
    pallas_call x1, Pallas kernels, layer_result(): pl.pallas_call(kernel_result, out_shape=(shape((total - TILE, width), BF1...  9.91 us
    ppermute x2, starting transfers between devices, swap_cores(): return lax.ppermute(block, 'dp', [(i, i ^ 1) for i in range(packs)])  7.88 us
    ppermute x3, starting transfers between devices, passed(): return lax.ppermute(block, 'mp', route)  7.02 us
  transfers between devices with their start and end apart: 7, of which 6 were waited for; matrix products, arithmetic and copies ran while one was open for 1% of the time, Pallas kernels for 27%

profile of v5, /device:TPU:1, one launch (start us, length us, event | category | flops | bytes accessed | tf_op | source)
XLA Modules:
  0.0 174.5 jit_solution(9897121581171189682)
XLA Ops:
  0.6 0.9 slice.13
  1.6 0.9 slice.12
  2.6 1.3 collective-permute-start
  3.9 17.7 %own_part.1 = (bf16[2048,1152]{1,0:T(8,128)(2,1)}, bf16[2304,384]{1,0:T(8,128)(2,1)}, bf16[2048,384]{1,0:T(8,128)(2,1)}, bf16[24,3,512,256]{3,2,1,0:T(8,128)(2,1...) custom-call(s32[1,8192]{1,0:T(1,128)} %seg_in.1, f32[384]{0:T(512)} %gain1.1, f32[384]{0:T(512)} %refs_1_.1, f32[2,384]{1,0:T(2,128)} %refs_2_.1, ...), custom_call_target="tpu_custom_call" | custom-call | flops 10871635968 | bytes 10000000 | tf_op jit(solution)/shard_map/own_part/pallas_call | solution.py:882
  22.3 50.6 %rest_part.1 = (f32[2304,384]{1,0:T(8,128)}, f32[2304,384]{1,0:T(8,128)}, bf16[2304,1536]{1,0:T(8,128)(2,1)}, bf16[2304,1152]{1,0:T(8,128)(2,1)}, bf16[256,384]{...) custom-call(s32[25,8]{1,0:T(8,128)} %get-tuple-element.47.table, f32[384]{0:T(512)} %gain1.1, ...), custom_call_target="tpu_custom_call" | custom-call | flops 59793997824 | bytes 30000000 | tf_op jit(solution)/shard_map/rest_part/pallas_call | solution.py:925
  72.9 3.5 %collective-permute-start.1 = (bf16[7168,128]{1,0:T(8,128)(2,1)}, bf16[7168,128]{1,0:T(8,128)(2,1)}, u32[]{:S(2)}, u32[]{:S(2)}) collective-permute-start(bf16[7168,128]{1,0:T(8,128)(2,1)} %get-tuple-element.54), channel_id=1, source_target_pairs={{0,4},{4,0},{8,12},{12,8},{16,20},{20,16},{24,28},{28,24},{32,36},... | collective-permute-start | bytes 5505032 | tf_op jit(solution)/shard_map/ppermute | solution.py:1115
  76.4 3.8 %collective-permute-done.1.other_in = bf16[7168,128]{1,0:T(8,128)(2,1)} collective-permute-done((bf16[7168,128]{1,0:T(8,128)(2,1)}, bf16[7168,128]{1,0:T(8,128)(2,1)}, u32[]{:S(2)}, u32[]{:S(2)}) %collective-permute-start.1) | collective-permute-done | bytes 1835040 | tf_op jit(solution)/shard_map/ppermute | solution.py:1115
  80.1 3.0 %add_halves.1.after = bf16[7168,128]{1,0:T(8,128)(2,1)} custom-call(bf16[7168,128]{1,0:T(8,128)(2,1)} %get-tuple-element.53.mine_in, bf16[7168,128]{1,0:T(8,128)(2,1)} %collective-permute-done.1.other_in), custom_call_target="tpu_custom_call" | custom-call | flops 917504 | bytes 5505024 | tf_op jit(solution)/shard_map/add_halves/pallas_call | solution.py:1026
  83.1 13.7 %all-to-all-start = ((bf16[64,112,128]{2,1,0:T(8,128)(2,1)}), bf16[64,112,128]{2,1,0:T(8,128)(2,1)}, u32[]{:S(2)}, u32[]{:S(2)}) async-start(bf16[64,112,128]{2,1,0:T(8,128)(2,1)} %bitcast.2), calls=%async_computation | async-start | bytes 3670016 | tf_op jit(solution)/shard_map/all_to_all | solution.py:1119
  96.8 10.3 %input_gradient.1 = (f32[2048,384]{1,0:T(8,128)}, f32[256,384]{1,0:T(8,128)}) custom-call(bf16[7168,128]{1,0:T(8,128)(2,1)} %add_halves.1.after, f32[384]{0:T(512)} %gain1.1, bf16[2048,384]{1,0:T(8,128)(2,1)} %x_in.3, bf16[256,384]{1,0:T(8,128)(2,1)} %get-tuple-element.55.edge_in, bf16[384,1152]{1,0:T(8,128)(2,1)} %w_in_in.3, ...), custom_call_target="tpu_custom_call" | custom-call | flops 5435817984 | bytes 14000000 | tf_op jit(solution)/shard_map/input_gradient/pallas_call | solution.py:984
  107.1 1.0 slice.14
  108.1 2.9 %collective-permute-start.2 = (f32[208,384]{1,0:T(8,128)S(1)}, f32[208,384]{1,0:T(8,128)S(1)}, u32[]{:S(2)}, u32[]{:S(2)}) collective-permute-start(f32[208,384]{1,0:T(8,128)S(1)} %slice.14), channel_id=1, source_target_pairs={{0,1},{1,2},{2,3},{4,5},{5,6},{6,7},{8,9},{9,10},{10,11},{12,13},{... | collective-permute-start | bytes 958472 | tf_op jit(solution)/shard_map/ppermute | solution.py:1125
  111.0 9.9 %layer_result.1 = (bf16[2048,384]{1,0:T(8,128)(2,1)}, bf16[256,384]{1,0:T(8,128)(2,1)}) custom-call(f32[256,384]{1,0:T(8,128)} %get-tuple-element.58.after, s32[25,8]{1,0:T(8,128)} %get-tuple-element.47.table, f32[384]{0:T(512)} %b_sh.1, f32[2304,384]{1,0:T(8,128)} %get-tuple-element.59.middle_in, bf16[2304,1536]{1,0:T(8,128)(2,1)} %get-tuple-element.60.hidden_in, ...), custom_call_target="tpu_custom_call" | custom-call | flops 5435817984 | bytes 13000000 | tf_op jit(solution)/shard_map/layer_result/pallas_call | solution.py:1006
  120.9 1.7 collective-permute-done.2.refs_0_
  123.3 2.7 %sum_parts.1.refs_1_ = bf16[64,112,128]{2,1,0:T(8,128)(2,1)} custom-call(f32[208,384]{1,0:T(8,128)} %copy-done, bf16[256,384]{1,0:T(8,128)(2,1)} %get-tuple-element.62.refs_1_.refs_0_, bf16[64,112,128]{2,1,0:T(8,128)(2,1)} %all-to-all-done.refs_2_), custom_call_target="tpu_custom_call" | custom-call | flops 917504 | bytes 3670016 | tf_op jit(solution)/shard_map/sum_parts/pallas_call | solution.py:1041
  126.0 11.3 %all-to-all-start.1 = ((bf16[64,112,128]{2,1,0:T(8,128)(2,1)}), bf16[64,112,128]{2,1,0:T(8,128)(2,1)}, u32[]{:S(2)}, u32[]{:S(2)}) async-start(bf16[64,112,128]{2,1,0:T(8,128)(2,1)} %sum_parts.1.refs_1_), calls=%async_computation.1 | async-start | bytes 3670016 | tf_op jit(solution)/shard_map/all_to_all | solution.py:1119
  137.4 0.9 slice.16
  138.3 2.9 %collective-permute-start.3 = (bf16[208,384]{1,0:T(8,128)(2,1)S(1)}, bf16[208,384]{1,0:T(8,128)(2,1)S(1)}, u32[]{:S(2)}, u32[]{:S(2)}) collective-permute-start(bf16[208,384]{1,0:T(8,128)(2,1)S(1)} %slice.16), channel_id=1, source_target_pairs={{0,1},{1,2},{2,3},{4,5},{5,6},{6,7},{8,9},{9,10},{10,11},{12,13},{... | collective-permute-start | bytes 479240 | tf_op jit(solution)/shard_map/ppermute | solution.py:1125
  141.2 2.8 %take_over.3.refs_1_ = f32[2048,384]{1,0:T(8,128)} custom-call(s32[25,8]{1,0:T(8,128)} %get-tuple-element.47.table, f32[2048,384]{1,0:T(8,128)} %get-tuple-element.63.own_in, f32[208,384]{1,0:T(8,128)} %touch.4.other_in), custom_call_target="tpu_custom_call", output_to_operand_aliasing={{}: (1, {})} | custom-call | tf_op jit(solution)/shard_map/take_over/pallas_call | solution.py:1146
  143.9 14.9 %collective-permute-done.3.other_in = bf16[208,384]{1,0:T(8,128)(2,1)S(1)} collective-permute-done((bf16[208,384]{1,0:T(8,128)(2,1)S(1)}, bf16[208,384]{1,0:T(8,128)(2,1)S(1)}, u32[]{:S(2)}, u32[]{:S(2)}) %collective-permute-start.3) | collective-permute-done | bytes 159776 | tf_op jit(solution)/shard_map/ppermute | solution.py:1125
  159.5 2.6 %take_over.2.refs_2_ = bf16[2048,384]{1,0:T(8,128)(2,1)} custom-call(s32[25,8]{1,0:T(8,128)} %get-tuple-element.47.table, bf16[2048,384]{1,0:T(8,128)(2,1)} %get-tuple-element.61.own_in, bf16[208,384]{1,0:T(8,128)(2,1)} %copy-done.1), custom_call_target="tpu_custom_call", output_to_operand_aliasing={{}: (1, {})} | custom-call | tf_op jit(solution)/shard_map/take_over/pallas_call | solution.py:1146
  162.5 4.3 %collective-permute-start.4 = (bf16[7168,128]{1,0:T(8,128)(2,1)}, bf16[7168,128]{1,0:T(8,128)(2,1)}, u32[]{:S(2)}, u32[]{:S(2)}) collective-permute-start(bf16[7168,128]{1,0:T(8,128)(2,1)} %touch.5.packed_in.first_in), channel_id=1, source_target_pairs={{0,4},{4,0},{8,12},{12,8},{16,20},{20,16},{24,28},{28,24},{32,36},... | collective-permute-start | bytes 5505032 | tf_op jit(solution)/shard_map/ppermute | solution.py:1115
  166.9 3.0 %unpack_first.1 = (f32[384,1536]{1,0:T(8,128)}, f32[384,384]{1,0:T(8,128)}, f32[384,1152]{1,0:T(8,128)}, f32[1536,384]{1,0:T(8,128)}) custom-call(bf16[7168,128]{1,0:T(8,128)(2,1)} %touch.5.packed_in.first_in), custom_call_target="tpu_custom_call" | custom-call | flops 917504 | bytes 5505024 | tf_op jit(solution)/shard_map/unpack_first/pallas_call | solution.py:1065
  170.6 3.7 %unpack_second.1 = (f32[384,1536]{1,0:T(8,128)}, f32[384,384]{1,0:T(8,128)}, f32[384,1152]{1,0:T(8,128)}, f32[1536,384]{1,0:T(8,128)}, f32[2,384]{1,0:T(2,128)},...) custom-call(bf16[7168,128]{1,0:T(8,128)(2,1)} %collective-permute-do, ...), custom_call_target="tpu_custom_call", output_to_operand_aliasing={{0}: (2, {}), {1}: (3, {}), {2}: (4, {}), {3}: (5, {})} | custom-call | flops 917504 | bytes 5505024 | tf_op jit(solution)/shard_map/unpack_second/pallas_call | solution.py:1081
  (14 shorter events, 3.2 us)
Async XLA Ops:
  2.6 19.0 %collective-permute-start = (bf16[208,768]{1,0:T(8,128)(2,1)S(1)}, bf16[208,768]{1,0:T(8,128)(2,1)S(1)}, u32[]{:S(2)}, u32[]{:S(2)}) collective-permute-start(bf16[208,768]{1,0:T(8,128)(2,1)S(1)} %pad_maximum_fusion), channel_id=1, source_target_pairs={{1,0},{2,1},{3,2},{5,4},{6,5},{7,6},{9,8},{10,9},{11,10},{13,12},{... | collective-permute-start | bytes 958472 | tf_op jit(solution)/shard_map/ppermute | solution.py:1125
  21.6 0.7 copy-start.2
  72.9 7.3 %collective-permute-start.1 = (bf16[7168,128]{1,0:T(8,128)(2,1)}, bf16[7168,128]{1,0:T(8,128)(2,1)}, u32[]{:S(2)}, u32[]{:S(2)}) collective-permute-start(bf16[7168,128]{1,0:T(8,128)(2,1)} %get-tuple-element.54), channel_id=1, source_target_pairs={{0,4},{4,0},{8,12},{12,8},{16,20},{20,16},{24,28},{28,24},{32,36},... | collective-permute-start | bytes 5505032 | tf_op jit(solution)/shard_map/ppermute | solution.py:1115
  83.1 39.9 %all-to-all-start = ((bf16[64,112,128]{2,1,0:T(8,128)(2,1)}), bf16[64,112,128]{2,1,0:T(8,128)(2,1)}, u32[]{:S(2)}, u32[]{:S(2)}) async-start(bf16[64,112,128]{2,1,0:T(8,128)(2,1)} %bitcast.2), calls=%async_computation | async-start | bytes 3670016 | tf_op jit(solution)/shard_map/all_to_all | solution.py:1119
  108.1 14.4 %collective-permute-start.2 = (f32[208,384]{1,0:T(8,128)S(1)}, f32[208,384]{1,0:T(8,128)S(1)}, u32[]{:S(2)}, u32[]{:S(2)}) collective-permute-start(f32[208,384]{1,0:T(8,128)S(1)} %slice.14), channel_id=1, source_target_pairs={{0,1},{1,2},{2,3},{4,5},{5,6},{6,7},{8,9},{9,10},{10,11},{12,13},{... | collective-permute-start | bytes 958472 | tf_op jit(solution)/shard_map/ppermute | solution.py:1125
  122.6 0.7 copy-start
  126.0 36.5 %all-to-all-start.1 = ((bf16[64,112,128]{2,1,0:T(8,128)(2,1)}), bf16[64,112,128]{2,1,0:T(8,128)(2,1)}, u32[]{:S(2)}, u32[]{:S(2)}) async-start(bf16[64,112,128]{2,1,0:T(8,128)(2,1)} %sum_parts.1.refs_1_), calls=%async_computation.1 | async-start | bytes 3670016 | tf_op jit(solution)/shard_map/all_to_all | solution.py:1119
  138.3 20.6 %collective-permute-start.3 = (bf16[208,384]{1,0:T(8,128)(2,1)S(1)}, bf16[208,384]{1,0:T(8,128)(2,1)S(1)}, u32[]{:S(2)}, u32[]{:S(2)}) collective-permute-start(bf16[208,384]{1,0:T(8,128)(2,1)S(1)} %slice.16), channel_id=1, source_target_pairs={{0,1},{1,2},{2,3},{4,5},{5,6},{6,7},{8,9},{9,10},{10,11},{12,13},{... | collective-permute-start | bytes 479240 | tf_op jit(solution)/shard_map/ppermute | solution.py:1125
  158.9 0.7 copy-start.1
  162.5 8.1 %collective-permute-start.4 = (bf16[7168,128]{1,0:T(8,128)(2,1)}, bf16[7168,128]{1,0:T(8,128)(2,1)}, u32[]{:S(2)}, u32[]{:S(2)}) collective-permute-start(bf16[7168,128]{1,0:T(8,128)(2,1)} %touch.5.packed_in.first_in), channel_id=1, source_target_pairs={{0,4},{4,0},{8,12},{12,8},{16,20},{20,16},{24,28},{28,24},{32,36},... | collective-permute-start | bytes 5505032 | tf_op jit(solution)/shard_map/ppermute | solution.py:1115

commit v6 on v5

--- a/solution.py
+++ b/solution.py
@@ -436,7 +436,7 @@
     own, over = pl.ds(0, rows), pl.ds(rows, HALO)
     gain1, shift1, b_in, b_out, gain2, shift2, b_ex = vectors
     near, far = pl.ds(2 * WIDE, rows - 2 * WIDE), pl.ds(0, 2 * WIDE)
-    first_copies = [move.start(halo_in.at[:, pl.ds(0, width)], x.at[over])]
+    first_copies = [move.start(halo_in.at[pl.ds(0, HALO)], x.at[over])]
     first_copies += [move.start(source, target) for source, target in zip(vectors_in, vectors)]
     first_copies.append(move.start(w_in_in, w_in))
     early = [
@@ -448,7 +448,7 @@
         move.start(w_out_in, w_out),
         move.start(x_in, x.at[own]),
         move.start(cot_in, back.at[own]),
-        move.start(halo_in.at[:, pl.ds(width, width)], back.at[over]),
+        move.start(halo_in.at[pl.ds(HALO, HALO)], back.at[over]),
     ]
     weight_copies = [move.start(w_ex_in, w_ex), move.start(w_sh_in, w_sh)]
     last = move.start(triple_in.at[far], triple.at[far])
@@ -640,30 +640,29 @@
             other[spot, :] = value
 
 
-def step_copies(arrays, step, sems):
+def step_copies(arrays, step, sems, skip=0):
     spot = pl.ds(step * WIDE, WIDE)
     return [
-        pltpu.make_async_copy(source.at[spot], target.at[spot], sems.at[step, at])
+        pltpu.make_async_copy(source.at[spot], target.at[spot], sems.at[step, skip + at])
         for at, (source, target) in enumerate(arrays)
     ]
 
 
-def leave(value_ref, own_out, halo_out, step, sems):
+def leave(value_ref, own_out, step, sem):
     rows = own_out.shape[0]
-    begin, end = step * WIDE, (step + 1) * WIDE
-    own = pl.ds(begin, min(rows, end) - begin)
-    copies = [pltpu.make_async_copy(value_ref.at[own], own_out.at[own], sems.at[step, 6])]
-    if end > rows:
-        copies.append(pltpu.make_async_copy(value_ref.at[pl.ds(rows, end - rows)], halo_out, sems.at[step, 7]))
-    for copy in copies:
-        copy.start()
-    return copies
-
-
-def kernel_input(
-    after, gain1, x_in, edge_in, w_in_in, triple_grad_in, middle_grad_in, out, out_halo,
-    x, w_in, triple_grad, middle_grad, sems, step_sems,
+    begin = step * WIDE
+    own = pl.ds(begin, min(rows, begin + WIDE) - begin)
+    copy = pltpu.make_async_copy(value_ref.at[own], own_out.at[own], sem)
+    copy.start()
+    return copy
+
+
+def kernel_rows(
+    after, table, gain1, b_sh, x_in, edge_in, w_in_in, triple_grad_in, middle_grad_in, middle_in, hidden_in, w_sh_in,
+    input_out, result_out, halo_out,
+    x, w_in, triple_grad, middle_grad, middle, hidden, w_sh, result, halo, sems, step_sems,
 ):
+    del after
     rows, width = x_in.shape
     total = x.shape[0]
     move = Mover(sems)
@@ -672,10 +671,15 @@
         move.start(x_in, x.at[pl.ds(0, rows)]),
         move.start(edge_in, x.at[pl.ds(rows, TILE)]),
     ]
-    arrays = ((triple_grad_in, triple_grad), (middle_grad_in, middle_grad))
+    arrays = ((triple_grad_in, triple_grad), (middle_grad_in, middle_grad), (middle_in, middle), (hidden_in, hidden))
     steps = range(total // WIDE)
-    parts = [step_copies(arrays, step, step_sems) for step in steps]
+    parts = [step_copies(arrays[:2], step, step_sems) for step in steps]
     for part in parts:
+        for copy in part:
+            copy.start()
+    weight_copy = move.start(w_sh_in, w_sh)
+    more = [step_copies(arrays[2:], step, step_sems, 2) for step in steps]
+    for part in more:
         for copy in part:
             copy.start()
     for copy in early:
@@ -688,33 +692,20 @@
         scaled, inverse = normalize(x[spot, :].astype(F32))
         normed_grad = dot_nt(triple_grad[spot, :], w_in[...])
         middle_grad[spot, :] = middle_grad[spot, :] + normalize_back(normed_grad, scaled, inverse, row_of(gain1))
-        leaving += leave(middle_grad, out, out_halo, step, step_sems)
-    for copy in leaving:
-        copy.wait()
-
-
-def kernel_result(
-    after, table, b_sh, middle_in, hidden_in, w_sh_in, out, out_halo, middle, hidden, w_sh, value, sems, step_sems,
-):
-    total = middle.shape[0]
-    move = Mover(sems)
-    weight_copy = move.start(w_sh_in, w_sh)
-    arrays = ((middle_in, middle), (hidden_in, hidden))
-    steps = range(total // WIDE)
-    parts = [step_copies(arrays, step, step_sems) for step in steps]
-    for part in parts:
-        for copy in part:
-            copy.start()
+        leaving.append(leave(middle_grad, input_out, step, step_sems.at[step, 4]))
     weight_copy.wait()
-    leaving = []
     for step in steps:
-        for copy in parts[step]:
+        for copy in more[step]:
             copy.wait()
         spot = pl.ds(step * WIDE, WIDE)
         keep = interval(step, table[GROUPS, 1], table[GROUPS, 2], WIDE)
         row = middle[spot, :] + row_of(b_sh) + dot(hidden[spot, :], w_sh[...])
-        value[spot, :] = jnp.where(keep, row, 0.0).astype(BF16)
-        leaving += leave(value, out, out_halo, step, step_sems)
+        result[spot, :] = jnp.where(keep, row, 0.0).astype(BF16)
+        leaving.append(leave(result, result_out, step, step_sems.at[step, 5]))
+    over = pl.ds(rows, HALO)
+    halo[:HALO, :] = middle_grad[over, :].astype(BF16)
+    halo[HALO:, :] = result[over, :]
+    leaving.append(move.start(halo, halo_out))
     for copy in leaving:
         copy.wait()
 
@@ -977,49 +968,32 @@
     )(table, *vectors, x, cot, halo, triple, attended, scaled, raised, stats, w_in, w_out, w_ex, w_sh)
 
 
-def input_gradient(after, gain1, x, halo, w_in, triple_grad, middle_grad):
+def row_outputs(after, table, gain1, b_sh, x, edge, w_in, triple_grad, middle_grad, middle, hidden, w_sh):
     rows, width = x.shape
     total = triple_grad.shape[0]
     vmem = pltpu.VMEM
     return pl.pallas_call(
-        kernel_input,
-        out_shape=(shape((rows, width), F32), shape((TILE, width), F32)),
-        in_specs=[ANY, VMEM] + [ANY] * 5,
-        out_specs=(ANY, ANY),
+        kernel_rows,
+        out_shape=(shape((rows, width), F32), shape((rows, width), BF16), shape((2 * HALO, width), BF16)),
+        in_specs=[ANY, SMEM, VMEM, VMEM] + [ANY] * 8,
+        out_specs=(ANY, ANY, ANY),
         scratch_shapes=[
             vmem((total, width), BF16),
             vmem(w_in.shape, BF16),
             vmem((total, 3 * width), BF16),
             vmem((total, width), F32),
-            pltpu.SemaphoreType.DMA((4,)),
-            pltpu.SemaphoreType.DMA((total // WIDE, 8)),
+            vmem((total, width), F32),
+            vmem(hidden.shape, BF16),
+            vmem(w_sh.shape, BF16),
+            vmem((total, width), BF16),
+            vmem((2 * HALO, width), BF16),
+            pltpu.SemaphoreType.DMA((8,)),
+            pltpu.SemaphoreType.DMA((total // WIDE, 6)),
         ],
         compiler_params=params(63),
-        cost_estimate=cost(2 * rows * width * 9 * width, 1.4e7),
-        name="input_gradient",
-    )(after, gain1, x, halo, w_in, triple_grad, middle_grad)
-
-
-def layer_result(after, table, b_sh, middle, hidden, w_sh):
-    total, width = middle.shape
-    vmem = pltpu.VMEM
-    return pl.pallas_call(
-        kernel_result,
-        out_shape=(shape((total - TILE, width), BF16), shape((TILE, width), BF16)),
-        in_specs=[ANY, SMEM, VMEM] + [ANY] * 3,
-        out_specs=(ANY, ANY),
-        scratch_shapes=[
-            vmem(middle.shape, F32),
-            vmem(hidden.shape, BF16),
-            vmem(w_sh.shape, BF16),
-            vmem(middle.shape, BF16),
-            pltpu.SemaphoreType.DMA((2,)),
-            pltpu.SemaphoreType.DMA((total // WIDE, 8)),
-        ],
-        compiler_params=params(63),
-        cost_estimate=cost(2 * total * width * 8 * width, 1.3e7),
-        name="layer_result",
-    )(after, table, b_sh, middle, hidden, w_sh)
+        cost_estimate=cost(2 * total * width * 16 * width, 2.7e7),
+        name="row_outputs",
+    )(after, table, gain1, b_sh, x, edge, w_in, triple_grad, middle_grad, middle, hidden, w_sh)
 
 
 def add_halves(mine, other):
@@ -1125,36 +1099,45 @@
     return lax.ppermute(block, "mp", route)
 
 
-def kernel_take_over(table, own_in, other_in, own_out, own, other, sems):
+def kernel_take_over(table, halo_in, input_in, result_in, input_out, result_out, halo, input_own, result_own, sems):
     rows = pl.ds(0, HALO)
     copies = [
-        pltpu.make_async_copy(own_in.at[rows], own, sems.at[0]), pltpu.make_async_copy(other_in, other, sems.at[1])
+        pltpu.make_async_copy(halo_in, halo, sems.at[0]),
+        pltpu.make_async_copy(input_in.at[rows], input_own, sems.at[1]),
+        pltpu.make_async_copy(result_in.at[rows], result_own, sems.at[2]),
     ]
     for copy in copies:
         copy.start()
     for copy in copies:
         copy.wait()
-    row = lax.broadcasted_iota(jnp.int32, (HALO, 1), 0)
-    mixed = jnp.where(row < table[GROUPS, 1], other[...].astype(F32), own[...].astype(F32))
-    own[...] = mixed.astype(own.dtype)
-    copy = pltpu.make_async_copy(own, own_out.at[rows], sems.at[2])
-    copy.start()
-    copy.wait()
-
-
-def take_over(table, own, other):
+    other = lax.broadcasted_iota(jnp.int32, (HALO, 1), 0) < table[GROUPS, 1]
+    input_own[...] = jnp.where(other, halo[:HALO, :].astype(F32), input_own[...])
+    result_own[...] = jnp.where(other, halo[HALO:, :].astype(F32), result_own[...].astype(F32)).astype(BF16)
+    copies = [
+        pltpu.make_async_copy(input_own, input_out.at[rows], sems.at[3]),
+        pltpu.make_async_copy(result_own, result_out.at[rows], sems.at[4]),
+    ]
+    for copy in copies:
+        copy.start()
+    for copy in copies:
+        copy.wait()
+
+
+def take_over(table, halo, input_grad, result):
+    width = input_grad.shape[1]
     return pl.pallas_call(
         kernel_take_over,
-        out_shape=shape(own.shape, own.dtype),
-        in_specs=[SMEM, ANY, ANY],
-        out_specs=ANY,
+        out_shape=(shape(input_grad.shape, F32), shape(result.shape, BF16)),
+        in_specs=[SMEM, ANY, ANY, ANY],
+        out_specs=(ANY, ANY),
         scratch_shapes=[
-            pltpu.VMEM(other.shape, own.dtype), pltpu.VMEM(other.shape, own.dtype), pltpu.SemaphoreType.DMA((3,)),
+            pltpu.VMEM(halo.shape, BF16), pltpu.VMEM((HALO, width), F32), pltpu.VMEM((HALO, width), BF16),
+            pltpu.SemaphoreType.DMA((5,)),
         ],
-        input_output_aliases={1: 0},
+        input_output_aliases={2: 0, 3: 1},
         compiler_params=params(63),
         name="take_over",
-    )(table, own, other)
+    )(table, halo, input_grad, result)
 
 
 def body(
@@ -1167,7 +1150,7 @@
     gain1, shift1, b_out, gain2, shift2, b_ex, b_sh = (
         first_gain, first_shift, outward_bias, second_gain, second_shift, expand_bias, shrink_bias
     )
-    halo = passed(jnp.concatenate([layer_input[:HALO], cotangent[:HALO]], axis=1), -1)
+    halo = passed(jnp.concatenate([layer_input[:HALO], cotangent[:HALO]], axis=0), -1)
     triple, attended, scaled, raised, stats, table = own_part(
         segments, gain1, shift1, inward_bias, layer_input, inward_weight
     )
@@ -1177,13 +1160,13 @@
     )
     both = add_halves(mine, swap_cores(other))
     parts = exchange(both.reshape(pieces, -1, LANES))
-    input_grad, input_halo = input_gradient(both, gain1, layer_input, edge, inward_weight, triple_grad, middle_grad)
-    result, result_halo = layer_result(input_halo, table, b_sh, middle, hidden, shrink_weight)
-    input_other = passed(input_halo[:HALO], 1)
-    summed = sum_parts((input_other, result_halo), parts)
+    input_grad, result, halo = row_outputs(
+        both, table, gain1, b_sh, layer_input, edge, inward_weight, triple_grad, middle_grad, middle, hidden,
+        shrink_weight,
+    )
+    summed = sum_parts((halo,), parts)
     mine = exchange(summed).reshape(-1, LANES)
-    input_grad = take_over(table, input_grad, touch(input_other, summed))
-    result = take_over(table, result, passed(touch(result_halo, summed)[:HALO], 1))
+    input_grad, result = take_over(table, touch(passed(halo, 1), summed), input_grad, result)
     mine = touch(mine, input_grad, result)
     other = swap_cores(mine)
     used = 192 * (2 * hidden_width + 4 * width) // LANES

time: 175 us -> 170 us (0.971)
  starting transfers between devices: 40 us -> 24.5 us
  waiting for transfers between devices: 21.8 us -> 35.9 us
  local copies, waits for them, and re-layouts: 5.43 us -> 3.31 us
  Pallas kernels: 106 us -> 104 us
    all_to_all x2, waiting for transfers between devices: 0.79 us -> 9.79 us  [exchange(): lax.all_to_all(parts, ('dp', 'mp'), 0, 0, axis_index_groups=same_core_gro...]
    all_to_all x2, starting transfers between devices: 25.1 us -> 16.4 us  [exchange(): lax.all_to_all(parts, ('dp', 'mp'), 0, 0, axis_index_groups=same_core_gro...]
    pallas_call x4 -> x2, Pallas kernels: 25.6 us -> 19.8 us  [the longest x1 16.9 us: row_outputs(): pl.pallas_call(kernel_rows, out_shape=(shape((rows, width), F32), shape((...]
    ppermute x3 -> x2, waiting for transfers between devices: 16.6 us -> 21.6 us  [passed(): return lax.ppermute(block, 'mp', route)]
    ppermute x2, starting transfers between devices: 7.88 us -> 4.02 us  [swap_cores(): return lax.ppermute(block, 'dp', [(i, i ^ 1) for i in range(packs)])]
    ppermute x3 -> x2, starting transfers between devices: 7.02 us -> 4.05 us  [passed(): return lax.ppermute(block, 'mp', route)]
    pallas_call x1, Pallas kernels: 50.6 us -> 52.6 us  [rest_part(): pl.pallas_call(kernel_rest, out_shape=(shape((total, width), F32), shape(...]
    slice x2 -> x0, local copies, waits for them, and re-layouts: 1.93 us -> none  [the longest x1 0.99 us: body(): input_other = passed(input_halo[:HALO], 1)]
  transfers between devices with their start and end apart: 7 -> 6, of which waited for: 6 -> 4; matrix products, arithmetic and copies ran while one was open for 1% -> 0% of each run, Pallas kernels for 27% -> 25%
where the time goes in v6:
time: 170 us; the launch traced here: 168 us
  Pallas kernels  104 us (61%)
  waiting for transfers between devices  35.9 us (21%)
  starting transfers between devices  24.5 us (14%)
  local copies, waits for them, and re-layouts  3.31 us (2%)
    pallas_call x1, Pallas kernels, rest_part(): pl.pallas_call(kernel_rest, out_shape=(shape((total, width), F32), shape(...  52.6 us
    ppermute x2, waiting for transfers between devices, passed(): return lax.ppermute(block, 'mp', route)  21.6 us
    pallas_call x1, Pallas kernels, own_part(): pl.pallas_call(kernel_own, out_shape=(shape((rows, 3 * width), BF16), sha...  19 us
    pallas_call x1, Pallas kernels, row_outputs(): pl.pallas_call(kernel_rows, out_shape=(shape((rows, width), F32), shape((...  16.9 us
    all_to_all x2, starting transfers between devices, exchange(): lax.all_to_all(parts, ('dp', 'mp'), 0, 0, axis_index_groups=same_core_gro...  16.4 us
    all_to_all x2, waiting for transfers between devices, exchange(): lax.all_to_all(parts, ('dp', 'mp'), 0, 0, axis_index_groups=same_core_gro...  9.79 us
    ppermute x2, waiting for transfers between devices, swap_cores(): return lax.ppermute(block, 'dp', [(i, i ^ 1) for i in range(packs)])  4.45 us
    ppermute x2, starting transfers between devices, passed(): return lax.ppermute(block, 'mp', route)  4.05 us
  transfers between devices with their start and end apart: 6, of which 4 were waited for; matrix products, arithmetic and copies ran while one was open for 0% of the time, Pallas kernels for 25%

profile of v6, /device:TPU:1, one launch (start us, length us, event | category | flops | bytes accessed | tf_op | source)
XLA Modules:
  0.0 168.4 jit_solution(13259100264832184762)
XLA Ops:
  0.6 0.9 slice.7
  1.6 0.9 slice.6
  2.6 1.3 collective-permute-start
  3.9 19.0 %own_part.1 = (bf16[2048,1152]{1,0:T(8,128)(2,1)}, bf16[2304,384]{1,0:T(8,128)(2,1)}, bf16[2048,384]{1,0:T(8,128)(2,1)}, bf16[24,3,512,256]{3,2,1,0:T(8,128)(2,1...) custom-call(s32[1,8192]{1,0:T(1,128)} %seg_in.1, f32[384]{0:T(512)} %gain1.1, f32[384]{0:T(512)} %refs_1_.1, f32[2,384]{1,0:T(2,128)} %refs_2_.1, ...), custom_call_target="tpu_custom_call" | custom-call | flops 10871635968 | bytes 10000000 | tf_op jit(solution)/shard_map/own_part/pallas_call | solution.py:873
  22.8 0.0 copy-start.2
  22.9 0.7 copy-done.2
  23.6 52.6 %rest_part.1 = (f32[2304,384]{1,0:T(8,128)}, f32[2304,384]{1,0:T(8,128)}, bf16[2304,1536]{1,0:T(8,128)(2,1)}, bf16[2304,1152]{1,0:T(8,128)(2,1)}, bf16[256,384]{...) custom-call(s32[25,8]{1,0:T(8,128)} %get-tuple-element.48.table, f32[384]{0:T(512)} %gain1.1, ...), custom_call_target="tpu_custom_call" | custom-call | flops 59793997824 | bytes 30000000 | tf_op jit(solution)/shard_map/rest_part/pallas_call | solution.py:916
  76.2 1.4 collective-permute-start.1
  77.6 3.8 %collective-permute-done.1.other_in = bf16[7168,128]{1,0:T(8,128)(2,1)} collective-permute-done((bf16[7168,128]{1,0:T(8,128)(2,1)}, bf16[7168,128]{1,0:T(8,128)(2,1)}, u32[]{:S(2)}, u32[]{:S(2)}) %collective-permute-start.1) | collective-permute-done | bytes 1835040 | tf_op jit(solution)/shard_map/ppermute | solution.py:1089
  81.4 3.0 %add_halves.1.after = bf16[7168,128]{1,0:T(8,128)(2,1)} custom-call(bf16[7168,128]{1,0:T(8,128)(2,1)} %get-tuple-element.54.mine_in, bf16[7168,128]{1,0:T(8,128)(2,1)} %collective-permute-done.1.other_in), custom_call_target="tpu_custom_call" | custom-call | flops 917504 | bytes 5505024 | tf_op jit(solution)/shard_map/add_halves/pallas_call | solution.py:1000
  84.3 10.7 %all-to-all-start = ((bf16[64,112,128]{2,1,0:T(8,128)(2,1)}), bf16[64,112,128]{2,1,0:T(8,128)(2,1)}, u32[]{:S(2)}, u32[]{:S(2)}) async-start(bf16[64,112,128]{2,1,0:T(8,128)(2,1)} %bitcast.2), calls=%async_computation | async-start | bytes 3670016 | tf_op jit(solution)/shard_map/all_to_all | solution.py:1093
  95.1 16.9 %row_outputs.1 = (f32[2048,384]{1,0:T(8,128)}, bf16[2048,384]{1,0:T(8,128)(2,1)}, bf16[416,384]{1,0:T(8,128)(2,1)}) custom-call(bf16[7168,128]{1,0:T(8,128)(2,1)} %add_halves.1.after, s32[25,8]{1,0:T(8,128)} %get-tuple-element.48.table, f32[384]{0:T(512)} %gain1.1, f32[384]{0:T(512)} %b_sh.1, bf16[2048,384]{1,0:T(8,128)(2,1)} %x_in.3, ...), custom_call_target="tpu_custom_call" | custom-call | flops 10871635968 | bytes 27000000 | tf_op jit(solution)/shard_map/row_outputs/pallas_call | solution.py:975
  112.0 9.8 %all-to-all-done.refs_1_ = bf16[64,112,128]{2,1,0:T(8,128)(2,1)} async-done(((bf16[64,112,128]{2,1,0:T(8,128)(2,1)}), bf16[64,112,128]{2,1,0:T(8,128)(2,1)}, u32[]{:S(2)}, u32[]{:S(2)}) %all-to-all-start) | async-done | bytes 1835040 | tf_op jit(solution)/shard_map/all_to_all | solution.py:1093
  121.8 2.7 %sum_parts.1.refs_1_ = bf16[64,112,128]{2,1,0:T(8,128)(2,1)} custom-call(bf16[416,384]{1,0:T(8,128)(2,1)} %get-tuple-element.61.refs_0_, bf16[64,112,128]{2,1,0:T(8,128)(2,1)} %all-to-all-done.refs_1_), custom_call_target="tpu_custom_call" | custom-call | flops 917504 | bytes 3670016 | tf_op jit(solution)/shard_map/sum_parts/pallas_call | solution.py:1015
  124.5 0.0 copy-start.1
  124.5 5.7 %all-to-all-start.1 = ((bf16[64,112,128]{2,1,0:T(8,128)(2,1)}), bf16[64,112,128]{2,1,0:T(8,128)(2,1)}, u32[]{:S(2)}, u32[]{:S(2)}) async-start(bf16[64,112,128]{2,1,0:T(8,128)(2,1)} %sum_parts.1.refs_1_), calls=%async_computation.1 | async-start | bytes 3670016 | tf_op jit(solution)/shard_map/all_to_all | solution.py:1093
  130.2 2.8 %collective-permute-start.2 = (bf16[416,384]{1,0:T(8,128)(2,1)S(1)}, bf16[416,384]{1,0:T(8,128)(2,1)S(1)}, u32[]{:S(2)}, u32[]{:S(2)}) collective-permute-start(bf16[416,384]{1,0:T(8,128)(2,1)S(1)} %copy-done.1), channel_id=1, source_target_pairs={{0,1},{1,2},{2,3},{4,5},{5,6},{6,7},{8,9},{9,10},{10,11},{12,13},{... | collective-permute-start | bytes 958472 | tf_op jit(solution)/shard_map/ppermute | solution.py:1099
  133.0 21.6 %collective-permute-done.2.refs_0_ = bf16[416,384]{1,0:T(8,128)(2,1)S(1)} collective-permute-done((bf16[416,384]{1,0:T(8,128)(2,1)S(1)}, bf16[416,384]{1,0:T(8,128)(2,1)S(1)}, u32[]{:S(2)}, u32[]{:S(2)}) %collective-permute-start.2) | collective-permute-done | bytes 319520 | tf_op jit(solution)/shard_map/ppermute | solution.py:1099
  154.6 0.7 copy-done
  155.3 2.9 %take_over.1 = (f32[2048,384]{1,0:T(8,128)}, bf16[2048,384]{1,0:T(8,128)(2,1)}) custom-call(s32[25,8]{1,0:T(8,128)} %get-tuple-element.48.table, bf16[416,384]{1,0:T(8,128)(2,1)} %touch.2.halo_in, f32[2048,384]{1,0:T(8,128)} %get-tuple-element.62.input_in, bf16[2048,384]{1,0:T(8,128)(2,1)} %get-tuple-element.63.result_in), custom_call_target="tpu_custom_call", output_to_operand_aliasing={{0}: (2, {}), {1}: (3, {})} | custom-call | tf_op jit(solution)/shard_map/take_over/pallas_call | solution.py:1128
  158.2 2.6 %collective-permute-start.3 = (bf16[7168,128]{1,0:T(8,128)(2,1)}, bf16[7168,128]{1,0:T(8,128)(2,1)}, u32[]{:S(2)}, u32[]{:S(2)}) collective-permute-start(bf16[7168,128]{1,0:T(8,128)(2,1)} %touch.3.packed_in.first_in), channel_id=1, source_target_pairs={{0,4},{4,0},{8,12},{12,8},{16,20},{20,16},{24,28},{28,24},{32,36},... | collective-permute-start | bytes 5505032 | tf_op jit(solution)/shard_map/ppermute | solution.py:1089
  160.8 3.0 %unpack_first.1 = (f32[384,1536]{1,0:T(8,128)}, f32[384,384]{1,0:T(8,128)}, f32[384,1152]{1,0:T(8,128)}, f32[1536,384]{1,0:T(8,128)}) custom-call(bf16[7168,128]{1,0:T(8,128)(2,1)} %touch.3.packed_in.first_in), custom_call_target="tpu_custom_call" | custom-call | flops 917504 | bytes 5505024 | tf_op jit(solution)/shard_map/unpack_first/pallas_call | solution.py:1039
  163.9 0.7 collective-permute-done.3.packed_in
  164.6 3.7 %unpack_second.1 = (f32[384,1536]{1,0:T(8,128)}, f32[384,384]{1,0:T(8,128)}, f32[384,1152]{1,0:T(8,128)}, f32[1536,384]{1,0:T(8,128)}, f32[2,384]{1,0:T(2,128)},...) custom-call(bf16[7168,128]{1,0:T(8,128)(2,1)} %collective-permute-do, ...), custom_call_target="tpu_custom_call", output_to_operand_aliasing={{0}: (2, {}), {1}: (3, {}), {2}: (4, {}), {3}: (5, {})} | custom-call | flops 917504 | bytes 5505024 | tf_op jit(solution)/shard_map/unpack_second/pallas_call | solution.py:1055
  (7 shorter events, 0.0 us)
Async XLA Ops:
  2.6 20.3 %collective-permute-start = (bf16[416,384]{1,0:T(8,128)(2,1)S(1)}, bf16[416,384]{1,0:T(8,128)(2,1)S(1)}, u32[]{:S(2)}, u32[]{:S(2)}) collective-permute-start(bf16[416,384]{1,0:T(8,128)(2,1)S(1)} %pad_maximum_fusion), channel_id=1, source_target_pairs={{1,0},{2,1},{3,2},{5,4},{6,5},{7,6},{9,8},{10,9},{11,10},{13,12},{... | collective-permute-start | bytes 958472 | tf_op jit(solution)/shard_map/ppermute | solution.py:1099
  22.8 0.7 copy-start.2
  76.2 5.2 %collective-permute-start.1 = (bf16[7168,128]{1,0:T(8,128)(2,1)}, bf16[7168,128]{1,0:T(8,128)(2,1)}, u32[]{:S(2)}, u32[]{:S(2)}) collective-permute-start(bf16[7168,128]{1,0:T(8,128)(2,1)} %get-tuple-element.55), channel_id=1, source_target_pairs={{0,4},{4,0},{8,12},{12,8},{16,20},{20,16},{24,28},{28,24},{32,36},... | collective-permute-start | bytes 5505032 | tf_op jit(solution)/shard_map/ppermute | solution.py:1089
  84.3 37.5 %all-to-all-start = ((bf16[64,112,128]{2,1,0:T(8,128)(2,1)}), bf16[64,112,128]{2,1,0:T(8,128)(2,1)}, u32[]{:S(2)}, u32[]{:S(2)}) async-start(bf16[64,112,128]{2,1,0:T(8,128)(2,1)} %bitcast.2), calls=%async_computation | async-start | bytes 3670016 | tf_op jit(solution)/shard_map/all_to_all | solution.py:1093
  124.5 5.7 %copy-start.1 = (bf16[416,384]{1,0:T(8,128)(2,1)S(1)}, bf16[416,384]{1,0:T(8,128)(2,1)}, u32[]{:S(2)}) copy-start(bf16[416,384]{1,0:T(8,128)(2,1)} %get-tuple-element.61.refs_0_) | copy-start | bytes 958468
  124.5 33.7 %all-to-all-start.1 = ((bf16[64,112,128]{2,1,0:T(8,128)(2,1)}), bf16[64,112,128]{2,1,0:T(8,128)(2,1)}, u32[]{:S(2)}, u32[]{:S(2)}) async-start(bf16[64,112,128]{2,1,0:T(8,128)(2,1)} %sum_parts.1.refs_1_), calls=%async_computation.1 | async-start | bytes 3670016 | tf_op jit(solution)/shard_map/all_to_all | solution.py:1093
  130.2 24.4 %collective-permute-start.2 = (bf16[416,384]{1,0:T(8,128)(2,1)S(1)}, bf16[416,384]{1,0:T(8,128)(2,1)S(1)}, u32[]{:S(2)}, u32[]{:S(2)}) collective-permute-start(bf16[416,384]{1,0:T(8,128)(2,1)S(1)} %copy-done.1), channel_id=1, source_target_pairs={{0,1},{1,2},{2,3},{4,5},{5,6},{6,7},{8,9},{9,10},{10,11},{12,13},{... | collective-permute-start | bytes 958472 | tf_op jit(solution)/shard_map/ppermute | solution.py:1099
  154.6 0.7 copy-start
  158.2 6.3 %collective-permute-start.3 = (bf16[7168,128]{1,0:T(8,128)(2,1)}, bf16[7168,128]{1,0:T(8,128)(2,1)}, u32[]{:S(2)}, u32[]{:S(2)}) collective-permute-start(bf16[7168,128]{1,0:T(8,128)(2,1)} %touch.3.packed_in.first_in), channel_id=1, source_target_pairs={{0,4},{4,0},{8,12},{12,8},{16,20},{20,16},{24,28},{28,24},{32,36},... | collective-permute-start | bytes 5505032 | tf_op jit(solution)/shard_map/ppermute | solution.py:1089
